TPU v7x, 128 devices: a whole 4x4x4 slice. The times are simulated.
128 devices in a mesh: dp: 8 (over x, core), shard: 16 (over y, z).
Axes of the slice: x: 4, y: 4, z: 4, core: 2. Of those that a mesh axis runs over, the one named last changes fastest.
Arguments:
- inputs: bfloat16 [98304, 7168], P(('dp', 'shard')), may hold values from -80 to 80, as said below
- cotangent: bfloat16 [98304, 512], P(('dp', 'shard')), may hold values from -20 to 20
- weight: bfloat16 [7168, 512], P('shard'), may hold values from -1 to 1
- norm_gain: float32 [512], replicated, may hold values from 0.25 to 1.75
Outputs:
- input_grad: bfloat16 [98304, 7168], P(('dp', 'shard'))
- weight_grad: float32 [7168, 512], P(('dp', 'shard'))
- gain_grad: float32 [512], replicated
Inputs may be any that keep to these rules, and one draw needn't show every extreme that they name: `inputs`: activations with per-token scales.
All inputs are finite; a program needn't handle non-finite values.
Results may differ from a plain program's by a relative error of at most 0.0049.
Values may be sent and summed in bfloat16 or wider, within the bound.
No kernel may reach another device: no remote copies, remote signals or barrier semaphores. Data moves between devices by JAX's collectives and lax.ppermute only.
A program may use at most 128 MiB of HBM per device.

v0:
```python
import jax
import jax.numpy as jnp
from jax import lax
from jax.sharding import PartitionSpec as P

epsilon = 1e-06


def shards(inputs, cotangent, weight, norm_gain):
    gathered = lax.all_gather(weight, "shard", axis=0, tiled=True)
    latent = jnp.dot(inputs, gathered, preferred_element_type=jnp.float32)
    inverse_scale = lax.rsqrt(jnp.mean(latent * latent, axis=-1, keepdims=True) + epsilon)
    normed = latent * inverse_scale
    upstream = cotangent.astype(jnp.float32)
    gain_grad = lax.psum(jnp.sum(upstream * normed, axis=0), ("dp", "shard"))
    scaled = upstream * norm_gain
    center = jnp.mean(scaled * normed, axis=-1, keepdims=True)
    latent_grad = (inverse_scale * (scaled - normed * center)).astype(jnp.bfloat16)
    input_grad = lax.dot_general(
        latent_grad, gathered, (((1,), (1,)), ((), ())), preferred_element_type=jnp.float32
    )
    input_grad = input_grad.astype(jnp.bfloat16)
    weight_grad = lax.psum_scatter(
        lax.dot_general(
            inputs, latent_grad, (((0,), (0,)), ((), ())), preferred_element_type=jnp.float32
        ),
        ("dp", "shard"),
        scatter_dimension=0,
        tiled=True,
    )
    return (input_grad, weight_grad, gain_grad)


def solution(mesh):
    placed = (P(("dp", "shard"), None), P(("dp", "shard"), None), P("shard", None), P())
    return jax.shard_map(
        shards,
        mesh=mesh,
        in_specs=placed,
        out_specs=(P(("dp", "shard"), None), P(("dp", "shard"), None), P()),
        check_vma=False,
    )
```

profile of v0, /device:TPU:0, one launch (start us, length us, event | category | flops | bytes accessed | tf_op | source)
XLA Modules:
  0.0 791.4 jit_solution(2815162191243083892)
XLA Ops:
  7.2 0.0 all-gather.2.cloned.1.call-start
  7.2 0.7 all-gather.2.cloned.1.call-update
  7.9 0.0 reduce-scatter.4.cloned.1.call-start
  7.9 1.4 copy.9
  9.4 0.0 copy-start
  9.4 69.6 %all-gather.2.cloned.1.call-done = bf16[7168,512]{1,0:T(8,128)(2,1)} async-done(((bf16[448,512]{1,0:T(8,128)(2,1)}), bf16[7168,512]{1,0:T(8,128)(2,1)}) %all-gather.2.cloned.1.call-update) | async-done | bytes 7340048 | tf_op jit(solution)/shard_map/all_gather | solution.py:10
  78.9 12.5 %multiply_reduce_fusion = (f32[768]{0:T(1024)S(1)}, f32[768,512]{0,1:T(8,128)S(1)}) fusion(bf16[768,7168]{1,0:T(8,128)(2,1)} %param.4, bf16[7168,512]{1,0:T(8,128)(2,1)} %all-gather.2.cloned.1.call-done), kind=kOutput, calls=%fused_computation.10 | convolution fusion | flops 5637929984 | bytes 19926016 | tf_op jit(solution)/shard_map/dot_general | solution.py:11
  91.5 0.0 copy-done
  91.5 0.6 fusion.5
  92.2 0.4 fusion.4
  92.6 13.3 %convolution_bitcast_fusion = f32[7168,512]{0,1:T(8,128)} fusion(bf16[768,512]{0,1:T(8,128)(2,1)S(1)} %fusion.4, bf16[768,7168]{1,0:T(8,128)(2,1)} %param.4), kind=kOutput, calls=%fused_computation.1 | convolution fusion | flops 5637144576 | bytes 26476544 | tf_op jit(solution)/shard_map/dot_general | solution.py:24
  105.9 15.3 %copy.11 = f32[7168,512]{1,0:T(8,128)} copy(f32[7168,512]{0,1:T(8,128)} %convolution_bitcast_fusion) | data formatting | bytes 29360128
  121.2 0.0 reduce-scatter.4.cloned.1.call-update
  121.3 66.6 %psum.7 = f32[512]{0:T(512)} all-reduce(f32[512]{0:T(512)S(1)} %get-tuple-element.9), channel_id=1, replica_groups=mesh['dp'=8,'shard'=16] {'dp','shard'}, use_global_device_ids=true, to_apply=%region_4.0 | all-reduce | flops 512 | bytes 4096 | tf_op jit(solution)/shard_map/psum | solution.py:15
  187.9 11.9 %convolution_convert_fusion = bf16[768,7168]{1,0:T(8,128)(2,1)} fusion(bf16[768,512]{0,1:T(8,128)(2,1)S(1)} %fusion.4, bf16[7168,512]{1,0:T(8,128)(2,1)} %all-gather.2.cloned.1.call-done), kind=kOutput, calls=%fused_computation | convolution fusion | flops 5642649600 | bytes 19136512 | tf_op jit(solution)/shard_map/dot_general | solution.py:19
  199.8 584.8 %reduce-scatter.4.cloned.1.call-done = f32[56,512]{1,0:T(8,128)} async-done(((f32[7168,512]{1,0:T(8,128)}), f32[56,512]{1,0:T(8,128)}) %reduce-scatter.4.cloned.1.call-update) | async-done | bytes 114704
  (2 shorter events, 0.0 us)
Async XLA Ops:
  7.2 71.8 %all-gather.2.cloned.1.call-start = ((), (), s32[]{:S(2)}) async-start(), calls=%async_computation.1 | async-start | bytes 7798784 | tf_op jit(solution)/shard_map/all_gather | solution.py:10
  7.9 776.7 %reduce-scatter.4.cloned.1.call-start = ((), (), s32[]{:S(2)}) async-start(), calls=%async_computation.2 | async-start | bytes 14794752
  9.4 82.2 %copy-start = (f32[512]{0:T(512)S(1)}, f32[512]{0:T(512)}, u32[]{:S(2)}) copy-start(f32[512]{0:T(512)} %param.7) | copy-start | bytes 6148
Sparse Core Ops, SparseCore 0:
  10.2 68.7 all-gather.1
  121.4 663.1 reduce-scatter.3
where the time goes:
time: 792 us; the launch traced here: 791 us
  waiting for transfers between devices  655 us (83%)
  blocking collectives  66.6 us (8%)
  matrix products  37.8 us (5%)
  local copies, waits for them, and re-layouts  16.7 us (2%)
  between operations  14.1 us (2%)
    unnamed x3, waiting for transfers between devices  585 us
    all_gather x1, waiting for transfers between devices, shards(): gathered = lax.all_gather(weight, 'shard', axis=0, tiled=True)  69.6 us
    psum x1, blocking collectives, shards(): gain_grad = lax.psum(jnp.sum(upstream * normed, axis=0), ('dp', 'shard'))  66.6 us
    unnamed x4, local copies, waits for them, and re-layouts  16.7 us
  transfers between devices with their start and end apart: 2, of which 2 were waited for; matrix products, arithmetic and copies ran while one was open for 2% of the time, Pallas kernels for 0%

commit v1 on v0

v1 whole, which is shorter than its diff:
```python
import jax
import jax.numpy as jnp
from jax import lax
from jax.sharding import PartitionSpec as P

epsilon = 1e-06
axes = ("dp", "shard")


def device(x, core, y, z):
    return ((x % 4) * 2 + core) * 16 + (y % 4) * 4 + z % 4


def permute(value, move):
    pairs = [
        (device(x, c, y, z), device(*move(x, c, y, z)))
        for x in range(4)
        for c in range(2)
        for y in range(4)
        for z in range(4)
    ]
    return lax.ppermute(value, axes, pairs)


def twin(value):
    return permute(value, lambda x, c, y, z: (x, 1 - c, y, z))


def shift(value, axis, by):
    step = [by if axis == name else 0 for name in "xyz"]
    return permute(value, lambda x, c, y, z: (x + step[0], c, y + step[1], z + step[2]))


def pick(value, index):
    return lax.dynamic_index_in_dim(value, index % 4, 0, keepdims=False)


def reduce_over(value, axis, position):
    own = pick(value, position).astype(jnp.float32)
    near = [shift(pick(value, position + by), axis, by).astype(jnp.float32) for by in (1, 2, 3)]
    return (own + near[1]) + (near[0] + near[2])


def sum_over(value, axis):
    near = [shift(value, axis, by) for by in (1, 2, 3)]
    return (value + near[1]) + (near[0] + near[2])


def shards(inputs, cotangent, weight, norm_gain):
    dp, shard = lax.axis_index("dp"), lax.axis_index("shard")
    place = {"x": dp // 2, "y": shard // 4, "z": shard % 4}
    core = dp % 2
    half = lax.dynamic_slice_in_dim(weight, core * 224, 224, 0)
    mine = lax.all_gather(half, "shard", axis=0, tiled=False)
    other = twin(mine)
    gathered = jnp.where(core == 0, jnp.stack([mine, other], 1), jnp.stack([other, mine], 1))
    gathered = gathered.reshape(7168, 512)
    latent = jnp.dot(inputs, gathered, preferred_element_type=jnp.float32)
    inverse_scale = lax.rsqrt(jnp.mean(latent * latent, axis=-1, keepdims=True) + epsilon)
    normed = latent * inverse_scale
    upstream = cotangent.astype(jnp.float32)
    gain_grad = jnp.sum(upstream * normed, axis=0)
    gain_grad = gain_grad + twin(gain_grad)
    for axis in "xyz":
        gain_grad = sum_over(gain_grad, axis)
    scaled = upstream * norm_gain
    center = jnp.mean(scaled * normed, axis=-1, keepdims=True)
    latent_grad = (inverse_scale * (scaled - normed * center)).astype(jnp.bfloat16)
    input_grad = lax.dot_general(
        latent_grad, gathered, (((1,), (1,)), ((), ())), preferred_element_type=jnp.float32
    )
    input_grad = input_grad.astype(jnp.bfloat16)
    partial = lax.dot_general(
        inputs, latent_grad, (((0,), (0,)), ((), ())), preferred_element_type=jnp.float32
    ).astype(jnp.bfloat16)
    partial = partial.reshape(4, 2, 4, 4, 56, 512)
    kept = lax.dynamic_index_in_dim(partial, core, 1, keepdims=False)
    sent = lax.dynamic_index_in_dim(partial, 1 - core, 1, keepdims=False)
    both = (kept.astype(jnp.float32) + twin(sent).astype(jnp.float32)).astype(jnp.bfloat16)
    pieces = []
    for start, stop, order in ((0, 24, "xyz"), (24, 40, "yzx"), (40, 56, "zxy")):
        piece = both[:, :, :, start:stop]
        left = "xyz"
        for axis in order:
            piece = jnp.moveaxis(piece, left.index(axis), 0)
            piece = reduce_over(piece, axis, place[axis])
            left = left.replace(axis, "")
            if left:
                piece = piece.astype(jnp.bfloat16)
        pieces.append(piece)
    weight_grad = jnp.concatenate(pieces, 0)
    return (input_grad, weight_grad, gain_grad)


def solution(mesh):
    placed = (P(("dp", "shard"), None), P(("dp", "shard"), None), P("shard", None), P())
    return jax.shard_map(
        shards,
        mesh=mesh,
        in_specs=placed,
        out_specs=(P(("dp", "shard"), None), P(("dp", "shard"), None), P()),
        check_vma=False,
    )
```

time: 792 us -> 229 us (0.29)
  waiting for transfers between devices: 655 us -> 83.3 us
  blocking collectives: 66.6 us -> 0 us
  starting transfers between devices: 0.08 us -> 63.3 us
  other arithmetic: 1.04 us -> 13.7 us
    unnamed x3 -> x1, waiting for transfers between devices: 585 us -> 0.02 us
    psum x1 -> x0, blocking collectives: 66.6 us -> none  [shards(): gain_grad = lax.psum(jnp.sum(upstream * normed, axis=0), ('dp', 'shard'))]
    ppermute x0 -> x39, starting transfers between devices: none -> 63.3 us  [permute(): return lax.ppermute(value, axes, pairs)]
    ppermute x0 -> x39, waiting for transfers between devices: none -> 29.1 us  [permute(): return lax.ppermute(value, axes, pairs)]
    all_gather x1, waiting for transfers between devices: 69.6 us -> 54.2 us  [shards(): mine = lax.all_gather(half, 'shard', axis=0, tiled=False)]
    unnamed x4 -> x13, local copies, waits for them, and re-layouts: 16.7 us -> 2.38 us
    convert_element_type x0 -> x1, local copies, waits for them, and re-layouts: none -> 10.4 us  [shards(): partial = lax.dot_general(inputs, latent_grad, (((0,), (0,)), ((), ())),...]
  transfers between devices with their start and end apart: 2 -> 40, of which waited for: 2 -> 16; matrix products, arithmetic and copies ran while one was open for 2% -> 6% of each run, Pallas kernels for 0% -> 0%
where the time goes in v1:
time: 229 us; the launch traced here: 228 us
  waiting for transfers between devices  83.3 us (36%)
  starting transfers between devices  63.3 us (28%)
  matrix products  35.1 us (15%)
  local copies, waits for them, and re-layouts  18.6 us (8%)
  between operations  14.4 us (6%)
  other arithmetic  13.7 us (6%)
    ppermute x39, starting transfers between devices, permute(): return lax.ppermute(value, axes, pairs)  63.3 us
    all_gather x1, waiting for transfers between devices, shards(): mine = lax.all_gather(half, 'shard', axis=0, tiled=False)  54.2 us
    ppermute x39, waiting for transfers between devices, permute(): return lax.ppermute(value, axes, pairs)  29.1 us
    dot_general x1, matrix products, shards(): lax.dot_general(inputs, latent_grad, (((0,), (0,)), ((), ())), preferred_...  12 us
    dot_general x1, matrix products, shards(): lax.dot_general(latent_grad, gathered, (((1,), (1,)), ((), ())), preferre...  11.9 us
    dot_general x1, matrix products, shards(): latent = jnp.dot(inputs, gathered, preferred_element_type=jnp.float32)  11.2 us
    convert_element_type x1, local copies, waits for them, and re-layouts, shards(): partial = lax.dot_general(inputs, latent_grad, (((0,), (0,)), ((), ())),...  10.4 us
    select_n x1, other arithmetic, shards(): jnp.where(core == 0, jnp.stack([mine, other], 1), jnp.stack([other, mine]...  7.42 us
  transfers between devices with their start and end apart: 40, of which 16 were waited for; matrix products, arithmetic and copies ran while one was open for 6% of the time, Pallas kernels for 0%

profile of v1, /device:TPU:0, one launch (start us, length us, event | category | flops | bytes accessed | tf_op | source)
XLA Modules:
  0.0 228.4 jit_solution(12472645130513108343)
XLA Ops:
  8.9 54.2 %all-gather.3.cloned.1.call-done = bf16[3584,512]{1,0:T(8,128)(2,1)} async-done(((bf16[224,512]{1,0:T(8,128)(2,1)}), bf16[3584,512]{1,0:T(8,128)(2,1)}) %all-gather.3.cloned.1.call-update) | async-done | bytes 3670032 | tf_op jit(solution)/shard_map/all_gather | solution.py:54
  64.6 5.3 %collective-permute-done = bf16[16,224,512]{2,1,0:T(8,128)(2,1)} collective-permute-done((bf16[16,224,512]{2,1,0:T(8,128)(2,1)}, bf16[16,224,512]{2,1,0:T(8,128)(2,1)}, u32[]{:S(2)}, u32[]{:S(2)}) %collective-permute-start) | collective-permute-done | bytes 3670048 | tf_op jit(solution)/shard_map/ppermute | solution.py:22
  69.9 7.4 %maximum_select_fusion = bf16[16,2,224,512]{3,2,1,0:T(8,128)(2,1)S(1)} fusion(bf16[16,1,224,512]{3,2,1,0:T(8,128)(2,1)} %bitcast.2, bf16[16,1,224,512]{3,2,1,0:T(8,128)(2,1)} %bitcast.112, pred[]{:T(512)S(6)} %eq.42), kind=kLoop, calls=%fused_computation.3 | loop fusion | flops 11010048 | bytes 14680065 | tf_op jit(solution)/shard_map/jit(_where)/select_n | solution.py:56
  77.3 11.2 %multiply_reduce_fusion = (f32[768]{0:T(1024)S(1)}, f32[512,768]{1,0:T(8,128)S(1)}) fusion(bf16[7168,512]{1,0:T(8,128)(2,1)S(1)} %bitcast.109, bf16[768,7168]{1,0:T(8,128)(2,1)} %param.4), kind=kOutput, calls=%fused_computation.16 | convolution fusion | flops 5637929984 | bytes 19926016 | tf_op jit(solution)/shard_map/dot_general | solution.py:58
  89.6 12.0 %fusion = bf16[7168,512]{0,1:T(8,128)(2,1)} fusion(bf16[768,512]{0,1:T(8,128)(2,1)S(1)} %fusion.6, bf16[768,7168]{1,0:T(8,128)(2,1)} %param.4), kind=kOutput, calls=%fused_computation.2 | convolution fusion | flops 5640814592 | bytes 19136512 | tf_op jit(solution)/shard_map/dot_general | solution.py:73
  101.6 10.4 %copy.11 = bf16[7168,512]{1,0:T(8,128)(2,1)} copy(bf16[7168,512]{0,1:T(8,128)(2,1)} %fusion) | data formatting | bytes 14680064 | tf_op jit(solution)/shard_map/convert_element_type | solution.py:75
  112.0 4.3 %dynamic-slice_bitcast_fusion = bf16[4,4,4,56,512]{4,3,2,1,0:T(8,128)(2,1)} fusion(bf16[4,2,4,4,56,512]{5,4,3,2,1,0:T(8,128)(2,1)} %bitcast.105, s32[]{:T(128)S(6)} %select_n.208), kind=kLoop, calls=%fused_computation.6 | loop fusion | bytes 7340036 | tf_op jit(solution)/shard_map/jit(dynamic_index_in_dim)/squeeze | solution.py:78
  116.8 4.1 %collective-permute-done.29 = f32[512]{0:T(512)S(1)} collective-permute-done((f32[512]{0:T(512)S(1)}, f32[512]{0:T(512)S(1)}, u32[]{:S(2)}, u32[]{:S(2)}) %collective-permute-start.29) | collective-permute-done | bytes 2080 | tf_op jit(solution)/shard_map/ppermute | solution.py:22
  121.0 3.0 %collective-permute-start.30 = (f32[512]{0:T(512)S(1)}, f32[512]{0:T(512)S(1)}, u32[]{:S(2)}, u32[]{:S(2)}) collective-permute-start(f32[512]{0:T(512)S(1)} %add.384), channel_id=1, source_target_pairs={{0,64},{1,65},{2,66},{3,67},{4,68},{5,69},{6,70},{7,71},{8,72},{9,... | collective-permute-start | bytes 6152 | tf_op jit(solution)/shard_map/ppermute | solution.py:22
  124.5 2.7 %collective-permute-start.32 = (f32[512]{0:T(512)S(1)}, f32[512]{0:T(512)S(1)}, u32[]{:S(2)}, u32[]{:S(2)}) collective-permute-start(f32[512]{0:T(512)S(1)} %add.384), channel_id=1, source_target_pairs={{0,96},{1,97},{2,98},{3,99},{4,100},{5,101},{6,102},{7,103},{8,104... | collective-permute-start | bytes 6152 | tf_op jit(solution)/shard_map/ppermute | solution.py:22
  128.8 2.5 %collective-permute-start.33 = (f32[512]{0:T(512)S(1)}, f32[512]{0:T(512)S(1)}, u32[]{:S(2)}, u32[]{:S(2)}) collective-permute-start(f32[512]{0:T(512)S(1)} %add_add_fusion.2), channel_id=1, source_target_pairs={{0,8},{1,9},{2,10},{3,11},{4,12},{5,13},{6,14},{7,15},{8,0},{9,1},... | collective-permute-start | bytes 6152 | tf_op jit(solution)/shard_map/ppermute | solution.py:22
  131.9 2.6 %collective-permute-start.35 = (f32[512]{0:T(512)S(1)}, f32[512]{0:T(512)S(1)}, u32[]{:S(2)}, u32[]{:S(2)}) collective-permute-start(f32[512]{0:T(512)S(1)} %add_add_fusion.2), channel_id=1, source_target_pairs={{0,12},{1,13},{2,14},{3,15},{4,0},{5,1},{6,2},{7,3},{8,4},{9,5},{1... | collective-permute-start | bytes 6152 | tf_op jit(solution)/shard_map/ppermute | solution.py:22
  138.3 2.7 %collective-permute-start.38 = (f32[512]{0:T(512)S(1)}, f32[512]{0:T(512)S(1)}, u32[]{:S(2)}, u32[]{:S(2)}) collective-permute-start(f32[512]{0:T(512)S(1)} %add_add_fusion.1), channel_id=1, source_target_pairs={{0,3},{1,0},{2,1},{3,2},{4,7},{5,4},{6,5},{7,6},{8,11},{9,8},{10,9... | collective-permute-start | bytes 6152 | tf_op jit(solution)/shard_map/ppermute | solution.py:22
  141.0 11.9 %convolution_convert_fusion = bf16[768,7168]{1,0:T(8,128)(2,1)} fusion(bf16[768,512]{0,1:T(8,128)(2,1)S(1)} %fusion.6, bf16[7168,512]{1,0:T(8,128)(2,1)} %bitcast.110), kind=kOutput, calls=%fused_computation | convolution fusion | flops 5642649600 | bytes 19136512 | tf_op jit(solution)/shard_map/dot_general | solution.py:69
  153.5 3.3 %fusion.1 = bf16[4,4,4,56,512]{4,3,2,1,0:T(8,128)(2,1)S(1)} fusion(bf16[4,4,4,56,512]{4,3,2,1,0:T(8,128)(2,1)} %collective-permute-done.1, bf16[4,2,4,4,56,512]{5,4,3,2,1,0:T(8,128)(2,1)S(1)} %bitcast.108, s32[]{:T(128)S(6)} %select_n.207), kind=kLoop, calls=%fused_computation.5 | loop fusion | flops 7340032 | bytes 11010052 | tf_op jit(solution)/shard_map/convert_element_type | solution.py:79
  157.3 1.7 collective-permute-start.11
  159.0 2.5 %collective-permute-start.12 = (bf16[4,4,16,512]{3,2,1,0:T(8,128)(2,1)S(1)}, bf16[4,4,16,512]{3,2,1,0:T(8,128)(2,1)S(1)}, u32[]{:S(2)}, u32[]{:S(2)}) collective-permute-start(bf16[4,4,16,512]{3,2,1,0:T(8,128)(2,1)S(1)} %get-tuple-element.12), channel_id=1, source_target_pairs={{0,4},{1,5},{2,6},{3,7},{4,8},{5,9},{6,10},{7,11},{8,12},{9,13},{1... | collective-permute-start | bytes 786440 | tf_op jit(solution)/shard_map/ppermute | solution.py:22
  163.8 2.6 %collective-permute-start.3 = (bf16[4,4,24,512]{3,2,1,0:T(8,128)(2,1)S(1)}, bf16[4,4,24,512]{3,2,1,0:T(8,128)(2,1)S(1)}, u32[]{:S(2)}, u32[]{:S(2)}) collective-permute-start(bf16[4,4,24,512]{3,2,1,0:T(8,128)(2,1)S(1)} %get-tuple-element.9), channel_id=1, source_target_pairs={{0,32},{1,33},{2,34},{3,35},{4,36},{5,37},{6,38},{7,39},{8,40},{9,... | collective-permute-start | bytes 1179656 | tf_op jit(solution)/shard_map/ppermute | solution.py:22
  169.8 2.9 %collective-permute-start.22 = (bf16[4,4,16,512]{3,2,1,0:T(8,128)(2,1)S(1)}, bf16[4,4,16,512]{3,2,1,0:T(8,128)(2,1)S(1)}, u32[]{:S(2)}, u32[]{:S(2)}) collective-permute-start(bf16[4,4,16,512]{3,2,1,0:T(8,128)(2,1)S(1)} %get-tuple-element.14), channel_id=1, source_target_pairs={{0,3},{1,0},{2,1},{3,2},{4,7},{5,4},{6,5},{7,6},{8,11},{9,8},{10,9... | collective-permute-start | bytes 786440 | tf_op jit(solution)/shard_map/ppermute | solution.py:22
  172.9 3.4 %collective-permute-done.20 = bf16[4,4,16,512]{3,2,1,0:T(8,128)(2,1)S(1)} collective-permute-done((bf16[4,4,16,512]{3,2,1,0:T(8,128)(2,1)S(1)}, bf16[4,4,16,512]{3,2,1,0:T(8,128)(2,1)S(1)}, u32[]{:S(2)}, u32[]{:S(2)}) %collective-permute-start.20) | collective-permute-done | bytes 262176 | tf_op jit(solution)/shard_map/ppermute | solution.py:22
  176.2 1.8 collective-permute-start.14
  178.1 2.1 collective-permute-done.21
  180.2 3.2 %collective-permute-start.16 = (bf16[4,16,512]{2,1,0:T(8,128)(2,1)S(1)}, bf16[4,16,512]{2,1,0:T(8,128)(2,1)S(1)}, u32[]{:S(2)}, u32[]{:S(2)}) collective-permute-start(bf16[4,16,512]{2,1,0:T(8,128)(2,1)S(1)} %get-tuple-element.20), channel_id=1, source_target_pairs={{0,3},{1,0},{2,1},{3,2},{4,7},{5,4},{6,5},{7,6},{8,11},{9,8},{10,9... | collective-permute-start | bytes 196616 | tf_op jit(solution)/shard_map/ppermute | solution.py:22
  183.6 2.7 %collective-permute-start.4 = (bf16[4,4,24,512]{3,2,1,0:T(8,128)(2,1)S(1)}, bf16[4,4,24,512]{3,2,1,0:T(8,128)(2,1)S(1)}, u32[]{:S(2)}, u32[]{:S(2)}) collective-permute-start(bf16[4,4,24,512]{3,2,1,0:T(8,128)(2,1)S(1)} %get-tuple-element.8), channel_id=1, source_target_pairs={{0,96},{1,97},{2,98},{3,99},{4,100},{5,101},{6,102},{7,103},{8,104... | collective-permute-start | bytes 1179656 | tf_op jit(solution)/shard_map/ppermute | solution.py:22
  187.1 2.0 collective-permute-start.24
  189.1 3.0 %collective-permute-done.23 = bf16[4,16,512]{2,1,0:T(8,128)(2,1)S(1)} collective-permute-done((bf16[4,16,512]{2,1,0:T(8,128)(2,1)S(1)}, bf16[4,16,512]{2,1,0:T(8,128)(2,1)S(1)}, u32[]{:S(2)}, u32[]{:S(2)}) %collective-permute-start.23) | collective-permute-done | bytes 65568 | tf_op jit(solution)/shard_map/ppermute | solution.py:22
  192.1 5.0 %collective-permute-start.25 = (bf16[4,16,512]{2,1,0:T(8,128)(2,1)S(1)}, bf16[4,16,512]{2,1,0:T(8,128)(2,1)S(1)}, u32[]{:S(2)}, u32[]{:S(2)}) collective-permute-start(bf16[4,16,512]{2,1,0:T(8,128)(2,1)S(1)} %get-tuple-element.23), channel_id=1, source_target_pairs={{0,96},{1,97},{2,98},{3,99},{4,100},{5,101},{6,102},{7,103},{8,104... | collective-permute-start | bytes 196616 | tf_op jit(solution)/shard_map/ppermute | solution.py:22
  200.7 2.4 %collective-permute-start.19 = (bf16[16,512]{1,0:T(8,128)(2,1)S(1)}, bf16[16,512]{1,0:T(8,128)(2,1)S(1)}, u32[]{:S(2)}, u32[]{:S(2)}) collective-permute-start(bf16[16,512]{1,0:T(8,128)(2,1)S(1)} %get-tuple-element.29), channel_id=1, source_target_pairs={{0,96},{1,97},{2,98},{3,99},{4,100},{5,101},{6,102},{7,103},{8,104... | collective-permute-start | bytes 49160 | tf_op jit(solution)/shard_map/ppermute | solution.py:22
  204.8 2.2 collective-permute-start.5
  207.0 2.0 collective-permute-start.6
  211.0 3.2 %collective-permute-start.28 = (bf16[16,512]{1,0:T(8,128)(2,1)S(1)}, bf16[16,512]{1,0:T(8,128)(2,1)S(1)}, u32[]{:S(2)}, u32[]{:S(2)}) collective-permute-start(bf16[16,512]{1,0:T(8,128)(2,1)S(1)} %get-tuple-element.32), channel_id=1, source_target_pairs={{0,12},{1,13},{2,14},{3,15},{4,0},{5,1},{6,2},{7,3},{8,4},{9,5},{1... | collective-permute-start | bytes 49160 | tf_op jit(solution)/shard_map/ppermute | solution.py:22
  216.5 1.8 collective-permute-done.10
  (100 shorter events, 31.8 us)
Async XLA Ops:
  7.2 55.9 %all-gather.3.cloned.1.call-start = ((), (), s32[]{:S(2)}) async-start(), calls=%async_computation | async-start | bytes 3899392 | tf_op jit(solution)/shard_map/all_gather | solution.py:54
  63.1 6.8 %collective-permute-start = (bf16[16,224,512]{2,1,0:T(8,128)(2,1)}, bf16[16,224,512]{2,1,0:T(8,128)(2,1)}, u32[]{:S(2)}, u32[]{:S(2)}) collective-permute-start(bf16[16,224,512]{2,1,0:T(8,128)(2,1)} %bitcast.111), channel_id=1, source_target_pairs={{0,16},{1,17},{2,18},{3,19},{4,20},{5,21},{6,22},{7,23},{8,24},{9,... | collective-permute-start | bytes 11010056 | tf_op jit(solution)/shard_map/ppermute | solution.py:22
  116.3 37.1 %collective-permute-start.1 = (bf16[4,4,4,56,512]{4,3,2,1,0:T(8,128)(2,1)}, bf16[4,4,4,56,512]{4,3,2,1,0:T(8,128)(2,1)}, u32[]{:S(2)}, u32[]{:S(2)}) collective-permute-start(bf16[4,4,4,56,512]{4,3,2,1,0:T(8,128)(2,1)} %dynamic-slice_bitcast_fusion), channel_id=1, source_target_pairs={{0,16},{1,17},{2,18},{3,19},{4,20},{5,21},{6,22},{7,23},{8,24},{9,... | collective-permute-start | bytes 11010056 | tf_op jit(solution)/shard_map/ppermute | solution.py:22
  121.0 6.2 %collective-permute-start.30 = (f32[512]{0:T(512)S(1)}, f32[512]{0:T(512)S(1)}, u32[]{:S(2)}, u32[]{:S(2)}) collective-permute-start(f32[512]{0:T(512)S(1)} %add.384), channel_id=1, source_target_pairs={{0,64},{1,65},{2,66},{3,67},{4,68},{5,69},{6,70},{7,71},{8,72},{9,... | collective-permute-start | bytes 6152 | tf_op jit(solution)/shard_map/ppermute | solution.py:22
  128.8 5.8 %collective-permute-start.33 = (f32[512]{0:T(512)S(1)}, f32[512]{0:T(512)S(1)}, u32[]{:S(2)}, u32[]{:S(2)}) collective-permute-start(f32[512]{0:T(512)S(1)} %add_add_fusion.2), channel_id=1, source_target_pairs={{0,8},{1,9},{2,10},{3,11},{4,12},{5,13},{6,14},{7,15},{8,0},{9,1},... | collective-permute-start | bytes 6152 | tf_op jit(solution)/shard_map/ppermute | solution.py:22
  136.1 16.7 %collective-permute-start.36 = (f32[512]{0:T(512)S(1)}, f32[512]{0:T(512)S(1)}, u32[]{:S(2)}, u32[]{:S(2)}) collective-permute-start(f32[512]{0:T(512)S(1)} %add_add_fusion.1), channel_id=1, source_target_pairs={{0,2},{1,3},{2,0},{3,1},{4,6},{5,7},{6,4},{7,5},{8,10},{9,11},{10,... | collective-permute-start | bytes 6152 | tf_op jit(solution)/shard_map/ppermute | solution.py:22
  137.7 15.1 %collective-permute-start.37 = (f32[512]{0:T(512)S(1)}, f32[512]{0:T(512)S(1)}, u32[]{:S(2)}, u32[]{:S(2)}) collective-permute-start(f32[512]{0:T(512)S(1)} %add_add_fusion.1), channel_id=1, source_target_pairs={{0,1},{1,2},{2,3},{3,0},{4,5},{5,6},{6,7},{7,4},{8,9},{9,10},{10,1... | collective-permute-start | bytes 6152 | tf_op jit(solution)/shard_map/ppermute | solution.py:22
  138.3 14.6 %collective-permute-start.38 = (f32[512]{0:T(512)S(1)}, f32[512]{0:T(512)S(1)}, u32[]{:S(2)}, u32[]{:S(2)}) collective-permute-start(f32[512]{0:T(512)S(1)} %add_add_fusion.1), channel_id=1, source_target_pairs={{0,3},{1,0},{2,1},{3,2},{4,7},{5,4},{6,5},{7,6},{8,11},{9,8},{10,9... | collective-permute-start | bytes 6152 | tf_op jit(solution)/shard_map/ppermute | solution.py:22
  157.3 9.4 %collective-permute-start.11 = (bf16[4,4,16,512]{3,2,1,0:T(8,128)(2,1)S(1)}, bf16[4,4,16,512]{3,2,1,0:T(8,128)(2,1)S(1)}, u32[]{:S(2)}, u32[]{:S(2)}) collective-permute-start(bf16[4,4,16,512]{3,2,1,0:T(8,128)(2,1)S(1)} %get-tuple-element.10), channel_id=1, source_target_pairs={{0,8},{1,9},{2,10},{3,11},{4,12},{5,13},{6,14},{7,15},{8,0},{9,1},... | collective-permute-start | bytes 786440 | tf_op jit(solution)/shard_map/ppermute | solution.py:22
  159.0 10.4 %collective-permute-start.12 = (bf16[4,4,16,512]{3,2,1,0:T(8,128)(2,1)S(1)}, bf16[4,4,16,512]{3,2,1,0:T(8,128)(2,1)S(1)}, u32[]{:S(2)}, u32[]{:S(2)}) collective-permute-start(bf16[4,4,16,512]{3,2,1,0:T(8,128)(2,1)S(1)} %get-tuple-element.12), channel_id=1, source_target_pairs={{0,4},{1,5},{2,6},{3,7},{4,8},{5,9},{6,10},{7,11},{8,12},{9,13},{1... | collective-permute-start | bytes 786440 | tf_op jit(solution)/shard_map/ppermute | solution.py:22
  161.5 8.3 %collective-permute-start.13 = (bf16[4,4,16,512]{3,2,1,0:T(8,128)(2,1)S(1)}, bf16[4,4,16,512]{3,2,1,0:T(8,128)(2,1)S(1)}, u32[]{:S(2)}, u32[]{:S(2)}) collective-permute-start(bf16[4,4,16,512]{3,2,1,0:T(8,128)(2,1)S(1)} %get-tuple-element.11), channel_id=1, source_target_pairs={{0,12},{1,13},{2,14},{3,15},{4,0},{5,1},{6,2},{7,3},{8,4},{9,5},{1... | collective-permute-start | bytes 786440 | tf_op jit(solution)/shard_map/ppermute | solution.py:22
  162.4 38.3 %collective-permute-start.2 = (bf16[4,4,24,512]{3,2,1,0:T(8,128)(2,1)S(1)}, bf16[4,4,24,512]{3,2,1,0:T(8,128)(2,1)S(1)}, u32[]{:S(2)}, u32[]{:S(2)}) collective-permute-start(bf16[4,4,24,512]{3,2,1,0:T(8,128)(2,1)S(1)} %get-tuple-element.7), channel_id=1, source_target_pairs={{0,64},{1,65},{2,66},{3,67},{4,68},{5,69},{6,70},{7,71},{8,72},{9,... | collective-permute-start | bytes 1179656 | tf_op jit(solution)/shard_map/ppermute | solution.py:22
  163.8 39.3 %collective-permute-start.3 = (bf16[4,4,24,512]{3,2,1,0:T(8,128)(2,1)S(1)}, bf16[4,4,24,512]{3,2,1,0:T(8,128)(2,1)S(1)}, u32[]{:S(2)}, u32[]{:S(2)}) collective-permute-start(bf16[4,4,24,512]{3,2,1,0:T(8,128)(2,1)S(1)} %get-tuple-element.9), channel_id=1, source_target_pairs={{0,32},{1,33},{2,34},{3,35},{4,36},{5,37},{6,38},{7,39},{8,40},{9,... | collective-permute-start | bytes 1179656 | tf_op jit(solution)/shard_map/ppermute | solution.py:22
  166.7 9.5 %collective-permute-start.20 = (bf16[4,4,16,512]{3,2,1,0:T(8,128)(2,1)S(1)}, bf16[4,4,16,512]{3,2,1,0:T(8,128)(2,1)S(1)}, u32[]{:S(2)}, u32[]{:S(2)}) collective-permute-start(bf16[4,4,16,512]{3,2,1,0:T(8,128)(2,1)S(1)} %get-tuple-element.13), channel_id=1, source_target_pairs={{0,2},{1,3},{2,0},{3,1},{4,6},{5,7},{6,4},{7,5},{8,10},{9,11},{10,... | collective-permute-start | bytes 786440 | tf_op jit(solution)/shard_map/ppermute | solution.py:22
  169.4 10.8 %collective-permute-start.21 = (bf16[4,4,16,512]{3,2,1,0:T(8,128)(2,1)S(1)}, bf16[4,4,16,512]{3,2,1,0:T(8,128)(2,1)S(1)}, u32[]{:S(2)}, u32[]{:S(2)}) collective-permute-start(bf16[4,4,16,512]{3,2,1,0:T(8,128)(2,1)S(1)} %get-tuple-element.15), channel_id=1, source_target_pairs={{0,1},{1,2},{2,3},{3,0},{4,5},{5,6},{6,7},{7,4},{8,9},{9,10},{10,1... | collective-permute-start | bytes 786440 | tf_op jit(solution)/shard_map/ppermute | solution.py:22
  169.8 10.4 %collective-permute-start.22 = (bf16[4,4,16,512]{3,2,1,0:T(8,128)(2,1)S(1)}, bf16[4,4,16,512]{3,2,1,0:T(8,128)(2,1)S(1)}, u32[]{:S(2)}, u32[]{:S(2)}) collective-permute-start(bf16[4,4,16,512]{3,2,1,0:T(8,128)(2,1)S(1)} %get-tuple-element.14), channel_id=1, source_target_pairs={{0,3},{1,0},{2,1},{3,2},{4,7},{5,4},{6,5},{7,6},{8,11},{9,8},{10,9... | collective-permute-start | bytes 786440 | tf_op jit(solution)/shard_map/ppermute | solution.py:22
  176.2 7.4 %collective-permute-start.14 = (bf16[4,16,512]{2,1,0:T(8,128)(2,1)S(1)}, bf16[4,16,512]{2,1,0:T(8,128)(2,1)S(1)}, u32[]{:S(2)}, u32[]{:S(2)}) collective-permute-start(bf16[4,16,512]{2,1,0:T(8,128)(2,1)S(1)} %get-tuple-element.19), channel_id=1, source_target_pairs={{0,2},{1,3},{2,0},{3,1},{4,6},{5,7},{6,4},{7,5},{8,10},{9,11},{10,... | collective-permute-start | bytes 196616 | tf_op jit(solution)/shard_map/ppermute | solution.py:22
  180.2 6.1 %collective-permute-start.15 = (bf16[4,16,512]{2,1,0:T(8,128)(2,1)S(1)}, bf16[4,16,512]{2,1,0:T(8,128)(2,1)S(1)}, u32[]{:S(2)}, u32[]{:S(2)}) collective-permute-start(bf16[4,16,512]{2,1,0:T(8,128)(2,1)S(1)} %get-tuple-element.21), channel_id=1, source_target_pairs={{0,1},{1,2},{2,3},{3,0},{4,5},{5,6},{6,7},{7,4},{8,9},{9,10},{10,1... | collective-permute-start | bytes 196616 | tf_op jit(solution)/shard_map/ppermute | solution.py:22
  180.2 6.9 %collective-permute-start.16 = (bf16[4,16,512]{2,1,0:T(8,128)(2,1)S(1)}, bf16[4,16,512]{2,1,0:T(8,128)(2,1)S(1)}, u32[]{:S(2)}, u32[]{:S(2)}) collective-permute-start(bf16[4,16,512]{2,1,0:T(8,128)(2,1)S(1)} %get-tuple-element.20), channel_id=1, source_target_pairs={{0,3},{1,0},{2,1},{3,2},{4,7},{5,4},{6,5},{7,6},{8,11},{9,8},{10,9... | collective-permute-start | bytes 196616 | tf_op jit(solution)/shard_map/ppermute | solution.py:22
  183.6 20.9 %collective-permute-start.4 = (bf16[4,4,24,512]{3,2,1,0:T(8,128)(2,1)S(1)}, bf16[4,4,24,512]{3,2,1,0:T(8,128)(2,1)S(1)}, u32[]{:S(2)}, u32[]{:S(2)}) collective-permute-start(bf16[4,4,24,512]{3,2,1,0:T(8,128)(2,1)S(1)} %get-tuple-element.8), channel_id=1, source_target_pairs={{0,96},{1,97},{2,98},{3,99},{4,100},{5,101},{6,102},{7,103},{8,104... | collective-permute-start | bytes 1179656 | tf_op jit(solution)/shard_map/ppermute | solution.py:22
  186.3 5.8 %collective-permute-start.23 = (bf16[4,16,512]{2,1,0:T(8,128)(2,1)S(1)}, bf16[4,16,512]{2,1,0:T(8,128)(2,1)S(1)}, u32[]{:S(2)}, u32[]{:S(2)}) collective-permute-start(bf16[4,16,512]{2,1,0:T(8,128)(2,1)S(1)} %get-tuple-element.22), channel_id=1, source_target_pairs={{0,64},{1,65},{2,66},{3,67},{4,68},{5,69},{6,70},{7,71},{8,72},{9,... | collective-permute-start | bytes 196616 | tf_op jit(solution)/shard_map/ppermute | solution.py:22
  187.1 10.1 %collective-permute-start.24 = (bf16[4,16,512]{2,1,0:T(8,128)(2,1)S(1)}, bf16[4,16,512]{2,1,0:T(8,128)(2,1)S(1)}, u32[]{:S(2)}, u32[]{:S(2)}) collective-permute-start(bf16[4,16,512]{2,1,0:T(8,128)(2,1)S(1)} %get-tuple-element.24), channel_id=1, source_target_pairs={{0,32},{1,33},{2,34},{3,35},{4,36},{5,37},{6,38},{7,39},{8,40},{9,... | collective-permute-start | bytes 196616 | tf_op jit(solution)/shard_map/ppermute | solution.py:22
  192.1 7.0 %collective-permute-start.25 = (bf16[4,16,512]{2,1,0:T(8,128)(2,1)S(1)}, bf16[4,16,512]{2,1,0:T(8,128)(2,1)S(1)}, u32[]{:S(2)}, u32[]{:S(2)}) collective-permute-start(bf16[4,16,512]{2,1,0:T(8,128)(2,1)S(1)} %get-tuple-element.23), channel_id=1, source_target_pairs={{0,96},{1,97},{2,98},{3,99},{4,100},{5,101},{6,102},{7,103},{8,104... | collective-permute-start | bytes 196616 | tf_op jit(solution)/shard_map/ppermute | solution.py:22
  197.1 7.7 %collective-permute-start.17 = (bf16[16,512]{1,0:T(8,128)(2,1)S(1)}, bf16[16,512]{1,0:T(8,128)(2,1)S(1)}, u32[]{:S(2)}, u32[]{:S(2)}) collective-permute-start(bf16[16,512]{1,0:T(8,128)(2,1)S(1)} %get-tuple-element.28), channel_id=1, source_target_pairs={{0,64},{1,65},{2,66},{3,67},{4,68},{5,69},{6,70},{7,71},{8,72},{9,... | collective-permute-start | bytes 49160 | tf_op jit(solution)/shard_map/ppermute | solution.py:22
  199.1 7.9 %collective-permute-start.18 = (bf16[16,512]{1,0:T(8,128)(2,1)S(1)}, bf16[16,512]{1,0:T(8,128)(2,1)S(1)}, u32[]{:S(2)}, u32[]{:S(2)}) collective-permute-start(bf16[16,512]{1,0:T(8,128)(2,1)S(1)} %get-tuple-element.30), channel_id=1, source_target_pairs={{0,32},{1,33},{2,34},{3,35},{4,36},{5,37},{6,38},{7,39},{8,40},{9,... | collective-permute-start | bytes 49160 | tf_op jit(solution)/shard_map/ppermute | solution.py:22
  200.7 8.3 %collective-permute-start.19 = (bf16[16,512]{1,0:T(8,128)(2,1)S(1)}, bf16[16,512]{1,0:T(8,128)(2,1)S(1)}, u32[]{:S(2)}, u32[]{:S(2)}) collective-permute-start(bf16[16,512]{1,0:T(8,128)(2,1)S(1)} %get-tuple-element.29), channel_id=1, source_target_pairs={{0,96},{1,97},{2,98},{3,99},{4,100},{5,101},{6,102},{7,103},{8,104... | collective-permute-start | bytes 49160 | tf_op jit(solution)/shard_map/ppermute | solution.py:22
  203.1 12.1 %collective-permute-start.26 = (bf16[16,512]{1,0:T(8,128)(2,1)S(1)}, bf16[16,512]{1,0:T(8,128)(2,1)S(1)}, u32[]{:S(2)}, u32[]{:S(2)}) collective-permute-start(bf16[16,512]{1,0:T(8,128)(2,1)S(1)} %get-tuple-element.31), channel_id=1, source_target_pairs={{0,8},{1,9},{2,10},{3,11},{4,12},{5,13},{6,14},{7,15},{8,0},{9,1},... | collective-permute-start | bytes 49160 | tf_op jit(solution)/shard_map/ppermute | solution.py:22
  204.6 11.9 %collective-permute-start.27 = (bf16[16,512]{1,0:T(8,128)(2,1)S(1)}, bf16[16,512]{1,0:T(8,128)(2,1)S(1)}, u32[]{:S(2)}, u32[]{:S(2)}) collective-permute-start(bf16[16,512]{1,0:T(8,128)(2,1)S(1)} %get-tuple-element.33), channel_id=1, source_target_pairs={{0,4},{1,5},{2,6},{3,7},{4,8},{5,9},{6,10},{7,11},{8,12},{9,13},{1... | collective-permute-start | bytes 49160 | tf_op jit(solution)/shard_map/ppermute | solution.py:22
  204.8 6.2 %collective-permute-start.5 = (bf16[4,24,512]{2,1,0:T(8,128)(2,1)S(1)}, bf16[4,24,512]{2,1,0:T(8,128)(2,1)S(1)}, u32[]{:S(2)}, u32[]{:S(2)}) collective-permute-start(bf16[4,24,512]{2,1,0:T(8,128)(2,1)S(1)} %get-tuple-element.16), channel_id=1, source_target_pairs={{0,8},{1,9},{2,10},{3,11},{4,12},{5,13},{6,14},{7,15},{8,0},{9,1},... | collective-permute-start | bytes 294920 | tf_op jit(solution)/shard_map/ppermute | solution.py:22
  207.0 7.3 %collective-permute-start.6 = (bf16[4,24,512]{2,1,0:T(8,128)(2,1)S(1)}, bf16[4,24,512]{2,1,0:T(8,128)(2,1)S(1)}, u32[]{:S(2)}, u32[]{:S(2)}) collective-permute-start(bf16[4,24,512]{2,1,0:T(8,128)(2,1)S(1)} %get-tuple-element.18), channel_id=1, source_target_pairs={{0,4},{1,5},{2,6},{3,7},{4,8},{5,9},{6,10},{7,11},{8,12},{9,13},{1... | collective-permute-start | bytes 294920 | tf_op jit(solution)/shard_map/ppermute | solution.py:22
  211.0 5.4 %collective-permute-start.28 = (bf16[16,512]{1,0:T(8,128)(2,1)S(1)}, bf16[16,512]{1,0:T(8,128)(2,1)S(1)}, u32[]{:S(2)}, u32[]{:S(2)}) collective-permute-start(bf16[16,512]{1,0:T(8,128)(2,1)S(1)} %get-tuple-element.32), channel_id=1, source_target_pairs={{0,12},{1,13},{2,14},{3,15},{4,0},{5,1},{6,2},{7,3},{8,4},{9,5},{1... | collective-permute-start | bytes 49160 | tf_op jit(solution)/shard_map/ppermute | solution.py:22
  215.2 5.7 %collective-permute-start.9 = (bf16[24,512]{1,0:T(8,128)(2,1)S(1)}, bf16[24,512]{1,0:T(8,128)(2,1)S(1)}, u32[]{:S(2)}, u32[]{:S(2)}) collective-permute-start(bf16[24,512]{1,0:T(8,128)(2,1)S(1)} %get-tuple-element.27), channel_id=1, source_target_pairs={{0,1},{1,2},{2,3},{3,0},{4,5},{5,6},{6,7},{7,4},{8,9},{9,10},{10,1... | collective-permute-start | bytes 73736 | tf_op jit(solution)/shard_map/ppermute | solution.py:22
  (14 other events, 144.3 us)
Sparse Core Ops, SparseCore 0:
  10.8 52.3 all-gather.2

commit v2 on v0

v2 whole, which is shorter than its diff:
```python
import jax
import jax.numpy as jnp
from jax import lax
from jax.sharding import PartitionSpec as P

epsilon = 1e-06
axes = ("dp", "shard")


def device(x, core, y, z):
    return (x * 2 + core) * 16 + y * 4 + z


four = range(4)
along_y = [[y * 4 + z for y in four] for z in four]
along_z = [[y * 4 + z for z in four] for y in four]
chips = [[device(x, c, y, z) for x in four for y in four for z in four] for c in range(2)]
cores = [(device(x, c, y, z), device(x, 1 - c, y, z)) for x in four for c in range(2) for y in four for z in four]


def twin(value):
    return lax.ppermute(value, axes, cores)


def gather(value, groups):
    copies = jnp.broadcast_to(value[None], (4,) + value.shape)
    return lax.all_to_all(copies, "shard", 0, 0, axis_index_groups=groups, tiled=True)


def shards(inputs, cotangent, weight, norm_gain):
    core = lax.axis_index("dp") % 2
    half = lax.dynamic_slice_in_dim(weight, core * 224, 224, 0)
    first = gather(gather(half[:112], along_y), along_z)
    second = gather(gather(half[112:], along_z), along_y)
    mine = jnp.stack([first.swapaxes(0, 1), second], 2)
    other = twin(mine)
    gathered = jnp.where(core == 0, jnp.stack([mine, other], 2), jnp.stack([other, mine], 2))
    gathered = gathered.reshape(7168, 512)
    latent = jnp.dot(inputs, gathered, preferred_element_type=jnp.float32)
    inverse_scale = lax.rsqrt(jnp.mean(latent * latent, axis=-1, keepdims=True) + epsilon)
    normed = latent * inverse_scale
    upstream = cotangent.astype(jnp.float32)
    gain_grad = jnp.sum(upstream * normed, axis=0)
    gain_grad = jnp.broadcast_to(gain_grad.reshape(1, 4, 128), (128, 4, 128))
    gain_grad = lax.all_to_all(gain_grad, axes, 0, 0, tiled=True)
    gain_grad = jnp.sum(gain_grad, axis=0).reshape(512)
    scaled = upstream * norm_gain
    center = jnp.mean(scaled * normed, axis=-1, keepdims=True)
    latent_grad = (inverse_scale * (scaled - normed * center)).astype(jnp.bfloat16)
    partial = lax.dot_general(
        inputs, latent_grad, (((0,), (0,)), ((), ())), preferred_element_type=jnp.float32
    ).astype(jnp.bfloat16)
    partial = partial.reshape(4, 2, 16, 56, 512)
    kept = lax.dynamic_index_in_dim(partial, core, 1, keepdims=False)
    sent = lax.dynamic_index_in_dim(partial, 1 - core, 1, keepdims=False)
    both = (kept.astype(jnp.float32) + twin(sent).astype(jnp.float32)).astype(jnp.bfloat16)
    pieces = lax.all_to_all(both.reshape(64, 56, 512), axes, 0, 0, axis_index_groups=chips, tiled=True)
    weight_grad = jnp.sum(pieces.astype(jnp.float32), axis=0)
    input_grad = lax.dot_general(
        latent_grad, gathered, (((1,), (1,)), ((), ())), preferred_element_type=jnp.float32
    )
    return (input_grad.astype(jnp.bfloat16), weight_grad, gain_grad)


def solution(mesh):
    placed = (P(("dp", "shard"), None), P(("dp", "shard"), None), P("shard", None), P())
    return jax.shard_map(
        shards,
        mesh=mesh,
        in_specs=placed,
        out_specs=(P(("dp", "shard"), None), P(("dp", "shard"), None), P()),
        check_vma=False,
    )
```

time: 792 us -> 211 us (0.27)
  waiting for transfers between devices: 655 us -> 63.6 us
  other arithmetic: 1.04 us -> 23.9 us
  blocking collectives: 66.6 us -> 49.3 us
  starting transfers between devices: 0.08 us -> 16.5 us
  between operations: 14.1 us -> 0.79 us
    unnamed x3 -> x0, waiting for transfers between devices: 585 us -> none
    all_gather x1 -> x0, waiting for transfers between devices: 69.6 us -> none  [shards(): gathered = lax.all_gather(weight, 'shard', axis=0, tiled=True)]
    psum x1 -> x0, blocking collectives: 66.6 us -> none  [shards(): gain_grad = lax.psum(jnp.sum(upstream * normed, axis=0), ('dp', 'shard'))]
    all_to_all x0 -> x3, waiting for transfers between devices: none -> 57.1 us  [the longest x1 33.9 us: shards(): lax.all_to_all(both.reshape(64, 56, 512), axes, 0, 0, axis_index_groups=c...]
    all_to_all x0 -> x3, blocking collectives: none -> 49.3 us  [gather(): lax.all_to_all(copies, 'shard', 0, 0, axis_index_groups=groups, tiled=True)]
    unnamed x4 -> x7, local copies, waits for them, and re-layouts: 16.7 us -> 0.29 us
    all_to_all x0 -> x3, starting transfers between devices: none -> 16.4 us  [the longest x1 6.18 us: shards(): gain_grad = lax.all_to_all(gain_grad, axes, 0, 0, tiled=True)]
    convert_element_type x0 -> x1, local copies, waits for them, and re-layouts: none -> 10.4 us  [shards(): partial = lax.dot_general(inputs, latent_grad, (((0,), (0,)), ((), ())),...]
  transfers between devices with their start and end apart: 2 -> 5, of which waited for: 2 -> 4; matrix products, arithmetic and copies ran while one was open for 2% -> 10% of each run, Pallas kernels for 0% -> 0%
where the time goes in v2:
time: 211 us; the launch traced here: 209 us
  waiting for transfers between devices  63.6 us (30%)
  blocking collectives  49.3 us (23%)
  matrix products  35.2 us (17%)
  other arithmetic  23.9 us (11%)
  local copies, waits for them, and re-layouts  19.7 us (9%)
  starting transfers between devices  16.5 us (8%)
    all_to_all x3, blocking collectives, gather(): lax.all_to_all(copies, 'shard', 0, 0, axis_index_groups=groups, tiled=True)  49.3 us
    all_to_all x1, waiting for transfers between devices, shards(): lax.all_to_all(both.reshape(64, 56, 512), axes, 0, 0, axis_index_groups=c...  33.9 us
    all_to_all x1, waiting for transfers between devices, gather(): lax.all_to_all(copies, 'shard', 0, 0, axis_index_groups=groups, tiled=True)  18.4 us
    dot_general x1, matrix products, shards(): lax.dot_general(inputs, latent_grad, (((0,), (0,)), ((), ())), preferred_...  12 us
    dot_general x1, matrix products, shards(): lax.dot_general(latent_grad, gathered, (((1,), (1,)), ((), ())), preferre...  11.9 us
    dot_general x1, matrix products, shards(): latent = jnp.dot(inputs, gathered, preferred_element_type=jnp.float32)  11.2 us
    convert_element_type x1, local copies, waits for them, and re-layouts, shards(): partial = lax.dot_general(inputs, latent_grad, (((0,), (0,)), ((), ())),...  10.4 us
    select_n x1, other arithmetic, shards(): jnp.where(core == 0, jnp.stack([mine, other], 2), jnp.stack([other, mine]...  7.25 us
  transfers between devices with their start and end apart: 5, of which 4 were waited for; matrix products, arithmetic and copies ran while one was open for 10% of the time, Pallas kernels for 0%

profile of v2, /device:TPU:0, one launch (start us, length us, event | category | flops | bytes accessed | tf_op | source)
XLA Modules:
  0.0 208.9 jit_solution(11999767654834056935)
XLA Ops:
  0.6 1.0 constant_dynamic-slice_fusion
  1.7 13.1 %all_to_all.30 = bf16[4,112,512]{2,1,0:T(8,128)(2,1)S(1)} all-to-all(bf16[4,112,512]{2,1,0:T(8,128)(2,1)S(1)} %broadcast_in_dim.12), channel_id=1, replica_groups={{0,4,8,12},{1,5,9,13},{2,6,10,14},{3,7,11,15},{16,20,24,28},{17,21,25,2..., dimensions={0} | all-to-all | bytes 917504 | tf_op jit(solution)/shard_map/all_to_all | solution.py:27
  14.8 12.8 %all_to_all.31 = bf16[4,112,512]{2,1,0:T(8,128)(2,1)S(1)} all-to-all(bf16[4,112,512]{2,1,0:T(8,128)(2,1)S(1)} %broadcast_in_dim.14), channel_id=1, replica_groups={{0,1,2,3},{4,5,6,7},{8,9,10,11},{12,13,14,15},{16,17,18,19},{20,21,22,2..., dimensions={0} | all-to-all | bytes 917504 | tf_op jit(solution)/shard_map/all_to_all | solution.py:27
  27.7 0.2 broadcast_in_dim.13
  27.8 23.3 %all_to_all.32 = bf16[4,4,112,512]{3,2,1,0:T(8,128)(2,1)S(1)} all-to-all(bf16[4,4,112,512]{3,2,1,0:T(8,128)(2,1)S(1)} %broadcast_in_dim.13), channel_id=1, replica_groups={{0,1,2,3},{4,5,6,7},{8,9,10,11},{12,13,14,15},{16,17,18,19},{20,21,22,2..., dimensions={0} | all-to-all | bytes 3670016 | tf_op jit(solution)/shard_map/all_to_all | solution.py:27
  51.2 1.4 broadcast_in_dim.15
  52.6 4.4 %all-to-all-start.3 = ((bf16[4,4,112,512]{3,2,1,0:T(8,128)(2,1)}), bf16[4,4,112,512]{3,2,1,0:T(8,128)(2,1)}, u32[]{:S(2)}, u32[]{:S(2)}) async-start(bf16[4,4,112,512]{3,2,1,0:T(8,128)(2,1)} %broadcast_in_dim.15), calls=%async_computation.3 | async-start | bytes 3670016 | tf_op jit(solution)/shard_map/all_to_all | solution.py:27
  57.0 1.4 copy.24
  58.5 18.4 %all-to-all-done.3 = bf16[4,4,112,512]{3,2,1,0:T(8,128)(2,1)} async-done(((bf16[4,4,112,512]{3,2,1,0:T(8,128)(2,1)}), bf16[4,4,112,512]{3,2,1,0:T(8,128)(2,1)}, u32[]{:S(2)}, u32[]{:S(2)}) %all-to-all-start.3) | async-done | bytes 1835040 | tf_op jit(solution)/shard_map/all_to_all | solution.py:27
  76.9 5.6 %fusion.8 = (bf16[4,4,1,2,112,512]{5,4,3,2,1,0:T(8,128)(2,1)}, bf16[4,4,2,112,512]{4,3,2,1,0:T(8,128)(2,1)}) fusion(bf16[4,4,1,112,512]{4,3,2,1,0:T(8,128)(2,1)} %bitcast.2, bf16[4,4,1,112,512]{4,3,2,1,0:T(8,128)(2,1)} %bitcast.38), kind=kLoop, calls=%fused_computation.24 | loop fusion | flops 1835008 | bytes 11010048 | tf_op jit(solution)/shard_map/stack | solution.py:37
  82.5 0.0 collective-permute-start
  82.5 0.3 copy.19
  82.8 6.5 %collective-permute-done = bf16[4,4,2,112,512]{4,3,2,1,0:T(8,128)(2,1)} collective-permute-done((bf16[4,4,2,112,512]{4,3,2,1,0:T(8,128)(2,1)}, bf16[4,4,2,112,512]{4,3,2,1,0:T(8,128)(2,1)}, u32[]{:S(2)}, u32[]{:S(2)}) %collective-permute-start) | collective-permute-done | bytes 3670048 | tf_op jit(solution)/shard_map/ppermute | solution.py:22
  89.2 7.2 %maximum_select_fusion = bf16[4,4,2,2,112,512]{5,4,3,2,1,0:T(8,128)(2,1)S(1)} fusion(bf16[4,4,1,2,112,512]{5,4,3,2,1,0:T(8,128)(2,1)} %bitcast.4, bf16[4,4,1,2,112,512]{5,4,3,2,1,0:T(8,128)(2,1)} %get-tuple-element.5, pred[]{:T(512)S(6)} %eq.5), kind=kLoop, calls=%fused_computation.3 | loop fusion | flops 11010048 | bytes 14680065 | tf_op jit(solution)/shard_map/jit(_where)/select_n | solution.py:37
  96.5 0.0 copy-start.2
  96.5 11.2 %multiply_reduce_fusion = (f32[768]{0:T(1024)S(1)}, f32[512,768]{1,0:T(8,128)S(1)}) fusion(bf16[7168,512]{1,0:T(8,128)(2,1)S(1)} %bitcast.36, bf16[768,7168]{1,0:T(8,128)(2,1)} %param.4), kind=kOutput, calls=%fused_computation.19 | convolution fusion | flops 5637929984 | bytes 19926016 | tf_op jit(solution)/shard_map/dot_general | solution.py:39
  107.8 0.6 fusion.7
  108.4 0.4 fusion.6
  108.8 12.0 %fusion = bf16[7168,512]{0,1:T(8,128)(2,1)} fusion(bf16[768,512]{0,1:T(8,128)(2,1)S(1)} %fusion.6, bf16[768,7168]{1,0:T(8,128)(2,1)} %param.4), kind=kOutput, calls=%fused_computation.2 | convolution fusion | flops 5640814592 | bytes 19136512 | tf_op jit(solution)/shard_map/dot_general | solution.py:50
  120.8 10.4 %copy.20 = bf16[7168,512]{1,0:T(8,128)(2,1)} copy(bf16[7168,512]{0,1:T(8,128)(2,1)} %fusion) | data formatting | bytes 14680064 | tf_op jit(solution)/shard_map/convert_element_type | solution.py:52
  131.2 4.2 %dynamic-slice_bitcast_fusion = bf16[4,16,56,512]{3,2,1,0:T(8,128)(2,1)} fusion(bf16[4,2,16,56,512]{4,3,2,1,0:T(8,128)(2,1)} %bitcast.33, s32[]{:T(128)S(6)} %select_n.35), kind=kLoop, calls=%fused_computation.8 | loop fusion | bytes 7340036 | tf_op jit(solution)/shard_map/jit(dynamic_index_in_dim)/squeeze | solution.py:55
  135.4 0.1 collective-permute-start.1
  135.5 0.8 broadcast_in_dim.17
  136.3 6.2 %all-to-all-start.5 = ((f32[128,4,128]{2,1,0:T(4,128)}), f32[128,4,128]{2,1,0:T(4,128)S(1)}, u32[]{:S(2)}, u32[]{:S(2)}) async-start(f32[128,4,128]{2,1,0:T(4,128)} %broadcast_in_dim.17), calls=%async_computation.5 | async-start | bytes 524288 | tf_op jit(solution)/shard_map/all_to_all | solution.py:45
  142.5 0.0 collective-permute-done.1
  142.5 6.1 %fusion.1 = bf16[4,16,56,512]{3,2,1,0:T(8,128)(2,1)} fusion(bf16[4,16,56,512]{3,2,1,0:T(8,128)(2,1)} %collective-permute-done.1, bf16[4,2,16,56,512]{4,3,2,1,0:T(8,128)(2,1)} %bitcast.34, s32[]{:T(128)S(6)} %select_n.34), kind=kLoop, calls=%fused_computation.5 | loop fusion | flops 7340032 | bytes 11010052 | tf_op jit(solution)/shard_map/convert_element_type | solution.py:56
  148.6 4.8 %all-to-all-done.5 = f32[128,4,128]{2,1,0:T(4,128)S(1)} async-done(((f32[128,4,128]{2,1,0:T(4,128)}), f32[128,4,128]{2,1,0:T(4,128)S(1)}, u32[]{:S(2)}, u32[]{:S(2)}) %all-to-all-start.5) | async-done | bytes 262176 | tf_op jit(solution)/shard_map/all_to_all | solution.py:45
  153.4 5.8 %all-to-all-start.4 = ((bf16[64,56,512]{2,1,0:T(8,128)(2,1)}), bf16[64,56,512]{2,1,0:T(8,128)(2,1)}, u32[]{:S(2)}, u32[]{:S(2)}) async-start(bf16[64,56,512]{2,1,0:T(8,128)(2,1)} %bitcast.35), calls=%async_computation.4 | async-start | bytes 7340032 | tf_op jit(solution)/shard_map/all_to_all | solution.py:57
  159.2 11.9 %convolution_convert_fusion = bf16[768,7168]{1,0:T(8,128)(2,1)} fusion(bf16[768,512]{0,1:T(8,128)(2,1)S(1)} %fusion.6, bf16[7168,512]{1,0:T(8,128)(2,1)} %bitcast.37), kind=kOutput, calls=%fused_computation | convolution fusion | flops 5642649600 | bytes 19136512 | tf_op jit(solution)/shard_map/dot_general | solution.py:59
  171.1 0.7 reduce_sum.49
  171.8 33.9 %all-to-all-done.4 = bf16[64,56,512]{2,1,0:T(8,128)(2,1)} async-done(((bf16[64,56,512]{2,1,0:T(8,128)(2,1)}), bf16[64,56,512]{2,1,0:T(8,128)(2,1)}, u32[]{:S(2)}, u32[]{:S(2)}) %all-to-all-start.4) | async-done | bytes 3670048 | tf_op jit(solution)/shard_map/all_to_all | solution.py:57
  205.7 3.2 %convert_reduce_fusion = f32[56,512]{1,0:T(8,128)} fusion(bf16[64,56,512]{2,1,0:T(8,128)(2,1)} %all-to-all-done.4), kind=kLoop, calls=%fused_computation.6 | loop fusion | flops 3641344 | bytes 3784704 | tf_op jit(solution)/shard_map/reduce_sum | solution.py:58
  (9 shorter events, 0.1 us)
Async XLA Ops:
  52.6 24.2 %all-to-all-start.3 = ((bf16[4,4,112,512]{3,2,1,0:T(8,128)(2,1)}), bf16[4,4,112,512]{3,2,1,0:T(8,128)(2,1)}, u32[]{:S(2)}, u32[]{:S(2)}) async-start(bf16[4,4,112,512]{3,2,1,0:T(8,128)(2,1)} %broadcast_in_dim.15), calls=%async_computation.3 | async-start | bytes 3670016 | tf_op jit(solution)/shard_map/all_to_all | solution.py:27
  76.9 5.7 %copy-start.1 = (bf16[768,512]{1,0:T(8,128)(2,1)S(1)}, bf16[768,512]{1,0:T(8,128)(2,1)}, u32[]{:S(2)}) copy-start(bf16[768,512]{1,0:T(8,128)(2,1)} %param.5) | copy-start | bytes 2359300
  82.5 6.8 %collective-permute-start = (bf16[4,4,2,112,512]{4,3,2,1,0:T(8,128)(2,1)}, bf16[4,4,2,112,512]{4,3,2,1,0:T(8,128)(2,1)}, u32[]{:S(2)}, u32[]{:S(2)}) collective-permute-start(bf16[4,4,2,112,512]{4,3,2,1,0:T(8,128)(2,1)} %get-tuple-element.6), channel_id=1, source_target_pairs={{0,16},{1,17},{2,18},{3,19},{4,20},{5,21},{6,22},{7,23},{8,24},{9,... | collective-permute-start | bytes 11010056 | tf_op jit(solution)/shard_map/ppermute | solution.py:22
  96.5 11.3 %copy-start = (bf16[4,4,2,2,112,512]{5,4,3,2,1,0:T(8,128)(2,1)}, bf16[4,4,2,2,112,512]{5,4,3,2,1,0:T(8,128)(2,1)S(1)}, u32[]{:S(2)}) copy-start(bf16[4,4,2,2,112,512]{5,4,3,2,1,0:T(8,128)(2,1)S(1)} %maximum_select_fusion) | copy-start | bytes 22020100
  96.5 11.3 %copy-start.2 = (f32[512]{0:T(512)S(1)}, f32[512]{0:T(512)}, u32[]{:S(2)}) copy-start(f32[512]{0:T(512)} %param.7) | copy-start | bytes 6148
  135.4 7.1 %collective-permute-start.1 = (bf16[4,16,56,512]{3,2,1,0:T(8,128)(2,1)}, bf16[4,16,56,512]{3,2,1,0:T(8,128)(2,1)}, u32[]{:S(2)}, u32[]{:S(2)}) collective-permute-start(bf16[4,16,56,512]{3,2,1,0:T(8,128)(2,1)} %dynamic-slice_bitcast_fusion), channel_id=1, source_target_pairs={{0,16},{1,17},{2,18},{3,19},{4,20},{5,21},{6,22},{7,23},{8,24},{9,... | collective-permute-start | bytes 11010056 | tf_op jit(solution)/shard_map/ppermute | solution.py:22
  136.3 17.1 %all-to-all-start.5 = ((f32[128,4,128]{2,1,0:T(4,128)}), f32[128,4,128]{2,1,0:T(4,128)S(1)}, u32[]{:S(2)}, u32[]{:S(2)}) async-start(f32[128,4,128]{2,1,0:T(4,128)} %broadcast_in_dim.17), calls=%async_computation.5 | async-start | bytes 524288 | tf_op jit(solution)/shard_map/all_to_all | solution.py:45
  153.4 52.3 %all-to-all-start.4 = ((bf16[64,56,512]{2,1,0:T(8,128)(2,1)}), bf16[64,56,512]{2,1,0:T(8,128)(2,1)}, u32[]{:S(2)}, u32[]{:S(2)}) async-start(bf16[64,56,512]{2,1,0:T(8,128)(2,1)} %bitcast.35), calls=%async_computation.4 | async-start | bytes 7340032 | tf_op jit(solution)/shard_map/all_to_all | solution.py:57

commit v3 on v0

v3 whole, which is shorter than its diff:
```python
import jax
import jax.numpy as jnp
from jax import lax
from jax.experimental import pallas as pl
from jax.experimental.pallas import tpu as pltpu
from jax.sharding import PartitionSpec as P

epsilon = 1e-06
axes = ("dp", "shard")
bf16, f32 = jnp.bfloat16, jnp.float32
MIB = 1024 * 1024


def device(x, core, y, z):
    return ((x % 4) * 2 + core) * 16 + (y % 4) * 4 + z % 4


four = range(4)
spots = [(x, c, y, z) for x in four for c in range(2) for y in four for z in four]
chips = [[device(x, c, y, z) for x in four for y in four for z in four] for c in range(2)]


def fetch(value, source):
    return lax.ppermute(value, axes, [(device(*source(*spot)), device(*spot)) for spot in spots])


def twin(value):
    return fetch(value, lambda x, c, y, z: (x, 1 - c, y, z))


def fetch_first(value, by):
    return fetch(value, lambda x, c, y, z: (x, c, y, z + by) if c else (x, c, y + by, z))


def fetch_second(value, by):
    return fetch(value, lambda x, c, y, z: (x, c, y + by, z) if c else (x, c, y, z + by))


def turn_kernel(place, kept, sent, after, kept_out, sent_out):
    for column in range(0, 896, 128):
        kept_out[column : column + 128, :] = kept[:, column : column + 128].T
        sent_out[column : column + 128, :] = sent[:, column : column + 128].T


def turn(place, inputs, after):
    return pl.pallas_call(
        turn_kernel,
        grid_spec=pltpu.PrefetchScalarGridSpec(
            num_scalar_prefetch=1,
            grid=(4,),
            in_specs=[
                pl.BlockSpec((768, 896), lambda i, place: (0, 2 * i + place[1])),
                pl.BlockSpec((768, 896), lambda i, place: (0, 2 * i + 1 - place[1])),
                pl.BlockSpec(memory_space=pl.ANY),
            ],
            out_specs=[pl.BlockSpec((896, 768), lambda i, place: (i, 0))] * 2,
        ),
        out_shape=[jax.ShapeDtypeStruct((3584, 768), bf16)] * 2,
        compiler_params=pltpu.CompilerParams(vmem_limit_bytes=24 * MIB),
        cost_estimate=pl.CostEstimate(flops=0, bytes_accessed=44 * MIB, transcendentals=0),
        name="turn",
    )(place, inputs, inputs, after)


def latent_kernel(place, inputs, cotangent, gain, *rest):
    pieces, (out, weight_out, held, leave) = rest[:8], rest[8:]
    step = pl.program_id(0)
    core, y, z = place[1], place[2], place[3]
    copy = pltpu.make_async_copy(held, weight_out, leave)

    @pl.when(step == 0)
    def _():
        for side in range(2):
            part = core if side == 0 else 1 - core
            for far in four:
                for near in four:
                    along_y = lax.rem(y + jnp.where(part == 0, near, far), 4)
                    along_z = lax.rem(z + jnp.where(part == 0, far, near), 4)
                    start = pl.multiple_of((along_y * 4 + along_z) * 448 + part * 224, 224)
                    held[pl.ds(start, 224), :] = pieces[side * 4 + far][near]
        copy.start()

    latent = jnp.dot(inputs[...], held[...], preferred_element_type=f32)
    scale = lax.rsqrt(jnp.mean(latent * latent, axis=1, keepdims=True) + epsilon)
    normed = latent * scale
    upstream = cotangent[...].astype(f32)
    scaled = upstream * gain[...]
    center = jnp.mean(scaled * normed, axis=1, keepdims=True)
    out[pl.ds(pl.multiple_of(step * 256, 256), 256), :] = (scale * (scaled - normed * center)).astype(bf16)
    gain_grad = jnp.sum(upstream * normed, axis=0, keepdims=True)

    @pl.when(step > 0)
    def _():
        out_gain = gain_grad + total_of(out)
        out[768:784, :] = split(out_gain)

    @pl.when(step == 0)
    def _():
        out[768:784, :] = split(gain_grad)

    @pl.when(step == 2)
    def _():
        copy.wait()


def split(value):
    high = value.astype(bf16).astype(f32)
    middle = (value - high).astype(bf16).astype(f32)
    low = value - high - middle
    return jnp.concatenate([high, middle, low, jnp.zeros((13, 512), f32)], axis=0).astype(bf16)


def total_of(rows):
    return jnp.sum(rows[768:784, :].astype(f32), axis=0, keepdims=True)


def latent_grads(place, inputs, cotangent, gain, pieces):
    return pl.pallas_call(
        latent_kernel,
        grid_spec=pltpu.PrefetchScalarGridSpec(
            num_scalar_prefetch=1,
            grid=(3,),
            in_specs=[
                pl.BlockSpec((256, 7168), lambda i, place: (i, 0)),
                pl.BlockSpec((256, 512), lambda i, place: (i, 0)),
                pl.BlockSpec((1, 512), lambda i, place: (0, 0)),
            ]
            + [pl.BlockSpec(memory_space=pltpu.VMEM)] * 8,
            out_specs=[
                pl.BlockSpec((784, 512), lambda i, place: (0, 0)),
                pl.BlockSpec(memory_space=pl.ANY),
            ],
            scratch_shapes=[pltpu.VMEM((7168, 512), bf16), pltpu.SemaphoreType.DMA],
        ),
        out_shape=[jax.ShapeDtypeStruct((784, 512), bf16), jax.ShapeDtypeStruct((7168, 512), bf16)],
        compiler_params=pltpu.CompilerParams(vmem_limit_bytes=40 * MIB),
        cost_estimate=pl.CostEstimate(flops=2 * 768 * 7168 * 512, bytes_accessed=28 * MIB, transcendentals=768),
        name="latent",
    )(place, inputs, cotangent, gain, *pieces)


def weight_kernel(mine, other, mine_grad, other_grad, out):
    product = jnp.dot(mine[...], mine_grad[:768, :], preferred_element_type=f32)
    product += jnp.dot(other[...], other_grad[:768, :], preferred_element_type=f32)
    pair = total_of(mine_grad) + total_of(other_grad)
    high = pair.astype(bf16).astype(f32)
    middle = (pair - high).astype(bf16).astype(f32)
    low = pair - high - middle
    lanes = [slice(128 * i, 128 * i + 128) for i in four]
    tail = [value[:, lane] for value in (high, middle, low) for lane in lanes] + [jnp.zeros((4, 128), f32)]
    for i in range(8):
        chunk = [product[56 * i : 56 * i + 56, lane] for lane in lanes]
        out[i, :, :] = jnp.concatenate(chunk + tail, axis=0).astype(bf16)


def weight_grads(mine, other, mine_grad, other_grad):
    return pl.pallas_call(
        weight_kernel,
        grid=(8,),
        in_specs=[pl.BlockSpec((448, 768), lambda i: (i, 0))] * 2 + [pl.BlockSpec((784, 512), lambda i: (0, 0))] * 2,
        out_specs=pl.BlockSpec((8, 240, 128), lambda i: (i, 0, 0)),
        out_shape=jax.ShapeDtypeStruct((64, 240, 128), bf16),
        compiler_params=pltpu.CompilerParams(vmem_limit_bytes=24 * MIB),
        cost_estimate=pl.CostEstimate(flops=2 * 768 * 7168 * 512, bytes_accessed=18 * MIB, transcendentals=0),
        name="weight_grads",
    )(mine, other, mine_grad, other_grad)


def sum_kernel(pieces, weight_grad, gain_grad):
    total = pieces[0].astype(f32)
    for i in range(1, 64):
        total = total + pieces[i].astype(f32)
    for i in four:
        weight_grad[:, 128 * i : 128 * i + 128] = total[56 * i : 56 * i + 56, :]
    gain_grad[...] = total[224:228, :] + total[228:232, :] + total[232:236, :]


def sums(pieces):
    return pl.pallas_call(
        sum_kernel,
        out_shape=[jax.ShapeDtypeStruct((56, 512), f32), jax.ShapeDtypeStruct((4, 128), f32)],
        compiler_params=pltpu.CompilerParams(vmem_limit_bytes=24 * MIB),
        name="sums",
    )(pieces)


def shards(inputs, cotangent, weight, norm_gain):
    dp, shard = lax.axis_index("dp"), lax.axis_index("shard")
    core = dp % 2
    place = jnp.stack([dp // 2, core, shard // 4, shard % 4]).astype(jnp.int32)
    half = lax.dynamic_slice_in_dim(weight, core * 224, 224, 0)
    line = jnp.stack([half] + [fetch_first(half, by) for by in (1, 2, 3)])
    mine = [line] + [fetch_second(line, by) for by in (1, 2, 3)]
    pieces = mine + [twin(piece) for piece in mine]
    kept, sent = turn(place, inputs, line)
    other = twin(sent)
    latent_grad, gathered = latent_grads(place, inputs, cotangent, norm_gain.reshape(1, 512), pieces)
    other_grad = twin(latent_grad)
    partial = weight_grads(kept, other, latent_grad, other_grad)
    partial = lax.all_to_all(partial, axes, 0, 0, axis_index_groups=chips, tiled=True)
    weight_grad, gain_grad = sums(partial)
    input_grad = lax.dot_general(
        latent_grad[:768], gathered, (((1,), (1,)), ((), ())), preferred_element_type=f32
    )
    return (input_grad.astype(bf16), weight_grad, gain_grad.reshape(512))


def solution(mesh):
    placed = (P(("dp", "shard"), None), P(("dp", "shard"), None), P("shard", None), P())
    return jax.shard_map(
        shards,
        mesh=mesh,
        in_specs=placed,
        out_specs=(P(("dp", "shard"), None), P(("dp", "shard"), None), P()),
        check_vma=False,
    )
```

time: 792 us -> 143 us (0.18)
  the two profiles are of different devices: /device:TPU:0 before, /device:TPU:50 now
where the time goes in v3:
time: 143 us; the launch traced here: 142 us
  waiting for transfers between devices  75 us (52%)
  Pallas kernels  26.2 us (18%)
  starting transfers between devices  21.5 us (15%)
  matrix products  11.7 us (8%)
  local copies, waits for them, and re-layouts  7.12 us (5%)
    all_to_all x1, waiting for transfers between devices, shards(): lax.all_to_all(partial, axes, 0, 0, axis_index_groups=chips, tiled=True)  43.1 us
    ppermute x12, waiting for transfers between devices, fetch(): lax.ppermute(value, axes, [(device(*source(*spot)), device(*spot)) for sp...  31.9 us
    all_to_all x1, starting transfers between devices, shards(): lax.all_to_all(partial, axes, 0, 0, axis_index_groups=chips, tiled=True)  12.2 us
    dot_general x1, matrix products, shards(): lax.dot_general(latent_grad[:768], gathered, (((1,), (1,)), ((), ())), pr...  11.7 us
    pallas_call x1, Pallas kernels, latent_grads(): pl.pallas_call(latent_kernel, grid_spec=pltpu.PrefetchScalarGridSpec(num_...  10.1 us
    ppermute x12, starting transfers between devices, fetch(): lax.ppermute(value, axes, [(device(*source(*spot)), device(*spot)) for sp...  9.26 us
    unnamed x10, local copies, waits for them, and re-layouts  7.09 us
    pallas_call x1, Pallas kernels, weight_grads(): pl.pallas_call(weight_kernel, grid=(8,), in_specs=[pl.BlockSpec((448, 768...  7.02 us
  transfers between devices with their start and end apart: 13, of which 10 were waited for; matrix products, arithmetic and copies ran while one was open for 8% of the time, Pallas kernels for 7%

profile of v3, /device:TPU:50, one launch (start us, length us, event | category | flops | bytes accessed | tf_op | source)
XLA Modules:
  0.0 142.4 jit_solution(17480237061380142922)
XLA Ops:
  0.6 0.0 copy-start
  0.7 1.0 copy-done
  1.7 0.5 collective-permute-start
  2.2 2.9 %collective-permute-start.1 = (bf16[224,512]{1,0:T(8,128)(2,1)S(1)}, bf16[224,512]{1,0:T(8,128)(2,1)S(1)}, u32[]{:S(2)}, u32[]{:S(2)}) collective-permute-start(bf16[224,512]{1,0:T(8,128)(2,1)S(1)} %constant_dynamic-slice_fusion), channel_id=1, source_target_pairs={{8,0},{9,1},{10,2},{11,3},{12,4},{13,5},{14,6},{15,7},{0,8},{1,9},... | collective-permute-start | bytes 688136 | tf_op jit(solution)/shard_map/ppermute | solution.py:24
  5.1 0.0 collective-permute-start.2
  5.1 0.1 pad_add_fusion.place
  5.2 2.6 %collective-permute-done = bf16[224,512]{1,0:T(8,128)(2,1)S(1)} collective-permute-done((bf16[224,512]{1,0:T(8,128)(2,1)S(1)}, bf16[224,512]{1,0:T(8,128)(2,1)S(1)}, u32[]{:S(2)}, u32[]{:S(2)}) %collective-permute-start) | collective-permute-done | bytes 229408 | tf_op jit(solution)/shard_map/ppermute | solution.py:24
  7.8 2.1 %collective-permute-done.1 = bf16[224,512]{1,0:T(8,128)(2,1)S(1)} collective-permute-done((bf16[224,512]{1,0:T(8,128)(2,1)S(1)}, bf16[224,512]{1,0:T(8,128)(2,1)S(1)}, u32[]{:S(2)}, u32[]{:S(2)}) %collective-permute-start.1) | collective-permute-done | bytes 229408 | tf_op jit(solution)/shard_map/ppermute | solution.py:24
  9.8 2.4 %collective-permute-done.2 = bf16[224,512]{1,0:T(8,128)(2,1)S(1)} collective-permute-done((bf16[224,512]{1,0:T(8,128)(2,1)S(1)}, bf16[224,512]{1,0:T(8,128)(2,1)S(1)}, u32[]{:S(2)}, u32[]{:S(2)}) %collective-permute-start.2) | collective-permute-done | bytes 229408 | tf_op jit(solution)/shard_map/ppermute | solution.py:24
  12.2 0.1 pad_maximum_fusion.rest_0_.after
  12.3 0.0 copy-start.1
  12.3 4.1 %copy-done.1 = bf16[768,7168]{1,0:T(8,128)(2,1)S(1)} copy-done((bf16[768,7168]{1,0:T(8,128)(2,1)S(1)}, bf16[768,7168]{1,0:T(8,128)(2,1)}, u32[]{:S(2)}) %copy-start.1) | copy-done | bytes 11010072
  16.4 5.8 %turn.1 = (bf16[3584,768]{1,0:T(8,128)(2,1)S(1)}, bf16[3584,768]{1,0:T(8,128)(2,1)}) custom-call(s32[4]{0:T(128)S(1)} %pad_add_fusion.place, bf16[768,7168]{1,0:T(8,128)(2,1)S(1)} %copy-done.1, bf16[768,7168]{1,0:T(8,128)(2,1)S(1)} %copy-done.1, bf16[4,224,512]{2,1,0:T(8,128)(2,1)S(1)} %pad_maximum_fusion.rest_0_.after), custom_call_target="tpu_custom_call" | custom-call | bytes 46137344 | tf_op jit(solution)/shard_map/turn/pallas_call | solution.py:46
  22.3 1.8 %collective-permute-start.3 = (bf16[4,224,512]{2,1,0:T(8,128)(2,1)S(1)}, bf16[4,224,512]{2,1,0:T(8,128)(2,1)S(1)}, u32[]{:S(2)}, u32[]{:S(2)}) collective-permute-start(bf16[4,224,512]{2,1,0:T(8,128)(2,1)S(1)} %pad_maximum_fusion.rest_0_.after), channel_id=1, source_target_pairs={{1,0},{2,1},{3,2},{0,3},{5,4},{6,5},{7,6},{4,7},{9,8},{10,9},{11,1... | collective-permute-start | bytes 2752520 | tf_op jit(solution)/shard_map/ppermute | solution.py:24
  24.1 1.6 %collective-permute-start.4 = (bf16[4,224,512]{2,1,0:T(8,128)(2,1)S(1)}, bf16[4,224,512]{2,1,0:T(8,128)(2,1)S(1)}, u32[]{:S(2)}, u32[]{:S(2)}) collective-permute-start(bf16[4,224,512]{2,1,0:T(8,128)(2,1)S(1)} %pad_maximum_fusion.rest_0_.after), channel_id=1, source_target_pairs={{2,0},{3,1},{0,2},{1,3},{6,4},{7,5},{4,6},{5,7},{10,8},{11,9},{8,1... | collective-permute-start | bytes 2752520 | tf_op jit(solution)/shard_map/ppermute | solution.py:24
  25.7 2.2 %collective-permute-start.5 = (bf16[4,224,512]{2,1,0:T(8,128)(2,1)S(1)}, bf16[4,224,512]{2,1,0:T(8,128)(2,1)S(1)}, u32[]{:S(2)}, u32[]{:S(2)}) collective-permute-start(bf16[4,224,512]{2,1,0:T(8,128)(2,1)S(1)} %pad_maximum_fusion.rest_0_.after), channel_id=1, source_target_pairs={{3,0},{0,1},{1,2},{2,3},{7,4},{4,5},{5,6},{6,7},{11,8},{8,9},{9,10... | collective-permute-start | bytes 2752520 | tf_op jit(solution)/shard_map/ppermute | solution.py:24
  27.9 0.0 collective-permute-start.6
  27.9 7.8 %collective-permute-done.3.rest_1_ = bf16[4,224,512]{2,1,0:T(8,128)(2,1)S(1)} collective-permute-done((bf16[4,224,512]{2,1,0:T(8,128)(2,1)S(1)}, bf16[4,224,512]{2,1,0:T(8,128)(2,1)S(1)}, u32[]{:S(2)}, u32[]{:S(2)}) %collective-permute-start.3) | collective-permute-done | bytes 917536 | tf_op jit(solution)/shard_map/ppermute | solution.py:24
  35.7 0.0 collective-permute-start.7
  35.7 11.2 %collective-permute-done.4.rest_2_ = bf16[4,224,512]{2,1,0:T(8,128)(2,1)S(1)} collective-permute-done((bf16[4,224,512]{2,1,0:T(8,128)(2,1)S(1)}, bf16[4,224,512]{2,1,0:T(8,128)(2,1)S(1)}, u32[]{:S(2)}, u32[]{:S(2)}) %collective-permute-start.4) | collective-permute-done | bytes 917536 | tf_op jit(solution)/shard_map/ppermute | solution.py:24
  46.9 0.8 collective-permute-done.5.rest_3_
  47.7 1.6 %collective-permute-done.8.rest_6_ = bf16[4,224,512]{2,1,0:T(8,128)(2,1)S(1)} collective-permute-done((bf16[4,224,512]{2,1,0:T(8,128)(2,1)S(1)}, bf16[4,224,512]{2,1,0:T(8,128)(2,1)S(1)}, u32[]{:S(2)}, u32[]{:S(2)}) %collective-permute-start.8) | collective-permute-done | bytes 917536 | tf_op jit(solution)/shard_map/ppermute | solution.py:24
  49.3 1.3 collective-permute-done.9.rest_7_
  50.6 10.1 %latent.1 = (bf16[784,512]{1,0:T(8,128)(2,1)S(1)}, bf16[7168,512]{1,0:T(8,128)(2,1)}) custom-call(s32[4]{0:T(128)S(1)} %pad_add_fusion.place, bf16[768,7168]{1,0:T(8,128)(2,1)} %sent.1, bf16[768,512]{1,0:T(8,128)(2,1)S(1)} %copy-done.3, f32[1,512]{1,0:T(1,128)S(1)} %bitcast.12, bf16[4,224,512]{2,1,0:T(8,128)(2,1)S(1)} %pad_maximum_fusion.rest_0_.after, ...), custom_call_target="tpu_custom_call" | custom-call | flops 5637144576 | bytes 29360128 | tf_op jit(solution)/shard_map/latent/pallas_call | solution.py:118
  60.7 0.2 collective-permute-start.11
  60.9 2.2 %collective-permute-done.11.other_grad = bf16[784,512]{1,0:T(8,128)(2,1)S(1)} collective-permute-done((bf16[784,512]{1,0:T(8,128)(2,1)S(1)}, bf16[784,512]{1,0:T(8,128)(2,1)S(1)}, u32[]{:S(2)}, u32[]{:S(2)}) %collective-permute-start.11) | collective-permute-done | bytes 802848 | tf_op jit(solution)/shard_map/ppermute | solution.py:24
  63.1 7.0 %weight_grads.1 = bf16[64,240,128]{2,1,0:T(8,128)(2,1)S(1)} custom-call(bf16[3584,768]{1,0:T(8,128)(2,1)S(1)} %get-tuple-element.11.mine, bf16[3584,768]{1,0:T(8,128)(2,1)S(1)} %collective-permute-done.10.other, bf16[784,512]{1,0:T(8,128)(2,1)S(1)} %get-tuple-element.9.mine_grad, bf16[784,512]{1,0:T(8,128)(2,1)S(1)} %collective-permute-done.11.other_grad), custom_call_target="tpu_custom_call" | custom-call | flops 5637144576 | bytes 18874368 | tf_op jit(solution)/shard_map/weight_grads/pallas_call | solution.py:157
  70.2 2.0 %copy-done.2 = bf16[64,240,128]{2,1,0:T(8,128)(2,1)} copy-done((bf16[64,240,128]{2,1,0:T(8,128)(2,1)}, bf16[64,240,128]{2,1,0:T(8,128)(2,1)S(1)}, u32[]{:S(2)}) %copy-start.2) | copy-done | bytes 3932184
  72.1 12.2 %all-to-all-start = ((bf16[64,240,128]{2,1,0:T(8,128)(2,1)}), bf16[64,240,128]{2,1,0:T(8,128)(2,1)}, u32[]{:S(2)}, u32[]{:S(2)}) async-start(bf16[64,240,128]{2,1,0:T(8,128)(2,1)} %copy-done.2), calls=%async_computation | async-start | bytes 7864320 | tf_op jit(solution)/shard_map/all_to_all | solution.py:200
  84.3 11.7 %convolution_convert_fusion = bf16[768,7168]{1,0:T(8,128)(2,1)} fusion(bf16[7168,512]{1,0:T(8,128)(2,1)} %get-tuple-element.10, bf16[784,512]{1,0:T(8,128)(2,1)S(1)} %get-tuple-element.9.mine_grad), kind=kOutput, calls=%fused_computation | convolution fusion | flops 5642649600 | bytes 19136512 | tf_op jit(solution)/shard_map/dot_general | solution.py:202
  96.0 43.1 %all-to-all-done.pieces = bf16[64,240,128]{2,1,0:T(8,128)(2,1)} async-done(((bf16[64,240,128]{2,1,0:T(8,128)(2,1)}), bf16[64,240,128]{2,1,0:T(8,128)(2,1)}, u32[]{:S(2)}, u32[]{:S(2)}) %all-to-all-start) | async-done | bytes 3932192 | tf_op jit(solution)/shard_map/all_to_all | solution.py:200
  139.1 3.3 %sums.1 = (f32[56,512]{1,0:T(8,128)}, f32[4,128]{1,0:T(4,128)}) custom-call(bf16[64,240,128]{2,1,0:T(8,128)(2,1)} %all-to-all-done.pieces), custom_call_target="tpu_custom_call" | custom-call | tf_op jit(solution)/shard_map/sums/pallas_call | solution.py:179
  (13 shorter events, 0.1 us)
Async XLA Ops:
  0.6 1.0 copy-start
  1.7 6.1 %collective-permute-start = (bf16[224,512]{1,0:T(8,128)(2,1)S(1)}, bf16[224,512]{1,0:T(8,128)(2,1)S(1)}, u32[]{:S(2)}, u32[]{:S(2)}) collective-permute-start(bf16[224,512]{1,0:T(8,128)(2,1)S(1)} %constant_dynamic-slice_fusion), channel_id=1, source_target_pairs={{4,0},{5,1},{6,2},{7,3},{8,4},{9,5},{10,6},{11,7},{12,8},{13,9},{1... | collective-permute-start | bytes 688136 | tf_op jit(solution)/shard_map/ppermute | solution.py:24
  2.2 7.6 %collective-permute-start.1 = (bf16[224,512]{1,0:T(8,128)(2,1)S(1)}, bf16[224,512]{1,0:T(8,128)(2,1)S(1)}, u32[]{:S(2)}, u32[]{:S(2)}) collective-permute-start(bf16[224,512]{1,0:T(8,128)(2,1)S(1)} %constant_dynamic-slice_fusion), channel_id=1, source_target_pairs={{8,0},{9,1},{10,2},{11,3},{12,4},{13,5},{14,6},{15,7},{0,8},{1,9},... | collective-permute-start | bytes 688136 | tf_op jit(solution)/shard_map/ppermute | solution.py:24
  5.1 7.1 %collective-permute-start.2 = (bf16[224,512]{1,0:T(8,128)(2,1)S(1)}, bf16[224,512]{1,0:T(8,128)(2,1)S(1)}, u32[]{:S(2)}, u32[]{:S(2)}) collective-permute-start(bf16[224,512]{1,0:T(8,128)(2,1)S(1)} %constant_dynamic-slice_fusion), channel_id=1, source_target_pairs={{12,0},{13,1},{14,2},{15,3},{0,4},{1,5},{2,6},{3,7},{4,8},{5,9},{6... | collective-permute-start | bytes 688136 | tf_op jit(solution)/shard_map/ppermute | solution.py:24
  12.3 4.1 %copy-start.1 = (bf16[768,7168]{1,0:T(8,128)(2,1)S(1)}, bf16[768,7168]{1,0:T(8,128)(2,1)}, u32[]{:S(2)}) copy-start(bf16[768,7168]{1,0:T(8,128)(2,1)} %sent.1) | copy-start | bytes 33030148
  16.4 34.2 %copy-start.3 = (bf16[768,512]{1,0:T(8,128)(2,1)S(1)}, bf16[768,512]{1,0:T(8,128)(2,1)}, u32[]{:S(2)}) copy-start(bf16[768,512]{1,0:T(8,128)(2,1)} %cotangent.1) | copy-start | bytes 2359300
  16.4 34.2 %copy-start.4 = (f32[512]{0:T(512)S(1)}, f32[512]{0:T(512)}, u32[]{:S(2)}) copy-start(f32[512]{0:T(512)} %param.7) | copy-start | bytes 6148
  22.3 40.9 %collective-permute-start.10 = (bf16[3584,768]{1,0:T(8,128)(2,1)}, bf16[3584,768]{1,0:T(8,128)(2,1)S(1)}, u32[]{:S(2)}, u32[]{:S(2)}) collective-permute-start(bf16[3584,768]{1,0:T(8,128)(2,1)} %get-tuple-element.12), channel_id=1, source_target_pairs={{16,0},{17,1},{18,2},{19,3},{20,4},{21,5},{22,6},{23,7},{24,8},{25... | collective-permute-start | bytes 16515080 | tf_op jit(solution)/shard_map/ppermute | solution.py:24
  22.3 13.4 %collective-permute-start.3 = (bf16[4,224,512]{2,1,0:T(8,128)(2,1)S(1)}, bf16[4,224,512]{2,1,0:T(8,128)(2,1)S(1)}, u32[]{:S(2)}, u32[]{:S(2)}) collective-permute-start(bf16[4,224,512]{2,1,0:T(8,128)(2,1)S(1)} %pad_maximum_fusion.rest_0_.after), channel_id=1, source_target_pairs={{1,0},{2,1},{3,2},{0,3},{5,4},{6,5},{7,6},{4,7},{9,8},{10,9},{11,1... | collective-permute-start | bytes 2752520 | tf_op jit(solution)/shard_map/ppermute | solution.py:24
  24.1 22.8 %collective-permute-start.4 = (bf16[4,224,512]{2,1,0:T(8,128)(2,1)S(1)}, bf16[4,224,512]{2,1,0:T(8,128)(2,1)S(1)}, u32[]{:S(2)}, u32[]{:S(2)}) collective-permute-start(bf16[4,224,512]{2,1,0:T(8,128)(2,1)S(1)} %pad_maximum_fusion.rest_0_.after), channel_id=1, source_target_pairs={{2,0},{3,1},{0,2},{1,3},{6,4},{7,5},{4,6},{5,7},{10,8},{11,9},{8,1... | collective-permute-start | bytes 2752520 | tf_op jit(solution)/shard_map/ppermute | solution.py:24
  25.7 22.0 %collective-permute-start.5 = (bf16[4,224,512]{2,1,0:T(8,128)(2,1)S(1)}, bf16[4,224,512]{2,1,0:T(8,128)(2,1)S(1)}, u32[]{:S(2)}, u32[]{:S(2)}) collective-permute-start(bf16[4,224,512]{2,1,0:T(8,128)(2,1)S(1)} %pad_maximum_fusion.rest_0_.after), channel_id=1, source_target_pairs={{3,0},{0,1},{1,2},{2,3},{7,4},{4,5},{5,6},{6,7},{11,8},{8,9},{9,10... | collective-permute-start | bytes 2752520 | tf_op jit(solution)/shard_map/ppermute | solution.py:24
  27.9 19.8 %collective-permute-start.6 = (bf16[4,224,512]{2,1,0:T(8,128)(2,1)S(1)}, bf16[4,224,512]{2,1,0:T(8,128)(2,1)S(1)}, u32[]{:S(2)}, u32[]{:S(2)}) collective-permute-start(bf16[4,224,512]{2,1,0:T(8,128)(2,1)S(1)} %pad_maximum_fusion.rest_0_.after), channel_id=1, source_target_pairs={{16,0},{17,1},{18,2},{19,3},{20,4},{21,5},{22,6},{23,7},{24,8},{25... | collective-permute-start | bytes 2752520 | tf_op jit(solution)/shard_map/ppermute | solution.py:24
  35.7 12.0 %collective-permute-start.7 = (bf16[4,224,512]{2,1,0:T(8,128)(2,1)S(1)}, bf16[4,224,512]{2,1,0:T(8,128)(2,1)S(1)}, u32[]{:S(2)}, u32[]{:S(2)}) collective-permute-start(bf16[4,224,512]{2,1,0:T(8,128)(2,1)S(1)} %collective-permute-done.3.rest_1_), channel_id=1, source_target_pairs={{16,0},{17,1},{18,2},{19,3},{20,4},{21,5},{22,6},{23,7},{24,8},{25... | collective-permute-start | bytes 2752520 | tf_op jit(solution)/shard_map/ppermute | solution.py:24
  46.9 2.5 %collective-permute-start.8 = (bf16[4,224,512]{2,1,0:T(8,128)(2,1)S(1)}, bf16[4,224,512]{2,1,0:T(8,128)(2,1)S(1)}, u32[]{:S(2)}, u32[]{:S(2)}) collective-permute-start(bf16[4,224,512]{2,1,0:T(8,128)(2,1)S(1)} %collective-permute-done.4.rest_2_), channel_id=1, source_target_pairs={{16,0},{17,1},{18,2},{19,3},{20,4},{21,5},{22,6},{23,7},{24,8},{25... | collective-permute-start | bytes 2752520 | tf_op jit(solution)/shard_map/ppermute | solution.py:24
  47.7 3.0 %collective-permute-start.9 = (bf16[4,224,512]{2,1,0:T(8,128)(2,1)S(1)}, bf16[4,224,512]{2,1,0:T(8,128)(2,1)S(1)}, u32[]{:S(2)}, u32[]{:S(2)}) collective-permute-start(bf16[4,224,512]{2,1,0:T(8,128)(2,1)S(1)} %collective-permute-done.5.rest_3_), channel_id=1, source_target_pairs={{16,0},{17,1},{18,2},{19,3},{20,4},{21,5},{22,6},{23,7},{24,8},{25... | collective-permute-start | bytes 2752520 | tf_op jit(solution)/shard_map/ppermute | solution.py:24
  60.7 2.4 %collective-permute-start.11 = (bf16[784,512]{1,0:T(8,128)(2,1)S(1)}, bf16[784,512]{1,0:T(8,128)(2,1)S(1)}, u32[]{:S(2)}, u32[]{:S(2)}) collective-permute-start(bf16[784,512]{1,0:T(8,128)(2,1)S(1)} %get-tuple-element.9.mine_grad), channel_id=1, source_target_pairs={{16,0},{17,1},{18,2},{19,3},{20,4},{21,5},{22,6},{23,7},{24,8},{25... | collective-permute-start | bytes 2408456 | tf_op jit(solution)/shard_map/ppermute | solution.py:24
  70.2 2.0 %copy-start.2 = (bf16[64,240,128]{2,1,0:T(8,128)(2,1)}, bf16[64,240,128]{2,1,0:T(8,128)(2,1)S(1)}, u32[]{:S(2)}) copy-start(bf16[64,240,128]{2,1,0:T(8,128)(2,1)S(1)} %weight_grads.1) | copy-start | bytes 11796484
  72.1 67.0 %all-to-all-start = ((bf16[64,240,128]{2,1,0:T(8,128)(2,1)}), bf16[64,240,128]{2,1,0:T(8,128)(2,1)}, u32[]{:S(2)}, u32[]{:S(2)}) async-start(bf16[64,240,128]{2,1,0:T(8,128)(2,1)} %copy-done.2), calls=%async_computation | async-start | bytes 7864320 | tf_op jit(solution)/shard_map/all_to_all | solution.py:200

commit v4 on v3

v4 whole, which is shorter than its diff:
```python
import jax
import jax.numpy as jnp
from jax import lax
from jax.experimental import pallas as pl
from jax.experimental.pallas import tpu as pltpu
from jax.sharding import PartitionSpec as P

epsilon = 1e-06
axes = ("dp", "shard")
bf16, f32 = jnp.bfloat16, jnp.float32
MIB = 1024 * 1024


def device(x, core, y, z):
    return ((x % 4) * 2 + core) * 16 + (y % 4) * 4 + z % 4


four = range(4)
spots = [(x, c, y, z) for x in four for c in range(2) for y in four for z in four]


def fetch(value, source):
    return lax.ppermute(value, axes, [(device(*source(*spot)), device(*spot)) for spot in spots])


def twin(value):
    return fetch(value, lambda x, c, y, z: (x, 1 - c, y, z))


def fetch_first(value, by):
    return fetch(value, lambda x, c, y, z: (x, c, y, z + by) if c else (x, c, y + by, z))


def fetch_second(value, by):
    return fetch(value, lambda x, c, y, z: (x, c, y + by, z) if c else (x, c, y, z + by))


order = jax.ShapeDtypeStruct((8, 128), f32)


def turn_kernel(place, rows, out, token):
    token[...] = jnp.zeros((8, 128), f32)
    for column in range(0, 896, 128):
        out[column : column + 128, :] = rows[:, column : column + 128].T


def turn(place, inputs):
    return pl.pallas_call(
        turn_kernel,
        grid_spec=pltpu.PrefetchScalarGridSpec(
            num_scalar_prefetch=1,
            grid=(4,),
            in_specs=[pl.BlockSpec((768, 896), lambda i, place: (0, 2 * i + place[1]))],
            out_specs=[
                pl.BlockSpec((896, 768), lambda i, place: (i, 0)),
                pl.BlockSpec((8, 128), lambda i, place: (0, 0)),
            ],
        ),
        out_shape=[jax.ShapeDtypeStruct((3584, 768), bf16), order],
        compiler_params=pltpu.CompilerParams(vmem_limit_bytes=52 * MIB),
        cost_estimate=pl.CostEstimate(flops=0, bytes_accessed=22 * MIB, transcendentals=0),
        name="turn",
    )(place, inputs)


def tie_kernel(value, token, out):
    out[...] = value[...]


def tie(value, token):
    vmem = pl.BlockSpec(memory_space=pltpu.VMEM)
    return pl.pallas_call(
        tie_kernel,
        in_specs=[vmem] * 2,
        out_specs=vmem,
        out_shape=jax.ShapeDtypeStruct(value.shape, value.dtype),
        compiler_params=pltpu.CompilerParams(vmem_limit_bytes=8 * MIB),
        cost_estimate=pl.CostEstimate(flops=0, bytes_accessed=2 * MIB, transcendentals=0),
        name="tie",
    )(value, token)


def join_kernel(one, two, three, four_, token, out):
    for i, ref in enumerate((one, two, three, four_)):
        out[i] = ref[...]


def join(values, token):
    vmem = pl.BlockSpec(memory_space=pltpu.VMEM)
    return pl.pallas_call(
        join_kernel,
        in_specs=[vmem] * 5,
        out_specs=vmem,
        out_shape=jax.ShapeDtypeStruct((4, 224, 512), bf16),
        compiler_params=pltpu.CompilerParams(vmem_limit_bytes=8 * MIB),
        cost_estimate=pl.CostEstimate(flops=0, bytes_accessed=2 * MIB, transcendentals=0),
        name="join",
    )(*values, token)


def latent_kernel(place, inputs, cotangent, gain, *rest):
    pieces, (out, weight_out, held, leave) = rest[:8], rest[8:]
    step = pl.program_id(0)
    core, y, z = place[1], place[2], place[3]
    copy = pltpu.make_async_copy(held, weight_out, leave)

    @pl.when(step == 0)
    def _():
        for side in range(2):
            part = core if side == 0 else 1 - core
            for far in four:
                for near in four:
                    along_y = lax.rem(y + jnp.where(part == 0, near, far), 4)
                    along_z = lax.rem(z + jnp.where(part == 0, far, near), 4)
                    start = pl.multiple_of((along_y * 4 + along_z) * 448 + part * 224, 224)
                    held[pl.ds(start, 224), :] = pieces[side * 4 + far][near]
        copy.start()

    latent = jnp.dot(inputs[...], held[...], preferred_element_type=f32)
    scale = lax.rsqrt(jnp.mean(latent * latent, axis=1, keepdims=True) + epsilon)
    normed = latent * scale
    upstream = cotangent[...].astype(f32)
    scaled = upstream * gain[...]
    center = jnp.mean(scaled * normed, axis=1, keepdims=True)
    out[pl.ds(pl.multiple_of(step * 256, 256), 256), :] = (scale * (scaled - normed * center)).astype(bf16)
    gain_grad = jnp.sum(upstream * normed, axis=0, keepdims=True)

    @pl.when(step > 0)
    def _():
        out_gain = gain_grad + total_of(out)
        out[768:784, :] = split(out_gain)

    @pl.when(step == 0)
    def _():
        out[768:784, :] = split(gain_grad)

    @pl.when(step == 2)
    def _():
        copy.wait()


def parts(value):
    high = value.astype(bf16).astype(f32)
    middle = (value - high).astype(bf16).astype(f32)
    return [high, middle, value - high - middle]


def split(value):
    return jnp.concatenate(parts(value) + [jnp.zeros((13, 512), f32)], axis=0).astype(bf16)


def total_of(rows):
    return jnp.sum(rows[768:784, :].astype(f32), axis=0, keepdims=True)


def latent_grads(place, inputs, cotangent, gain, pieces):
    return pl.pallas_call(
        latent_kernel,
        grid_spec=pltpu.PrefetchScalarGridSpec(
            num_scalar_prefetch=1,
            grid=(3,),
            in_specs=[
                pl.BlockSpec((256, 7168), lambda i, place: (i, 0)),
                pl.BlockSpec((256, 512), lambda i, place: (i, 0)),
                pl.BlockSpec((1, 512), lambda i, place: (0, 0)),
            ]
            + [pl.BlockSpec(memory_space=pltpu.VMEM)] * 8,
            out_specs=[
                pl.BlockSpec((784, 512), lambda i, place: (0, 0)),
                pl.BlockSpec(memory_space=pl.ANY),
            ],
            scratch_shapes=[pltpu.VMEM((7168, 512), bf16), pltpu.SemaphoreType.DMA],
        ),
        out_shape=[jax.ShapeDtypeStruct((784, 512), bf16), jax.ShapeDtypeStruct((7168, 512), bf16)],
        compiler_params=pltpu.CompilerParams(vmem_limit_bytes=24 * MIB),
        cost_estimate=pl.CostEstimate(flops=2 * 768 * 7168 * 512, bytes_accessed=28 * MIB, transcendentals=768),
        name="latent",
    )(place, inputs, cotangent, gain, *pieces)


def input_kernel(grad, weight, before, out, token):
    token[...] = jnp.zeros((8, 128), f32)
    out[...] = lax.dot_general(
        grad[:768, :], weight[...], (((1,), (1,)), ((), ())), preferred_element_type=f32
    ).astype(bf16)


def input_grads(grad, weight, token):
    return pl.pallas_call(
        input_kernel,
        grid=(7,),
        in_specs=[
            pl.BlockSpec((784, 512), lambda i: (0, 0)),
            pl.BlockSpec((1024, 512), lambda i: (i, 0)),
            pl.BlockSpec((8, 128), lambda i: (0, 0)),
        ],
        out_specs=[pl.BlockSpec((768, 1024), lambda i: (0, i)), pl.BlockSpec((8, 128), lambda i: (0, 0))],
        out_shape=[jax.ShapeDtypeStruct((768, 7168), bf16), order],
        compiler_params=pltpu.CompilerParams(vmem_limit_bytes=52 * MIB),
        cost_estimate=pl.CostEstimate(flops=0, bytes_accessed=MIB, transcendentals=0),
        name="input_grads",
    )(grad, weight, token)


lanes = [slice(128 * i, 128 * i + 128) for i in four]


def flat(rows):
    return jnp.concatenate([rows[:, lane] for lane in lanes], axis=0)


def weight_kernel(place, *refs):
    mine, other, mine_grad, other_grad = refs[:2], refs[2:4], *refs[4:6]
    out, token, held = refs[-3:]
    token[...] = jnp.zeros((8, 128), f32)
    rows = jnp.concatenate([mine[0][...], mine[1][...]], axis=0)
    product = jnp.dot(rows, mine_grad[:768, :], preferred_element_type=f32)
    rows = jnp.concatenate([other[0][...], other[1][...]], axis=0)
    product += jnp.dot(rows, other_grad[:768, :], preferred_element_type=f32)
    held[...] = product.reshape(8, 56, 512)
    for i in range(8):
        out[0, 224 * i : 224 * i + 224, :] = flat(held[i]).astype(bf16)
    gain = total_of(mine_grad) + total_of(other_grad)
    out[0, 1792:1808, :] = gain_rows(flat(gain))


def gain_rows(gain):
    return jnp.concatenate(parts(gain) + [jnp.zeros((4, 128), f32)], axis=0).astype(bf16)


def gain_of(rows):
    rows = rows.astype(f32)
    return (rows[0:4] + rows[4:8]) + rows[8:12]


def weight_grads(place, mine, other, mine_grad, other_grad, by, tokens):
    def rows(i):
        def index(pair, place):
            x_ahead = lax.rem(place[0] + by, 4) * 4 + pair * 2 + i
            y_ahead = (pair * 2 + i) * 4 + lax.rem(place[2] + by, 4)
            return jnp.where(place[1] == 0, x_ahead, y_ahead), 0

        return pl.BlockSpec((224, 768), index)

    whole = pl.BlockSpec((784, 512), lambda pair, place: (0, 0))
    small = pl.BlockSpec((8, 128), lambda pair, place: (0, 0))
    return pl.pallas_call(
        weight_kernel,
        grid_spec=pltpu.PrefetchScalarGridSpec(
            num_scalar_prefetch=1,
            grid=(2,),
            in_specs=[rows(0), rows(1)] * 2 + [whole] * 2 + [small] * len(tokens),
            out_specs=[pl.BlockSpec((1, 1808, 128), lambda pair, place: (pair, 0, 0)), small],
            scratch_shapes=[pltpu.VMEM((8, 56, 512), f32)],
        ),
        out_shape=[jax.ShapeDtypeStruct((2, 1808, 128), bf16), order],
        compiler_params=pltpu.CompilerParams(vmem_limit_bytes=14 * MIB),
        cost_estimate=pl.CostEstimate(flops=0, bytes_accessed=MIB, transcendentals=0),
        name="weight_grads",
    )(place, mine, mine, other, other, mine_grad, other_grad, *tokens)


def add(values):
    own, one, two, three = [value.astype(f32) for value in values]
    return (own + two) + (one + three)


def first_kernel(place, *refs):
    partial, out = refs[:4], refs[-4:]
    other = jnp.where(place[1] == 0, place[2], place[0])
    for to in four:
        at = lax.rem(other + to, 4)
        for z in four:
            rows = pl.ds(pl.multiple_of(lax.rem(at, 2) * 896 + z * 224, 32), 224)
            out[to][224 * z : 224 * z + 224, :] = add([ref[lax.div(at, 2), rows, :] for ref in partial]).astype(bf16)
        for i in four:
            out[to][896 + 16 * i : 912 + 16 * i, :] = partial[i][0, 1792:1808, :]


def second_kernel(place, *refs):
    sums, out, held = refs[:4], refs[4:8], refs[8]
    x, core, y, z = [place[i] for i in four]
    for i in four:
        held[i] = sums[i][896:960, :].astype(f32)
    gain = jnp.zeros((4, 128), f32)
    for from_x in four:
        for from_y in four:
            back_x, back_y = lax.rem(x + 4 - from_x, 4), lax.rem(y + 4 - from_y, 4)
            major, other = jnp.where(core == 0, back_x, back_y), jnp.where(core == 0, back_y, back_x)
            gain = gain + gain_of(held[other, pl.ds(pl.multiple_of(major * 16, 16), 16), :])
    for to in four:
        rows = pl.ds(pl.multiple_of(lax.rem(z + to, 4) * 224, 32), 224)
        out[to][0:224, :] = add([ref[rows, :] for ref in sums]).astype(bf16)
        out[to][224:240, :] = gain_rows(gain)


def third_kernel(place, *refs):
    sums, weight_grad, gain_grad = refs[:4], *refs[4:]
    total = add([ref[0:224, :] for ref in sums])
    for i in four:
        weight_grad[:, lanes[i]] = total[56 * i : 56 * i + 56, :]
    gain_grad[...] = add([gain_of(ref[224:240, :]) for ref in sums])


def touch_kernel(value, token, out):
    out[...] = token[...] + value[0, 0:8, :].astype(f32)


def touch(value, token):
    return pl.pallas_call(
        touch_kernel,
        grid=(1,),
        in_specs=[pl.BlockSpec((1, 16, 128), lambda i: (0, 0, 0)), pl.BlockSpec((8, 128), lambda i: (0, 0))],
        out_specs=pl.BlockSpec((8, 128), lambda i: (0, 0)),
        out_shape=order,
        compiler_params=pltpu.CompilerParams(vmem_limit_bytes=4 * MIB),
        cost_estimate=pl.CostEstimate(flops=0, bytes_accessed=4096, transcendentals=0),
        name="touch",
    )(value, token)


def combine(kernel, shapes, place, values, scratch=(), tokens=()):
    vmem = pl.BlockSpec(memory_space=pltpu.VMEM)
    return pl.pallas_call(
        kernel,
        in_specs=[pl.BlockSpec(memory_space=pltpu.SMEM)]
        + [vmem] * (len(values) + len(tokens)),
        out_specs=[vmem] * len(shapes),
        out_shape=[jax.ShapeDtypeStruct(*shape) for shape in shapes],
        scratch_shapes=list(scratch),
        compiler_params=pltpu.CompilerParams(vmem_limit_bytes=24 * MIB),
        cost_estimate=pl.CostEstimate(flops=0, bytes_accessed=MIB, transcendentals=0),
        name=kernel.__name__,
    )(place, *values, *tokens)


def along_major(value, by):
    return fetch(value, lambda x, c, y, z: (x, c, y - by, z) if c else (x - by, c, y, z))


def along_other(value, by):
    return fetch(value, lambda x, c, y, z: (x - by, c, y, z) if c else (x, c, y - by, z))


def along_z(value, by):
    return fetch(value, lambda x, c, y, z: (x, c, y, z - by))


def exchange(values, along):
    return [values[0]] + [along(values[by], by) for by in (1, 2, 3)]


def reduce_scatter(place, partial, token):
    sums = exchange(partial, along_major)
    token = touch(sums[1], touch(sums[2], token))
    sums = combine(first_kernel, [((960, 128), bf16)] * 4, place, sums, tokens=[token])
    sums = exchange(sums, along_other)
    sums = combine(second_kernel, [((240, 128), bf16)] * 4, place, sums, [pltpu.VMEM((4, 64, 128), f32)])
    sums = exchange(sums, along_z)
    return combine(third_kernel, [((56, 512), f32), ((4, 128), f32)], place, sums)


def shards(inputs, cotangent, weight, norm_gain):
    dp, shard = lax.axis_index("dp"), lax.axis_index("shard")
    core = dp % 2
    place = jnp.stack([dp // 2, core, shard // 4, shard % 4]).astype(jnp.int32)
    half = lax.dynamic_slice_in_dim(weight, core * 224, 224, 0)
    other_inputs = twin(inputs)
    kept, token = turn(place, inputs)
    line = join([half] + [fetch_first(half, by) for by in (1, 2, 3)], token)
    mine = [line] + [fetch_second(line, by) for by in (1, 2, 3)]
    other, token = turn(place, other_inputs)
    mine[3] = tie(mine[3], token)
    pieces = mine + [twin(piece) for piece in mine]
    latent_grad, gathered = latent_grads(place, inputs, cotangent, norm_gain.reshape(1, 512), pieces)
    other_grad = twin(latent_grad)
    partial, tokens = [None] * 4, []
    for by in (2, 1, 3, 0):
        partial[by], token = weight_grads(place, kept, other, latent_grad, other_grad, by, tokens)
        tokens = [token]
    input_grad, token = input_grads(latent_grad, gathered, token)
    weight_grad, gain_grad = reduce_scatter(place, partial, token)
    return (input_grad, weight_grad, gain_grad.reshape(512))


def solution(mesh):
    placed = (P(("dp", "shard"), None), P(("dp", "shard"), None), P("shard", None), P())
    return jax.shard_map(
        shards,
        mesh=mesh,
        in_specs=placed,
        out_specs=(P(("dp", "shard"), None), P(("dp", "shard"), None), P()),
        check_vma=False,
    )
```

time: 143 us -> 127 us (0.89)
  the two profiles are of different devices: /device:TPU:50 before, /device:TPU:0 now
where the time goes in v4:
time: 127 us; the launch traced here: 126 us
  Pallas kernels  50.9 us (40%)
  waiting for transfers between devices  36.8 us (29%)
  starting transfers between devices  25.9 us (20%)
  local copies, waits for them, and re-layouts  11.8 us (9%)
    ppermute x21, waiting for transfers between devices, fetch(): lax.ppermute(value, axes, [(device(*source(*spot)), device(*spot)) for sp...  36.8 us
    ppermute x21, starting transfers between devices, fetch(): lax.ppermute(value, axes, [(device(*source(*spot)), device(*spot)) for sp...  25.9 us
    pallas_call x2, Pallas kernels, turn(): pl.pallas_call(turn_kernel, grid_spec=pltpu.PrefetchScalarGridSpec(num_sc...  13.2 us
    pallas_call x1, Pallas kernels, input_grads(): pl.pallas_call(input_kernel, grid=(7,), in_specs=[pl.BlockSpec((784, 512)...  11.9 us
    unnamed x32, local copies, waits for them, and re-layouts  11.8 us
    pallas_call x4, Pallas kernels, weight_grads(): pl.pallas_call(weight_kernel, grid_spec=pltpu.PrefetchScalarGridSpec(num_...  11.6 us
    pallas_call x1, Pallas kernels, latent_grads(): pl.pallas_call(latent_kernel, grid_spec=pltpu.PrefetchScalarGridSpec(num_...  10.5 us
    pallas_call x3, Pallas kernels, combine(): pl.pallas_call(kernel, in_specs=[pl.BlockSpec(memory_space=pltpu.SMEM)] +...  3.61 us
  transfers between devices with their start and end apart: 21, of which 9 were waited for; matrix products, arithmetic and copies ran while one was open for 0% of the time, Pallas kernels for 27%

profile of v4, /device:TPU:0, one launch (start us, length us, event | category | flops | bytes accessed | tf_op | source)
XLA Modules:
  0.0 126.2 jit_solution(16310731937934304825)
XLA Ops:
  1.7 3.2 %collective-permute-start = (bf16[224,512]{1,0:T(8,128)(2,1)S(1)}, bf16[224,512]{1,0:T(8,128)(2,1)S(1)}, u32[]{:S(2)}, u32[]{:S(2)}) collective-permute-start(bf16[224,512]{1,0:T(8,128)(2,1)S(1)} %constant_dynamic-slice_fusion.one), channel_id=1, source_target_pairs={{4,0},{5,1},{6,2},{7,3},{8,4},{9,5},{10,6},{11,7},{12,8},{13,9},{1... | collective-permute-start | bytes 688136 | tf_op jit(solution)/shard_map/ppermute | solution.py:23
  5.5 1.0 collective-permute-start.2
  6.5 6.6 %turn.2 = (bf16[3584,768]{1,0:T(8,128)(2,1)}, f32[8,128]{1,0:T(8,128)S(1)}) custom-call(s32[4]{0:T(128)S(1)} %pad_add_fusion.place, bf16[768,7168]{1,0:T(8,128)(2,1)} %inputs.1), custom_call_target="tpu_custom_call" | custom-call | bytes 23068672 | tf_op jit(solution)/shard_map/turn/pallas_call | solution.py:48
  13.1 1.7 %collective-permute-done.2.four_ = bf16[224,512]{1,0:T(8,128)(2,1)S(1)} collective-permute-done((bf16[224,512]{1,0:T(8,128)(2,1)S(1)}, bf16[224,512]{1,0:T(8,128)(2,1)S(1)}, u32[]{:S(2)}, u32[]{:S(2)}) %collective-permute-start.2) | collective-permute-done | bytes 229408 | tf_op jit(solution)/shard_map/ppermute | solution.py:23
  14.9 4.1 %collective-permute-start.3 = (bf16[4,224,512]{2,1,0:T(8,128)(2,1)S(1)}, bf16[4,224,512]{2,1,0:T(8,128)(2,1)S(1)}, u32[]{:S(2)}, u32[]{:S(2)}) collective-permute-start(bf16[4,224,512]{2,1,0:T(8,128)(2,1)S(1)} %join.1.rest_0_), channel_id=1, source_target_pairs={{1,0},{2,1},{3,2},{0,3},{5,4},{6,5},{7,6},{4,7},{9,8},{10,9},{11,1... | collective-permute-start | bytes 2752520 | tf_op jit(solution)/shard_map/ppermute | solution.py:23
  19.0 1.3 collective-permute-start.5
  20.3 19.5 %collective-permute-done.3.rest_1_ = bf16[4,224,512]{2,1,0:T(8,128)(2,1)S(1)} collective-permute-done((bf16[4,224,512]{2,1,0:T(8,128)(2,1)S(1)}, bf16[4,224,512]{2,1,0:T(8,128)(2,1)S(1)}, u32[]{:S(2)}, u32[]{:S(2)}) %collective-permute-start.3) | collective-permute-done | bytes 917536 | tf_op jit(solution)/shard_map/ppermute | solution.py:23
  40.3 6.6 %turn.3 = (bf16[3584,768]{1,0:T(8,128)(2,1)}, f32[8,128]{1,0:T(8,128)S(1)}) custom-call(s32[4]{0:T(128)S(1)} %pad_add_fusion.place, bf16[768,7168]{1,0:T(8,128)(2,1)} %collective-permute-done.6.rows), custom_call_target="tpu_custom_call" | custom-call | bytes 23068672 | tf_op jit(solution)/shard_map/turn/pallas_call | solution.py:48
  48.0 1.4 %collective-permute-done.10.rest_7_ = bf16[4,224,512]{2,1,0:T(8,128)(2,1)S(1)} collective-permute-done((bf16[4,224,512]{2,1,0:T(8,128)(2,1)S(1)}, bf16[4,224,512]{2,1,0:T(8,128)(2,1)S(1)}, u32[]{:S(2)}, u32[]{:S(2)}) %collective-permute-start.10) | collective-permute-done | bytes 917536 | tf_op jit(solution)/shard_map/ppermute | solution.py:23
  49.5 4.3 %copy-done.2 = bf16[768,7168]{1,0:T(8,128)(2,1)S(1)} copy-done((bf16[768,7168]{1,0:T(8,128)(2,1)S(1)}, bf16[768,7168]{1,0:T(8,128)(2,1)}, u32[]{:S(2)}) %copy-start.2) | copy-done | bytes 11010072
  53.8 1.2 copy-done.7
  54.9 1.2 copy-done.9
  56.1 1.1 copy-done.10
  57.2 10.5 %latent.1 = (bf16[784,512]{1,0:T(8,128)(2,1)S(1)}, bf16[7168,512]{1,0:T(8,128)(2,1)S(1)}) custom-call(s32[4]{0:T(128)S(1)} %pad_add_fusion.place, bf16[768,7168]{1,0:T(8,128)(2,1)S(1)} %copy-done.2, bf16[768,512]{1,0:T(8,128)(2,1)S(1)} %copy-done.10, f32[1,512]{1,0:T(1,128)S(1)} %bitcast.10, bf16[4,224,512]{2,1,0:T(8,128)(2,1)S(1)} %join.1.rest_0_, ...), custom_call_target="tpu_custom_call" | custom-call | flops 5637144576 | bytes 29360128 | tf_op jit(solution)/shard_map/latent/pallas_call | solution.py:157
  67.9 2.2 %collective-permute-done.11.refs_5_ = bf16[784,512]{1,0:T(8,128)(2,1)S(1)} collective-permute-done((bf16[784,512]{1,0:T(8,128)(2,1)S(1)}, bf16[784,512]{1,0:T(8,128)(2,1)S(1)}, u32[]{:S(2)}, u32[]{:S(2)}) %collective-permute-start.11) | collective-permute-done | bytes 802848 | tf_op jit(solution)/shard_map/ppermute | solution.py:23
  70.2 3.1 %weight_grads.4 = (bf16[2,1808,128]{2,1,0:T(8,128)(2,1)}, f32[8,128]{1,0:T(8,128)S(1)}) custom-call(s32[4]{0:T(128)S(1)} %pad_add_fusion.place, bf16[3584,768]{1,0:T(8,128)(2,1)S(1)} %bitcast.7, bf16[3584,768]{1,0:T(8,128)(2,1)S(1)} %bitcast.7, bf16[3584,768]{1,0:T(8,128)(2,1)S(1)} %bitcast.9, bf16[3584,768]{1,0:T(8,128)(2,1)S(1)} %bitcast.9, ...), custom_call_target="tpu_custom_call" | custom-call | bytes 1048576 | tf_op jit(solution)/shard_map/weight_grads/pallas_call | solution.py:247
  73.3 3.0 %collective-permute-start.13 = (bf16[2,1808,128]{2,1,0:T(8,128)(2,1)}, bf16[2,1808,128]{2,1,0:T(8,128)(2,1)S(1)}, u32[]{:S(2)}, u32[]{:S(2)}) collective-permute-start(bf16[2,1808,128]{2,1,0:T(8,128)(2,1)} %get-tuple-element.42), channel_id=1, source_target_pairs={{64,0},{65,1},{66,2},{67,3},{68,4},{69,5},{70,6},{71,7},{72,8},{73... | collective-permute-start | bytes 2777096 | tf_op jit(solution)/shard_map/ppermute | solution.py:23
  76.3 3.1 %weight_grads.5 = (bf16[2,1808,128]{2,1,0:T(8,128)(2,1)}, f32[8,128]{1,0:T(8,128)S(1)}) custom-call(s32[4]{0:T(128)S(1)} %pad_add_fusion.place, bf16[3584,768]{1,0:T(8,128)(2,1)S(1)} %bitcast.7, bf16[3584,768]{1,0:T(8,128)(2,1)S(1)} %bitcast.7, bf16[3584,768]{1,0:T(8,128)(2,1)S(1)} %bitcast.9, bf16[3584,768]{1,0:T(8,128)(2,1)S(1)} %bitcast.9, ...), custom_call_target="tpu_custom_call" | custom-call | bytes 1048576 | tf_op jit(solution)/shard_map/weight_grads/pallas_call | solution.py:247
  80.0 3.1 %weight_grads.6 = (bf16[2,1808,128]{2,1,0:T(8,128)(2,1)}, f32[8,128]{1,0:T(8,128)S(1)}) custom-call(s32[4]{0:T(128)S(1)} %pad_add_fusion.place, bf16[3584,768]{1,0:T(8,128)(2,1)S(1)} %bitcast.7, bf16[3584,768]{1,0:T(8,128)(2,1)S(1)} %bitcast.7, bf16[3584,768]{1,0:T(8,128)(2,1)S(1)} %bitcast.9, bf16[3584,768]{1,0:T(8,128)(2,1)S(1)} %bitcast.9, ...), custom_call_target="tpu_custom_call" | custom-call | bytes 1048576 | tf_op jit(solution)/shard_map/weight_grads/pallas_call | solution.py:247
  83.1 2.7 %collective-permute-start.14 = (bf16[2,1808,128]{2,1,0:T(8,128)(2,1)}, bf16[2,1808,128]{2,1,0:T(8,128)(2,1)}, u32[]{:S(2)}, u32[]{:S(2)}) collective-permute-start(bf16[2,1808,128]{2,1,0:T(8,128)(2,1)} %get-tuple-element.43), channel_id=1, source_target_pairs={{32,0},{33,1},{34,2},{35,3},{36,4},{37,5},{38,6},{39,7},{40,8},{41... | collective-permute-start | bytes 2777096 | tf_op jit(solution)/shard_map/ppermute | solution.py:23
  85.8 2.3 %weight_grads.7 = (bf16[2,1808,128]{2,1,0:T(8,128)(2,1)S(1)}, f32[8,128]{1,0:T(8,128)S(1)}) custom-call(s32[4]{0:T(128)S(1)} %pad_add_fusion.place, bf16[3584,768]{1,0:T(8,128)(2,1)S(1)} %bitcast.7, bf16[3584,768]{1,0:T(8,128)(2,1)S(1)} %bitcast.7, bf16[3584,768]{1,0:T(8,128)(2,1)S(1)} %bitcast.9, bf16[3584,768]{1,0:T(8,128)(2,1)S(1)} %bitcast.9, ...), custom_call_target="tpu_custom_call" | custom-call | bytes 1048576 | tf_op jit(solution)/shard_map/weight_grads/pallas_call | solution.py:247
  89.0 11.9 %input_grads.1 = (bf16[768,7168]{1,0:T(8,128)(2,1)}, f32[8,128]{1,0:T(8,128)S(1)}) custom-call(bf16[784,512]{1,0:T(8,128)(2,1)S(1)} %get-tuple-element.31.refs_4_.grad, bf16[7168,512]{1,0:T(8,128)(2,1)} %copy-done.3, f32[8,128]{1,0:T(8,128)S(1)} %get-tuple-element.38.before), custom_call_target="tpu_custom_call" | custom-call | bytes 1048576 | tf_op jit(solution)/shard_map/input_grads/pallas_call | solution.py:189
  101.0 1.2 copy-done.5
  102.1 1.7 %first_kernel.1 = (bf16[960,128]{1,0:T(8,128)(2,1)S(1)}, bf16[960,128]{1,0:T(8,128)(2,1)S(1)}, bf16[960,128]{1,0:T(8,128)(2,1)S(1)}, bf16[960,128]{1,0:T(8,128)(2,1)S(1)}) custom-call(s32[4]{0:T(128)S(1)} %pad_add_fusion.place, bf16[2,1808,128]{2,1,0:T(8,128)(2,1)S(1)} %copy-done.5, bf16[2,1808,128]{2,1,0:T(8,128)(2,1)S(1)} %collective-permute-done.12.value.refs_1_, ...), custom_call_target="tpu_custom_call" | custom-call | bytes 1048576 | tf_op jit(solution)/shard_map/first_kernel/pallas_call | solution.py:324
  104.1 1.9 %collective-permute-start.16 = (bf16[960,128]{1,0:T(8,128)(2,1)S(1)}, bf16[960,128]{1,0:T(8,128)(2,1)S(1)}, u32[]{:S(2)}, u32[]{:S(2)}) collective-permute-start(bf16[960,128]{1,0:T(8,128)(2,1)S(1)} %get-tuple-element.47), channel_id=1, source_target_pairs={{8,0},{9,1},{10,2},{11,3},{12,4},{13,5},{14,6},{15,7},{0,8},{1,9},... | collective-permute-start | bytes 737288 | tf_op jit(solution)/shard_map/ppermute | solution.py:23
  105.9 1.2 collective-permute-start.17
  107.1 6.8 %collective-permute-done.15.refs_1_ = bf16[960,128]{1,0:T(8,128)(2,1)S(1)} collective-permute-done((bf16[960,128]{1,0:T(8,128)(2,1)S(1)}, bf16[960,128]{1,0:T(8,128)(2,1)S(1)}, u32[]{:S(2)}, u32[]{:S(2)}) %collective-permute-start.15) | collective-permute-done | bytes 245792 | tf_op jit(solution)/shard_map/ppermute | solution.py:23
  115.6 1.4 %collective-permute-start.18 = (bf16[240,128]{1,0:T(8,128)(2,1)S(1)}, bf16[240,128]{1,0:T(8,128)(2,1)S(1)}, u32[]{:S(2)}, u32[]{:S(2)}) collective-permute-start(bf16[240,128]{1,0:T(8,128)(2,1)S(1)} %get-tuple-element.50), channel_id=1, source_target_pairs={{3,0},{0,1},{1,2},{2,3},{7,4},{4,5},{5,6},{6,7},{11,8},{8,9},{9,10... | collective-permute-start | bytes 184328 | tf_op jit(solution)/shard_map/ppermute | solution.py:23
  117.0 3.8 %collective-permute-start.19 = (bf16[240,128]{1,0:T(8,128)(2,1)S(1)}, bf16[240,128]{1,0:T(8,128)(2,1)S(1)}, u32[]{:S(2)}, u32[]{:S(2)}) collective-permute-start(bf16[240,128]{1,0:T(8,128)(2,1)S(1)} %get-tuple-element.51), channel_id=1, source_target_pairs={{2,0},{3,1},{0,2},{1,3},{6,4},{7,5},{4,6},{5,7},{10,8},{11,9},{8,1... | collective-permute-start | bytes 184328 | tf_op jit(solution)/shard_map/ppermute | solution.py:23
  121.5 2.1 %collective-permute-done.19.refs_2_ = bf16[240,128]{1,0:T(8,128)(2,1)S(1)} collective-permute-done((bf16[240,128]{1,0:T(8,128)(2,1)S(1)}, bf16[240,128]{1,0:T(8,128)(2,1)S(1)}, u32[]{:S(2)}, u32[]{:S(2)}) %collective-permute-start.19) | collective-permute-done | bytes 61472 | tf_op jit(solution)/shard_map/ppermute | solution.py:23
  123.6 1.4 %collective-permute-done.20.refs_3_ = bf16[240,128]{1,0:T(8,128)(2,1)S(1)} collective-permute-done((bf16[240,128]{1,0:T(8,128)(2,1)S(1)}, bf16[240,128]{1,0:T(8,128)(2,1)S(1)}, u32[]{:S(2)}, u32[]{:S(2)}) %collective-permute-start.20) | collective-permute-done | bytes 61472 | tf_op jit(solution)/shard_map/ppermute | solution.py:23
  125.0 1.2 third_kernel.1
  (61 shorter events, 7.9 us)
Async XLA Ops:
  0.6 39.6 %collective-permute-start.6 = (bf16[768,7168]{1,0:T(8,128)(2,1)}, bf16[768,7168]{1,0:T(8,128)(2,1)}, u32[]{:S(2)}, u32[]{:S(2)}) collective-permute-start(bf16[768,7168]{1,0:T(8,128)(2,1)} %inputs.1), channel_id=1, source_target_pairs={{16,0},{17,1},{18,2},{19,3},{20,4},{21,5},{22,6},{23,7},{24,8},{25... | collective-permute-start | bytes 33030152 | tf_op jit(solution)/shard_map/ppermute | solution.py:23
  1.7 11.4 %collective-permute-start = (bf16[224,512]{1,0:T(8,128)(2,1)S(1)}, bf16[224,512]{1,0:T(8,128)(2,1)S(1)}, u32[]{:S(2)}, u32[]{:S(2)}) collective-permute-start(bf16[224,512]{1,0:T(8,128)(2,1)S(1)} %constant_dynamic-slice_fusion.one), channel_id=1, source_target_pairs={{4,0},{5,1},{6,2},{7,3},{8,4},{9,5},{10,6},{11,7},{12,8},{13,9},{1... | collective-permute-start | bytes 688136 | tf_op jit(solution)/shard_map/ppermute | solution.py:23
  4.8 8.3 %collective-permute-start.1 = (bf16[224,512]{1,0:T(8,128)(2,1)S(1)}, bf16[224,512]{1,0:T(8,128)(2,1)S(1)}, u32[]{:S(2)}, u32[]{:S(2)}) collective-permute-start(bf16[224,512]{1,0:T(8,128)(2,1)S(1)} %constant_dynamic-slice_fusion.one), channel_id=1, source_target_pairs={{8,0},{9,1},{10,2},{11,3},{12,4},{13,5},{14,6},{15,7},{0,8},{1,9},... | collective-permute-start | bytes 688136 | tf_op jit(solution)/shard_map/ppermute | solution.py:23
  5.5 9.4 %collective-permute-start.2 = (bf16[224,512]{1,0:T(8,128)(2,1)S(1)}, bf16[224,512]{1,0:T(8,128)(2,1)S(1)}, u32[]{:S(2)}, u32[]{:S(2)}) collective-permute-start(bf16[224,512]{1,0:T(8,128)(2,1)S(1)} %constant_dynamic-slice_fusion.one), channel_id=1, source_target_pairs={{12,0},{13,1},{14,2},{15,3},{0,4},{1,5},{2,6},{3,7},{4,8},{5,9},{6... | collective-permute-start | bytes 688136 | tf_op jit(solution)/shard_map/ppermute | solution.py:23
  6.5 43.0 %copy-start.11 = (f32[512]{0:T(512)S(1)}, f32[512]{0:T(512)}, u32[]{:S(2)}) copy-start(f32[512]{0:T(512)} %param.7) | copy-start | bytes 6148
  14.9 24.8 %collective-permute-start.3 = (bf16[4,224,512]{2,1,0:T(8,128)(2,1)S(1)}, bf16[4,224,512]{2,1,0:T(8,128)(2,1)S(1)}, u32[]{:S(2)}, u32[]{:S(2)}) collective-permute-start(bf16[4,224,512]{2,1,0:T(8,128)(2,1)S(1)} %join.1.rest_0_), channel_id=1, source_target_pairs={{1,0},{2,1},{3,2},{0,3},{5,4},{6,5},{7,6},{4,7},{9,8},{10,9},{11,1... | collective-permute-start | bytes 2752520 | tf_op jit(solution)/shard_map/ppermute | solution.py:23
  19.0 20.8 %collective-permute-start.4 = (bf16[4,224,512]{2,1,0:T(8,128)(2,1)S(1)}, bf16[4,224,512]{2,1,0:T(8,128)(2,1)S(1)}, u32[]{:S(2)}, u32[]{:S(2)}) collective-permute-start(bf16[4,224,512]{2,1,0:T(8,128)(2,1)S(1)} %join.1.rest_0_), channel_id=1, source_target_pairs={{2,0},{3,1},{0,2},{1,3},{6,4},{7,5},{4,6},{5,7},{10,8},{11,9},{8,1... | collective-permute-start | bytes 2752520 | tf_op jit(solution)/shard_map/ppermute | solution.py:23
  19.0 27.8 %collective-permute-start.5 = (bf16[4,224,512]{2,1,0:T(8,128)(2,1)S(1)}, bf16[4,224,512]{2,1,0:T(8,128)(2,1)S(1)}, u32[]{:S(2)}, u32[]{:S(2)}) collective-permute-start(bf16[4,224,512]{2,1,0:T(8,128)(2,1)S(1)} %join.1.rest_0_), channel_id=1, source_target_pairs={{3,0},{0,1},{1,2},{2,3},{7,4},{4,5},{5,6},{6,7},{11,8},{8,9},{9,10... | collective-permute-start | bytes 2752520 | tf_op jit(solution)/shard_map/ppermute | solution.py:23
  20.3 26.8 %collective-permute-start.7 = (bf16[4,224,512]{2,1,0:T(8,128)(2,1)S(1)}, bf16[4,224,512]{2,1,0:T(8,128)(2,1)S(1)}, u32[]{:S(2)}, u32[]{:S(2)}) collective-permute-start(bf16[4,224,512]{2,1,0:T(8,128)(2,1)S(1)} %join.1.rest_0_), channel_id=1, source_target_pairs={{16,0},{17,1},{18,2},{19,3},{20,4},{21,5},{22,6},{23,7},{24,8},{25... | collective-permute-start | bytes 2752520 | tf_op jit(solution)/shard_map/ppermute | solution.py:23
  39.7 8.3 %collective-permute-start.8 = (bf16[4,224,512]{2,1,0:T(8,128)(2,1)S(1)}, bf16[4,224,512]{2,1,0:T(8,128)(2,1)}, u32[]{:S(2)}, u32[]{:S(2)}) collective-permute-start(bf16[4,224,512]{2,1,0:T(8,128)(2,1)S(1)} %collective-permute-done.3.rest_1_), channel_id=1, source_target_pairs={{16,0},{17,1},{18,2},{19,3},{20,4},{21,5},{22,6},{23,7},{24,8},{25... | collective-permute-start | bytes 2752520 | tf_op jit(solution)/shard_map/ppermute | solution.py:23
  39.7 9.7 %copy-start.6 = (bf16[4,224,512]{2,1,0:T(8,128)(2,1)}, bf16[4,224,512]{2,1,0:T(8,128)(2,1)S(1)}, u32[]{:S(2)}) copy-start(bf16[4,224,512]{2,1,0:T(8,128)(2,1)S(1)} %collective-permute-done.4.rest_2_) | copy-start | bytes 2752516
  39.7 8.3 %collective-permute-start.9 = (bf16[4,224,512]{2,1,0:T(8,128)(2,1)S(1)}, bf16[4,224,512]{2,1,0:T(8,128)(2,1)}, u32[]{:S(2)}, u32[]{:S(2)}) collective-permute-start(bf16[4,224,512]{2,1,0:T(8,128)(2,1)S(1)} %collective-permute-done.4.rest_2_), channel_id=1, source_target_pairs={{16,0},{17,1},{18,2},{19,3},{20,4},{21,5},{22,6},{23,7},{24,8},{25... | collective-permute-start | bytes 2752520 | tf_op jit(solution)/shard_map/ppermute | solution.py:23
  46.8 23.3 %slice-start = ((s8[5505024]{0:T(1024)(128)(4,1)}), s8[4194304]{0:T(1024)(128)(4,1)S(1)}, s32[]{:S(2)}) async-start(s8[5505024]{0:T(1024)(128)(4,1)} %bitcast.6), calls=%async_computation | async-start | bytes 8388608
  46.8 23.3 %slice-start.2 = ((s8[5505024]{0:T(1024)(128)(4,1)}), s8[4194304]{0:T(1024)(128)(4,1)S(1)}, s32[]{:S(2)}) async-start(s8[5505024]{0:T(1024)(128)(4,1)} %bitcast.8), calls=%async_computation.2 | async-start | bytes 8388608
  46.9 2.6 %collective-permute-start.10 = (bf16[4,224,512]{2,1,0:T(8,128)(2,1)S(1)}, bf16[4,224,512]{2,1,0:T(8,128)(2,1)S(1)}, u32[]{:S(2)}, u32[]{:S(2)}) collective-permute-start(bf16[4,224,512]{2,1,0:T(8,128)(2,1)S(1)} %tie.1.rest_3_), channel_id=1, source_target_pairs={{16,0},{17,1},{18,2},{19,3},{20,4},{21,5},{22,6},{23,7},{24,8},{25... | collective-permute-start | bytes 2752520 | tf_op jit(solution)/shard_map/ppermute | solution.py:23
  49.5 4.3 %copy-start.2 = (bf16[768,7168]{1,0:T(8,128)(2,1)S(1)}, bf16[768,7168]{1,0:T(8,128)(2,1)}, u32[]{:S(2)}) copy-start(bf16[768,7168]{1,0:T(8,128)(2,1)} %inputs.1) | copy-start | bytes 33030148
  54.9 1.2 copy-start.9
  57.2 12.9 %slice-start.1 = ((s8[5505024]{0:T(1024)(128)(4,1)}), s8[1310720]{0:T(1024)(128)(4,1)S(1)}, s32[]{:S(2)}) async-start(s8[5505024]{0:T(1024)(128)(4,1)} %bitcast.6), calls=%async_computation.1 | async-start | bytes 2621440
  57.2 12.9 %slice-start.3 = ((s8[5505024]{0:T(1024)(128)(4,1)}), s8[1310720]{0:T(1024)(128)(4,1)S(1)}, s32[]{:S(2)}) async-start(s8[5505024]{0:T(1024)(128)(4,1)} %bitcast.8), calls=%async_computation.3 | async-start | bytes 2621440
  67.7 5.5 %copy-start.3 = (bf16[7168,512]{1,0:T(8,128)(2,1)}, bf16[7168,512]{1,0:T(8,128)(2,1)S(1)}, u32[]{:S(2)}) copy-start(bf16[7168,512]{1,0:T(8,128)(2,1)S(1)} %get-tuple-element.32.weight) | copy-start | bytes 22020100
  67.8 2.4 %collective-permute-start.11 = (bf16[784,512]{1,0:T(8,128)(2,1)S(1)}, bf16[784,512]{1,0:T(8,128)(2,1)S(1)}, u32[]{:S(2)}, u32[]{:S(2)}) collective-permute-start(bf16[784,512]{1,0:T(8,128)(2,1)S(1)} %get-tuple-element.31.refs_4_.grad), channel_id=1, source_target_pairs={{16,0},{17,1},{18,2},{19,3},{20,4},{21,5},{22,6},{23,7},{24,8},{25... | collective-permute-start | bytes 2408456 | tf_op jit(solution)/shard_map/ppermute | solution.py:23
  73.3 27.7 %collective-permute-start.13 = (bf16[2,1808,128]{2,1,0:T(8,128)(2,1)}, bf16[2,1808,128]{2,1,0:T(8,128)(2,1)S(1)}, u32[]{:S(2)}, u32[]{:S(2)}) collective-permute-start(bf16[2,1808,128]{2,1,0:T(8,128)(2,1)} %get-tuple-element.42), channel_id=1, source_target_pairs={{64,0},{65,1},{66,2},{67,3},{68,4},{69,5},{70,6},{71,7},{72,8},{73... | collective-permute-start | bytes 2777096 | tf_op jit(solution)/shard_map/ppermute | solution.py:23
  79.4 21.5 %collective-permute-start.12 = (bf16[2,1808,128]{2,1,0:T(8,128)(2,1)}, bf16[2,1808,128]{2,1,0:T(8,128)(2,1)S(1)}, u32[]{:S(2)}, u32[]{:S(2)}) collective-permute-start(bf16[2,1808,128]{2,1,0:T(8,128)(2,1)} %get-tuple-element.41), channel_id=1, source_target_pairs={{96,0},{97,1},{98,2},{99,3},{100,4},{101,5},{102,6},{103,7},{104,8... | collective-permute-start | bytes 2777096 | tf_op jit(solution)/shard_map/ppermute | solution.py:23
  83.1 17.8 %collective-permute-start.14 = (bf16[2,1808,128]{2,1,0:T(8,128)(2,1)}, bf16[2,1808,128]{2,1,0:T(8,128)(2,1)}, u32[]{:S(2)}, u32[]{:S(2)}) collective-permute-start(bf16[2,1808,128]{2,1,0:T(8,128)(2,1)} %get-tuple-element.43), channel_id=1, source_target_pairs={{32,0},{33,1},{34,2},{35,3},{36,4},{37,5},{38,6},{39,7},{40,8},{41... | collective-permute-start | bytes 2777096 | tf_op jit(solution)/shard_map/ppermute | solution.py:23
  85.8 40.5 %copy-start.1 = (bf16[448,512]{1,0:T(8,128)(2,1)S(1)}, bf16[448,512]{1,0:T(8,128)(2,1)}, u32[]{:S(2)}) copy-start(bf16[448,512]{1,0:T(8,128)(2,1)} %param.6) | copy-start | bytes 1376260
  101.0 1.2 copy-start.5
  103.8 10.1 %collective-permute-start.15 = (bf16[960,128]{1,0:T(8,128)(2,1)S(1)}, bf16[960,128]{1,0:T(8,128)(2,1)S(1)}, u32[]{:S(2)}, u32[]{:S(2)}) collective-permute-start(bf16[960,128]{1,0:T(8,128)(2,1)S(1)} %get-tuple-element.46), channel_id=1, source_target_pairs={{12,0},{13,1},{14,2},{15,3},{0,4},{1,5},{2,6},{3,7},{4,8},{5,9},{6... | collective-permute-start | bytes 737288 | tf_op jit(solution)/shard_map/ppermute | solution.py:23
  104.1 9.9 %collective-permute-start.16 = (bf16[960,128]{1,0:T(8,128)(2,1)S(1)}, bf16[960,128]{1,0:T(8,128)(2,1)S(1)}, u32[]{:S(2)}, u32[]{:S(2)}) collective-permute-start(bf16[960,128]{1,0:T(8,128)(2,1)S(1)} %get-tuple-element.47), channel_id=1, source_target_pairs={{8,0},{9,1},{10,2},{11,3},{12,4},{13,5},{14,6},{15,7},{0,8},{1,9},... | collective-permute-start | bytes 737288 | tf_op jit(solution)/shard_map/ppermute | solution.py:23
  105.9 8.9 %collective-permute-start.17 = (bf16[960,128]{1,0:T(8,128)(2,1)S(1)}, bf16[960,128]{1,0:T(8,128)(2,1)S(1)}, u32[]{:S(2)}, u32[]{:S(2)}) collective-permute-start(bf16[960,128]{1,0:T(8,128)(2,1)S(1)} %get-tuple-element.48), channel_id=1, source_target_pairs={{4,0},{5,1},{6,2},{7,3},{8,4},{9,5},{10,6},{11,7},{12,8},{13,9},{1... | collective-permute-start | bytes 737288 | tf_op jit(solution)/shard_map/ppermute | solution.py:23
  115.6 6.0 %collective-permute-start.18 = (bf16[240,128]{1,0:T(8,128)(2,1)S(1)}, bf16[240,128]{1,0:T(8,128)(2,1)S(1)}, u32[]{:S(2)}, u32[]{:S(2)}) collective-permute-start(bf16[240,128]{1,0:T(8,128)(2,1)S(1)} %get-tuple-element.50), channel_id=1, source_target_pairs={{3,0},{0,1},{1,2},{2,3},{7,4},{4,5},{5,6},{6,7},{11,8},{8,9},{9,10... | collective-permute-start | bytes 184328 | tf_op jit(solution)/shard_map/ppermute | solution.py:23
  117.0 6.7 %collective-permute-start.19 = (bf16[240,128]{1,0:T(8,128)(2,1)S(1)}, bf16[240,128]{1,0:T(8,128)(2,1)S(1)}, u32[]{:S(2)}, u32[]{:S(2)}) collective-permute-start(bf16[240,128]{1,0:T(8,128)(2,1)S(1)} %get-tuple-element.51), channel_id=1, source_target_pairs={{2,0},{3,1},{0,2},{1,3},{6,4},{7,5},{4,6},{5,7},{10,8},{11,9},{8,1... | collective-permute-start | bytes 184328 | tf_op jit(solution)/shard_map/ppermute | solution.py:23
  120.8 4.2 %collective-permute-start.20 = (bf16[240,128]{1,0:T(8,128)(2,1)S(1)}, bf16[240,128]{1,0:T(8,128)(2,1)S(1)}, u32[]{:S(2)}, u32[]{:S(2)}) collective-permute-start(bf16[240,128]{1,0:T(8,128)(2,1)S(1)} %get-tuple-element.52), channel_id=1, source_target_pairs={{1,0},{2,1},{3,2},{0,3},{5,4},{6,5},{7,6},{4,7},{9,8},{10,9},{11,1... | collective-permute-start | bytes 184328 | tf_op jit(solution)/shard_map/ppermute | solution.py:23
  (5 other events, 5.2 us)

commit v5 on v4

--- a/solution.py
+++ b/solution.py
@@ -1,3 +1,5 @@
+import functools
+
 import jax
 import jax.numpy as jnp
 from jax import lax
@@ -57,27 +59,27 @@
             ],
         ),
         out_shape=[jax.ShapeDtypeStruct((3584, 768), bf16), order],
-        compiler_params=pltpu.CompilerParams(vmem_limit_bytes=52 * MIB),
+        compiler_params=pltpu.CompilerParams(vmem_limit_bytes=16 * MIB),
         cost_estimate=pl.CostEstimate(flops=0, bytes_accessed=22 * MIB, transcendentals=0),
         name="turn",
     )(place, inputs)
 
 
-def tie_kernel(value, token, out):
-    out[...] = value[...]
-
-
-def tie(value, token):
+def tie_kernel(value, *refs):
+    refs[-1][...] = value[...]
+
+
+def tie(value, *tokens):
     vmem = pl.BlockSpec(memory_space=pltpu.VMEM)
     return pl.pallas_call(
         tie_kernel,
-        in_specs=[vmem] * 2,
+        in_specs=[vmem] * (1 + len(tokens)),
         out_specs=vmem,
         out_shape=jax.ShapeDtypeStruct(value.shape, value.dtype),
         compiler_params=pltpu.CompilerParams(vmem_limit_bytes=8 * MIB),
         cost_estimate=pl.CostEstimate(flops=0, bytes_accessed=2 * MIB, transcendentals=0),
         name="tie",
-    )(value, token)
+    )(value, *tokens)
 
 
 def join_kernel(one, two, three, four_, token, out):
@@ -91,52 +93,119 @@
         join_kernel,
         in_specs=[vmem] * 5,
         out_specs=vmem,
-        out_shape=jax.ShapeDtypeStruct((4, 224, 512), bf16),
+        out_shape=jax.ShapeDtypeStruct((4, 448, 256), bf16),
         compiler_params=pltpu.CompilerParams(vmem_limit_bytes=8 * MIB),
         cost_estimate=pl.CostEstimate(flops=0, bytes_accessed=2 * MIB, transcendentals=0),
         name="join",
     )(*values, token)
 
 
-def latent_kernel(place, inputs, cotangent, gain, *rest):
-    pieces, (out, weight_out, held, leave) = rest[:8], rest[8:]
-    step = pl.program_id(0)
-    core, y, z = place[1], place[2], place[3]
-    copy = pltpu.make_async_copy(held, weight_out, leave)
-
-    @pl.when(step == 0)
-    def _():
-        for side in range(2):
-            part = core if side == 0 else 1 - core
-            for far in four:
-                for near in four:
-                    along_y = lax.rem(y + jnp.where(part == 0, near, far), 4)
-                    along_z = lax.rem(z + jnp.where(part == 0, far, near), 4)
-                    start = pl.multiple_of((along_y * 4 + along_z) * 448 + part * 224, 224)
-                    held[pl.ds(start, 224), :] = pieces[side * 4 + far][near]
+def spot(place, side, far, near):
+    part = place[1] if side == 0 else 1 - place[1]
+    along_y = lax.rem(place[2] + jnp.where(part == 0, near, far), 4)
+    along_z = lax.rem(place[3] + jnp.where(part == 0, far, near), 4)
+    return along_y * 4 + along_z, part
+
+
+def norm(place, first, second, cotangent, gain, out, row):
+    core = place[1]
+    own = pl.ds(pl.multiple_of(core * 256, 256), 256)
+    other = pl.ds(pl.multiple_of(256 - core * 256, 256), 256)
+
+    def body(i, sums):
+        tokens = pl.ds(pl.multiple_of(i * 64, 64), 64)
+        latent = [first[tokens, :], second[tokens, :]]
+        square = sum(jnp.sum(value * value, axis=1, keepdims=True) for value in latent)
+        scale = lax.rsqrt(square * (1.0 / 512) + epsilon)
+        normed = [value * scale for value in latent]
+        upstream = [cotangent[tokens, lane].astype(f32) for lane in (own, other)]
+        scaled = [value * gain[:, lane] for value, lane in zip(upstream, (own, other))]
+        center = sum(jnp.sum(u * v, axis=1, keepdims=True) for u, v in zip(scaled, normed)) * (1.0 / 512)
+        for lane, u, v in zip((own, other), scaled, normed):
+            out[tokens, lane] = (scale * (u - v * center)).astype(bf16)
+        return tuple(
+            total + jnp.sum((u * v).reshape(8, 8, 256), axis=0) for total, u, v in zip(sums, upstream, normed)
+        )
+
+    sums = lax.fori_loop(0, 12, body, (jnp.zeros((8, 256), f32),) * 2, unroll=2)
+    for lane, value in zip((own, other), sums):
+        row[:, lane] = jnp.broadcast_to(jnp.sum(value, axis=0, keepdims=True), (8, 256))
+    out[768:784, :] = split(row[0:1, :])
+
+
+def latent_kernel(side, far, has_before, last, place, inputs, piece, *refs):
+    at = 1 * has_before
+    ending = refs[at : at + 3 * last]
+    out, token, filled, window, arrive, *extra = refs[at + 3 * last :]
+    token[...] = jnp.zeros((8, 128), f32)
+    total = extra[0] if last else out
+    copies = []
+    for near in four:
+        block, part = spot(place, side, far, near)
+        first = pl.multiple_of(lax.div(block * 7, 2) * 128, 128)
+        copy = pltpu.make_async_copy(
+            inputs.at[:, pl.ds(first, 512)], window.at[:, 512 * near : 512 * near + 512], arrive.at[near]
+        )
         copy.start()
-
-    latent = jnp.dot(inputs[...], held[...], preferred_element_type=f32)
-    scale = lax.rsqrt(jnp.mean(latent * latent, axis=1, keepdims=True) + epsilon)
-    normed = latent * scale
-    upstream = cotangent[...].astype(f32)
-    scaled = upstream * gain[...]
-    center = jnp.mean(scaled * normed, axis=1, keepdims=True)
-    out[pl.ds(pl.multiple_of(step * 256, 256), 256), :] = (scale * (scaled - normed * center)).astype(bf16)
-    gain_grad = jnp.sum(upstream * normed, axis=0, keepdims=True)
-
-    @pl.when(step > 0)
-    def _():
-        out_gain = gain_grad + total_of(out)
-        out[768:784, :] = split(out_gain)
-
-    @pl.when(step == 0)
-    def _():
-        out[768:784, :] = split(gain_grad)
-
-    @pl.when(step == 2)
-    def _():
+        copies.append(copy)
+    for near in four:
+        block, part = spot(place, side, far, near)
+        odd = lax.rem(block, 2)
+        filled[pl.ds(pl.multiple_of(512 * near + odd * 64, 64), 448), :] = piece[near]
+        filled[pl.ds(pl.multiple_of(512 * near + 448 - odd * 448, 64), 64), :] = jnp.zeros((64, 256), bf16)
+    for copy in copies:
         copy.wait()
+    for start in range(0, 768, 256):
+        product = jnp.dot(window[start : start + 256, :], filled[...], preferred_element_type=f32)
+        total[start : start + 256, :] = refs[0][start : start + 256, :] + product if has_before else product
+    if last:
+        norm(place, ending[0], total, ending[1], ending[2], out, extra[1])
+
+
+def latent_part(place, inputs, piece, side, far, before=None, ending=()):
+    hbm, vmem = pl.BlockSpec(memory_space=pltpu.HBM), pl.BlockSpec(memory_space=pltpu.VMEM)
+    last = len(ending) > 0
+    operands = [place, inputs, piece] + ([] if before is None else [before]) + list(ending)
+    specs = [pl.BlockSpec(memory_space=pltpu.SMEM), hbm] + [vmem] * (len(operands) - 2)
+    scratch = [pltpu.VMEM((2048, 256), bf16), pltpu.VMEM((768, 2048), bf16), pltpu.SemaphoreType.DMA((4,))]
+    out = jax.ShapeDtypeStruct((768, 256), f32)
+    if last:
+        scratch += [pltpu.VMEM((768, 256), f32), pltpu.VMEM((8, 512), f32)]
+        out = jax.ShapeDtypeStruct((784, 512), bf16)
+    return pl.pallas_call(
+        functools.partial(latent_kernel, side, far, before is not None, last),
+        in_specs=specs,
+        out_specs=[vmem] * 2,
+        scratch_shapes=scratch,
+        out_shape=[out, order],
+        compiler_params=pltpu.CompilerParams(vmem_limit_bytes=14 * MIB),
+        cost_estimate=pl.CostEstimate(flops=768 * 2048 * 512, bytes_accessed=6 * MIB, transcendentals=0),
+        name="latent",
+    )(*operands)
+
+
+def assemble_kernel(place, *refs):
+    out = refs[9]
+    for side in range(2):
+        for far in four:
+            for near in four:
+                block, part = spot(place, side, far, near)
+                rows = pl.ds(pl.multiple_of(block * 448, 64), 448)
+                columns = pl.ds(pl.multiple_of(part * 256, 256), 256)
+                out[rows, columns] = refs[side * 4 + far][near]
+
+
+def assemble(place, pieces, token):
+    vmem = pl.BlockSpec(memory_space=pltpu.VMEM)
+    return pl.pallas_call(
+        assemble_kernel,
+        in_specs=[pl.BlockSpec(memory_space=pltpu.SMEM)] + [vmem] * 9,
+        out_specs=vmem,
+        out_shape=jax.ShapeDtypeStruct((7168, 512), bf16),
+        compiler_params=pltpu.CompilerParams(vmem_limit_bytes=20 * MIB),
+        cost_estimate=pl.CostEstimate(flops=0, bytes_accessed=MIB, transcendentals=0),
+        name="assemble",
+    )(place, *pieces, token)
 
 
 def parts(value):
@@ -153,53 +222,32 @@
     return jnp.sum(rows[768:784, :].astype(f32), axis=0, keepdims=True)
 
 
-def latent_grads(place, inputs, cotangent, gain, pieces):
-    return pl.pallas_call(
-        latent_kernel,
-        grid_spec=pltpu.PrefetchScalarGridSpec(
-            num_scalar_prefetch=1,
-            grid=(3,),
-            in_specs=[
-                pl.BlockSpec((256, 7168), lambda i, place: (i, 0)),
-                pl.BlockSpec((256, 512), lambda i, place: (i, 0)),
-                pl.BlockSpec((1, 512), lambda i, place: (0, 0)),
-            ]
-            + [pl.BlockSpec(memory_space=pltpu.VMEM)] * 8,
-            out_specs=[
-                pl.BlockSpec((784, 512), lambda i, place: (0, 0)),
-                pl.BlockSpec(memory_space=pl.ANY),
-            ],
-            scratch_shapes=[pltpu.VMEM((7168, 512), bf16), pltpu.SemaphoreType.DMA],
-        ),
-        out_shape=[jax.ShapeDtypeStruct((784, 512), bf16), jax.ShapeDtypeStruct((7168, 512), bf16)],
-        compiler_params=pltpu.CompilerParams(vmem_limit_bytes=24 * MIB),
-        cost_estimate=pl.CostEstimate(flops=2 * 768 * 7168 * 512, bytes_accessed=28 * MIB, transcendentals=768),
-        name="latent",
-    )(place, inputs, cotangent, gain, *pieces)
-
-
-def input_kernel(grad, weight, before, out, token):
+def input_kernel(grad, weight, before, *refs):
+    out, token = refs[-2:]
     token[...] = jnp.zeros((8, 128), f32)
     out[...] = lax.dot_general(
         grad[:768, :], weight[...], (((1,), (1,)), ((), ())), preferred_element_type=f32
     ).astype(bf16)
 
 
-def input_grads(grad, weight, token):
+def input_grads(grad, weight, token, first, count, begun=()):
+    small = pl.BlockSpec((8, 128), lambda i: (0, 0))
     return pl.pallas_call(
         input_kernel,
-        grid=(7,),
+        grid=(count,),
         in_specs=[
             pl.BlockSpec((784, 512), lambda i: (0, 0)),
-            pl.BlockSpec((1024, 512), lambda i: (i, 0)),
-            pl.BlockSpec((8, 128), lambda i: (0, 0)),
-        ],
-        out_specs=[pl.BlockSpec((768, 1024), lambda i: (0, i)), pl.BlockSpec((8, 128), lambda i: (0, 0))],
+            pl.BlockSpec((1024, 512), lambda i: (first + i, 0)),
+            small,
+        ]
+        + [pl.BlockSpec(memory_space=pltpu.HBM)] * len(begun),
+        out_specs=[pl.BlockSpec((768, 1024), lambda i: (0, first + i)), small],
         out_shape=[jax.ShapeDtypeStruct((768, 7168), bf16), order],
-        compiler_params=pltpu.CompilerParams(vmem_limit_bytes=52 * MIB),
+        input_output_aliases={3: 0} if begun else {},
+        compiler_params=pltpu.CompilerParams(vmem_limit_bytes=40 * MIB),
         cost_estimate=pl.CostEstimate(flops=0, bytes_accessed=MIB, transcendentals=0),
         name="input_grads",
-    )(grad, weight, token)
+    )(grad, weight, token, *begun)
 
 
 lanes = [slice(128 * i, 128 * i + 128) for i in four]
@@ -266,7 +314,8 @@
 
 
 def first_kernel(place, *refs):
-    partial, out = refs[:4], refs[-4:]
+    partial, out, token = refs[:4], refs[-5:-1], refs[-1]
+    token[...] = jnp.zeros((8, 128), f32)
     other = jnp.where(place[1] == 0, place[2], place[0])
     for to in four:
         at = lax.rem(other + to, 4)
@@ -278,7 +327,7 @@
 
 
 def second_kernel(place, *refs):
-    sums, out, held = refs[:4], refs[4:8], refs[8]
+    sums, out, held = refs[:4], refs[5:9], refs[9]
     x, core, y, z = [place[i] for i in four]
     for i in four:
         held[i] = sums[i][896:960, :].astype(f32)
@@ -350,36 +399,59 @@
     return [values[0]] + [along(values[by], by) for by in (1, 2, 3)]
 
 
-def reduce_scatter(place, partial, token):
+def first_sums(place, partial, latent_grad, gathered, token):
     sums = exchange(partial, along_major)
+    input_grad, token = input_grads(latent_grad, gathered, token, 0, 4)
     token = touch(sums[1], touch(sums[2], token))
-    sums = combine(first_kernel, [((960, 128), bf16)] * 4, place, sums, tokens=[token])
-    sums = exchange(sums, along_other)
-    sums = combine(second_kernel, [((240, 128), bf16)] * 4, place, sums, [pltpu.VMEM((4, 64, 128), f32)])
+    outs = [((960, 128), bf16)] * 4 + [((8, 128), f32)]
+    return combine(first_kernel, outs, place, sums, tokens=[token]), input_grad
+
+
+def last_sums(place, sums, latent_grad, gathered, input_grad):
+    token = sums[4]
+    sums = exchange(sums[:4], along_other)
+    input_grad, token = input_grads(latent_grad, gathered, token, 4, 3, [input_grad])
+    scratch = [pltpu.VMEM((4, 64, 128), f32)]
+    sums = combine(second_kernel, [((240, 128), bf16)] * 4, place, sums, scratch, [token])
     sums = exchange(sums, along_z)
-    return combine(third_kernel, [((56, 512), f32), ((4, 128), f32)], place, sums)
+    return *combine(third_kernel, [((56, 512), f32), ((4, 128), f32)], place, sums), input_grad
 
 
 def shards(inputs, cotangent, weight, norm_gain):
     dp, shard = lax.axis_index("dp"), lax.axis_index("shard")
     core = dp % 2
     place = jnp.stack([dp // 2, core, shard // 4, shard % 4]).astype(jnp.int32)
-    half = lax.dynamic_slice_in_dim(weight, core * 224, 224, 0)
+    half = lax.dynamic_slice_in_dim(weight, core * 256, 256, 1)
     other_inputs = twin(inputs)
     kept, token = turn(place, inputs)
     line = join([half] + [fetch_first(half, by) for by in (1, 2, 3)], token)
     mine = [line] + [fetch_second(line, by) for by in (1, 2, 3)]
     other, token = turn(place, other_inputs)
-    mine[3] = tie(mine[3], token)
-    pieces = mine + [twin(piece) for piece in mine]
-    latent_grad, gathered = latent_grads(place, inputs, cotangent, norm_gain.reshape(1, 512), pieces)
+    gain = norm_gain.reshape(1, 512)
+    parts_of = functools.partial(latent_part, place, inputs)
+    theirs = [twin(line)]
+    first, _ = parts_of(mine[0], 0, 0)
+    second, done = parts_of(theirs[0], 1, 0)
+    mine[1] = tie(mine[1], token, done)
+    theirs.append(twin(mine[1]))
+    theirs.append(twin(mine[2]))
+    first, _ = parts_of(mine[1], 0, 1, first)
+    first, done = parts_of(mine[2], 0, 2, first)
+    second, after = parts_of(theirs[1], 1, 1, second)
+    mine[3] = tie(mine[3], done, after)
+    theirs.append(twin(mine[3]))
+    second, _ = parts_of(theirs[2], 1, 2, second)
+    first, _ = parts_of(mine[3], 0, 3, first)
+    second, _ = parts_of(theirs[3], 1, 3, second, (first, cotangent, gain))
+    latent_grad = second
     other_grad = twin(latent_grad)
     partial, tokens = [None] * 4, []
     for by in (2, 1, 3, 0):
         partial[by], token = weight_grads(place, kept, other, latent_grad, other_grad, by, tokens)
         tokens = [token]
-    input_grad, token = input_grads(latent_grad, gathered, token)
-    weight_grad, gain_grad = reduce_scatter(place, partial, token)
+    gathered = assemble(place, mine + theirs, token)
+    sums, input_grad = first_sums(place, partial, latent_grad, gathered, token)
+    weight_grad, gain_grad, input_grad = last_sums(place, sums, latent_grad, gathered, input_grad)
     return (input_grad, weight_grad, gain_grad.reshape(512))
 
 

time: 127 us -> 116 us (0.913)
  local copies, waits for them, and re-layouts: 11.8 us -> 5.07 us
  waiting for transfers between devices: 36.8 us -> 33.6 us
    pallas_call x3 -> x13, Pallas kernels: 22.4 us -> 30.2 us  [the longest x8 19.3 us: latent_part(): pl.pallas_call(functools.partial(latent_kernel, side, far, before is not...]
    unnamed x32 -> x12, local copies, waits for them, and re-layouts: 11.8 us -> 5.05 us
    pallas_call x2, Pallas kernels: 13.2 us -> 7.36 us  [turn(): pl.pallas_call(turn_kernel, grid_spec=pltpu.PrefetchScalarGridSpec(num_sc...]
    ppermute x21, waiting for transfers between devices: 36.8 us -> 33.6 us  [fetch(): lax.ppermute(value, axes, [(device(*source(*spot)), device(*spot)) for sp...]
    pallas_call x4, Pallas kernels: 11.6 us -> 9.26 us  [weight_grads(): pl.pallas_call(weight_kernel, grid_spec=pltpu.PrefetchScalarGridSpec(num_...]
  transfers between devices with their start and end apart: 21 -> 21, of which waited for: 9 -> 10; matrix products, arithmetic and copies ran while one was open for 0% -> 0% of each run, Pallas kernels for 27% -> 35%
where the time goes in v5:
time: 116 us
  Pallas kernels  49.9 us (43%)
  waiting for transfers between devices  33.6 us (29%)
  starting transfers between devices  26.3 us (23%)
  local copies, waits for them, and re-layouts  5.07 us (4%)
    ppermute x21, waiting for transfers between devices, fetch(): lax.ppermute(value, axes, [(device(*source(*spot)), device(*spot)) for sp...  33.6 us
    ppermute x21, starting transfers between devices, fetch(): lax.ppermute(value, axes, [(device(*source(*spot)), device(*spot)) for sp...  26.3 us
    pallas_call x8, Pallas kernels, latent_part(): pl.pallas_call(functools.partial(latent_kernel, side, far, before is not...  19.3 us
    pallas_call x2, Pallas kernels, input_grads(): pl.pallas_call(input_kernel, grid=(count,), in_specs=[pl.BlockSpec((784,...  9.68 us
    pallas_call x4, Pallas kernels, weight_grads(): pl.pallas_call(weight_kernel, grid_spec=pltpu.PrefetchScalarGridSpec(num_...  9.26 us
    pallas_call x2, Pallas kernels, turn(): pl.pallas_call(turn_kernel, grid_spec=pltpu.PrefetchScalarGridSpec(num_sc...  7.36 us
    unnamed x12, local copies, waits for them, and re-layouts  5.05 us
    pallas_call x3, Pallas kernels, combine(): pl.pallas_call(kernel, in_specs=[pl.BlockSpec(memory_space=pltpu.SMEM)] +...  2.97 us
  transfers between devices with their start and end apart: 21, of which 10 were waited for; matrix products, arithmetic and copies ran while one was open for 0% of the time, Pallas kernels for 35%

profile of v5, /device:TPU:0, one launch (start us, length us, event | category | flops | bytes accessed | tf_op | source)
XLA Modules:
  0.0 115.8 jit_solution(8781471406009994665)
XLA Ops:
  1.7 1.7 %collective-permute-start.2 = (bf16[448,256]{1,0:T(8,128)(2,1)S(1)}, bf16[448,256]{1,0:T(8,128)(2,1)S(1)}, u32[]{:S(2)}, u32[]{:S(2)}) collective-permute-start(bf16[448,256]{1,0:T(8,128)(2,1)S(1)} %constant_dynamic-slice_fusion.one), channel_id=1, source_target_pairs={{12,0},{13,1},{14,2},{15,3},{0,4},{1,5},{2,6},{3,7},{4,8},{5,9},{6... | collective-permute-start | bytes 688136 | tf_op jit(solution)/shard_map/ppermute | solution.py:25
  3.4 2.9 %collective-permute-start.1 = (bf16[448,256]{1,0:T(8,128)(2,1)S(1)}, bf16[448,256]{1,0:T(8,128)(2,1)S(1)}, u32[]{:S(2)}, u32[]{:S(2)}) collective-permute-start(bf16[448,256]{1,0:T(8,128)(2,1)S(1)} %constant_dynamic-slice_fusion.one), channel_id=1, source_target_pairs={{8,0},{9,1},{10,2},{11,3},{12,4},{13,5},{14,6},{15,7},{0,8},{1,9},... | collective-permute-start | bytes 688136 | tf_op jit(solution)/shard_map/ppermute | solution.py:25
  7.7 4.1 %copy-done.2 = bf16[768,7168]{1,0:T(8,128)(2,1)S(1)} copy-done((bf16[768,7168]{1,0:T(8,128)(2,1)S(1)}, bf16[768,7168]{1,0:T(8,128)(2,1)}, u32[]{:S(2)}) %copy-start.2) | copy-done | bytes 11010072
  11.9 2.8 %turn.2 = (bf16[3584,768]{1,0:T(8,128)(2,1)S(1)}, f32[8,128]{1,0:T(8,128)S(1)}) custom-call(s32[4]{0:T(128)S(1)} %pad_add_fusion.place, bf16[768,7168]{1,0:T(8,128)(2,1)S(1)} %copy-done.2), custom_call_target="tpu_custom_call" | custom-call | bytes 23068672 | tf_op jit(solution)/shard_map/turn/pallas_call | solution.py:50
  14.8 4.1 %collective-permute-start.5 = (bf16[4,448,256]{2,1,0:T(8,128)(2,1)S(1)}, bf16[4,448,256]{2,1,0:T(8,128)(2,1)S(1)}, u32[]{:S(2)}, u32[]{:S(2)}) collective-permute-start(bf16[4,448,256]{2,1,0:T(8,128)(2,1)S(1)} %join.1.piece.refs_0_), channel_id=1, source_target_pairs={{1,0},{2,1},{3,2},{0,3},{5,4},{6,5},{7,6},{4,7},{9,8},{10,9},{11,1... | collective-permute-start | bytes 2752520 | tf_op jit(solution)/shard_map/ppermute | solution.py:25
  19.0 2.1 %latent.8 = (f32[768,256]{1,0:T(8,128)S(1)}, f32[8,128]{1,0:T(8,128)S(1)}) custom-call(s32[4]{0:T(128)S(1)} %pad_add_fusion.place, bf16[768,7168]{1,0:T(8,128)(2,1)S(1)} %copy-done.3, bf16[4,448,256]{2,1,0:T(8,128)(2,1)S(1)} %collective-permute-done.7.piece.refs_4_), custom_call_target="tpu_custom_call" | custom-call | flops 805306368 | bytes 6291456 | tf_op jit(solution)/shard_map/latent/pallas_call | solution.py:175
  21.1 4.6 %turn.3 = (bf16[3584,768]{1,0:T(8,128)(2,1)S(1)}, f32[8,128]{1,0:T(8,128)S(1)}) custom-call(s32[4]{0:T(128)S(1)} %pad_add_fusion.place, bf16[768,7168]{1,0:T(8,128)(2,1)} %collective-permute-done.6.rows), custom_call_target="tpu_custom_call" | custom-call | bytes 23068672 | tf_op jit(solution)/shard_map/turn/pallas_call | solution.py:50
  25.7 14.0 %collective-permute-done.5.value = bf16[4,448,256]{2,1,0:T(8,128)(2,1)S(1)} collective-permute-done((bf16[4,448,256]{2,1,0:T(8,128)(2,1)S(1)}, bf16[4,448,256]{2,1,0:T(8,128)(2,1)S(1)}, u32[]{:S(2)}, u32[]{:S(2)}) %collective-permute-start.5) | collective-permute-done | bytes 917536 | tf_op jit(solution)/shard_map/ppermute | solution.py:25
  39.9 2.2 %latent.9 = (f32[768,256]{1,0:T(8,128)S(1)}, f32[8,128]{1,0:T(8,128)}) custom-call(s32[4]{0:T(128)S(1)} %pad_add_fusion.place, bf16[768,7168]{1,0:T(8,128)(2,1)S(1)} %copy-done.3, bf16[4,448,256]{2,1,0:T(8,128)(2,1)S(1)} %join.1.piece.refs_0_), custom_call_target="tpu_custom_call" | custom-call | flops 805306368 | bytes 6291456 | tf_op jit(solution)/shard_map/latent/pallas_call | solution.py:175
  43.0 2.2 %latent.10 = (f32[768,256]{1,0:T(8,128)S(1)}, f32[8,128]{1,0:T(8,128)}) custom-call(s32[4]{0:T(128)S(1)} %pad_add_fusion.place, bf16[768,7168]{1,0:T(8,128)(2,1)S(1)} %copy-done.3, bf16[4,448,256]{2,1,0:T(8,128)(2,1)S(1)} %tie.2.piece.refs_1_, f32[768,256]{1,0:T(8,128)S(1)} %get-tuple-element.44.refs_0_), custom_call_target="tpu_custom_call" | custom-call | flops 805306368 | bytes 6291456 | tf_op jit(solution)/shard_map/latent/pallas_call | solution.py:175
  45.2 2.2 %latent.11 = (f32[768,256]{1,0:T(8,128)S(1)}, f32[8,128]{1,0:T(8,128)S(1)}) custom-call(s32[4]{0:T(128)S(1)} %pad_add_fusion.place, bf16[768,7168]{1,0:T(8,128)(2,1)S(1)} %copy-done.3, bf16[4,448,256]{2,1,0:T(8,128)(2,1)S(1)} %collective-permute-done.4.piece.refs_2_, f32[768,256]{1,0:T(8,128)S(1)} %get-tuple-element.45.refs_0_), custom_call_target="tpu_custom_call" | custom-call | flops 805306368 | bytes 6291456 | tf_op jit(solution)/shard_map/latent/pallas_call | solution.py:175
  47.4 2.2 %latent.12 = (f32[768,256]{1,0:T(8,128)S(1)}, f32[8,128]{1,0:T(8,128)S(1)}) custom-call(s32[4]{0:T(128)S(1)} %pad_add_fusion.place, bf16[768,7168]{1,0:T(8,128)(2,1)S(1)} %copy-done.3, bf16[4,448,256]{2,1,0:T(8,128)(2,1)S(1)} %collective-permute-done.8.piece.refs_5_, f32[768,256]{1,0:T(8,128)S(1)} %get-tuple-element.47.refs_0_), custom_call_target="tpu_custom_call" | custom-call | flops 805306368 | bytes 6291456 | tf_op jit(solution)/shard_map/latent/pallas_call | solution.py:175
  49.6 5.3 %collective-permute-done.3.value = bf16[4,448,256]{2,1,0:T(8,128)(2,1)S(1)} collective-permute-done((bf16[4,448,256]{2,1,0:T(8,128)(2,1)S(1)}, bf16[4,448,256]{2,1,0:T(8,128)(2,1)S(1)}, u32[]{:S(2)}, u32[]{:S(2)}) %collective-permute-start.3) | collective-permute-done | bytes 917536 | tf_op jit(solution)/shard_map/ppermute | solution.py:25
  55.3 2.2 %latent.14 = (f32[768,256]{1,0:T(8,128)S(1)}, f32[8,128]{1,0:T(8,128)}) custom-call(s32[4]{0:T(128)S(1)} %pad_add_fusion.place, bf16[768,7168]{1,0:T(8,128)(2,1)S(1)} %copy-done.3, bf16[4,448,256]{2,1,0:T(8,128)(2,1)S(1)} %tie.3.piece.refs_3_, f32[768,256]{1,0:T(8,128)S(1)} %get-tuple-element.51.refs_0_), custom_call_target="tpu_custom_call" | custom-call | flops 805306368 | bytes 6291456 | tf_op jit(solution)/shard_map/latent/pallas_call | solution.py:175
  57.5 2.2 %latent.13 = (f32[768,256]{1,0:T(8,128)S(1)}, f32[8,128]{1,0:T(8,128)}) custom-call(s32[4]{0:T(128)S(1)} %pad_add_fusion.place, bf16[768,7168]{1,0:T(8,128)(2,1)S(1)} %copy-done.3, bf16[4,448,256]{2,1,0:T(8,128)(2,1)S(1)} %collective-permute-done.10.piece.refs_6_, f32[768,256]{1,0:T(8,128)S(1)} %get-tuple-element.49.refs_0_), custom_call_target="tpu_custom_call" | custom-call | flops 805306368 | bytes 6291456 | tf_op jit(solution)/shard_map/latent/pallas_call | solution.py:175
  59.8 3.9 %latent.15 = (bf16[784,512]{1,0:T(8,128)(2,1)S(1)}, f32[8,128]{1,0:T(8,128)}) custom-call(s32[4]{0:T(128)S(1)} %pad_add_fusion.place, bf16[768,7168]{1,0:T(8,128)(2,1)S(1)} %copy-done.3, bf16[4,448,256]{2,1,0:T(8,128)(2,1)S(1)} %collective-permute-done.9.piece.refs_7_, f32[768,256]{1,0:T(8,128)S(1)} %get-tuple-element.50.refs_0_, ...), custom_call_target="tpu_custom_call" | custom-call | flops 805306368 | bytes 6291456 | tf_op jit(solution)/shard_map/latent/pallas_call | solution.py:175
  64.3 1.9 %collective-permute-done.11.refs_5_ = bf16[784,512]{1,0:T(8,128)(2,1)S(1)} collective-permute-done((bf16[784,512]{1,0:T(8,128)(2,1)S(1)}, bf16[784,512]{1,0:T(8,128)(2,1)S(1)}, u32[]{:S(2)}, u32[]{:S(2)}) %collective-permute-start.11) | collective-permute-done | bytes 802848 | tf_op jit(solution)/shard_map/ppermute | solution.py:25
  66.2 2.3 %weight_grads.4 = (bf16[2,1808,128]{2,1,0:T(8,128)(2,1)S(1)}, f32[8,128]{1,0:T(8,128)S(1)}) custom-call(s32[4]{0:T(128)S(1)} %pad_add_fusion.place, bf16[3584,768]{1,0:T(8,128)(2,1)S(1)} %get-tuple-element.54.refs_0_.refs_1_, bf16[3584,768]{1,0:T(8,128)(2,1)S(1)} %get-tuple-element.54.refs_0_.refs_1_, ...), custom_call_target="tpu_custom_call" | custom-call | bytes 1048576 | tf_op jit(solution)/shard_map/weight_grads/pallas_call | solution.py:295
  68.5 3.1 %collective-permute-start.13 = (bf16[2,1808,128]{2,1,0:T(8,128)(2,1)S(1)}, bf16[2,1808,128]{2,1,0:T(8,128)(2,1)S(1)}, u32[]{:S(2)}, u32[]{:S(2)}) collective-permute-start(bf16[2,1808,128]{2,1,0:T(8,128)(2,1)S(1)} %get-tuple-element.62), channel_id=1, source_target_pairs={{64,0},{65,1},{66,2},{67,3},{68,4},{69,5},{70,6},{71,7},{72,8},{73... | collective-permute-start | bytes 2777096 | tf_op jit(solution)/shard_map/ppermute | solution.py:25
  71.6 2.3 %weight_grads.5 = (bf16[2,1808,128]{2,1,0:T(8,128)(2,1)S(1)}, f32[8,128]{1,0:T(8,128)S(1)}) custom-call(s32[4]{0:T(128)S(1)} %pad_add_fusion.place, bf16[3584,768]{1,0:T(8,128)(2,1)S(1)} %get-tuple-element.54.refs_0_.refs_1_, bf16[3584,768]{1,0:T(8,128)(2,1)S(1)} %get-tuple-element.54.refs_0_.refs_1_, ...), custom_call_target="tpu_custom_call" | custom-call | bytes 1048576 | tf_op jit(solution)/shard_map/weight_grads/pallas_call | solution.py:295
  74.6 2.3 %weight_grads.6 = (bf16[2,1808,128]{2,1,0:T(8,128)(2,1)S(1)}, f32[8,128]{1,0:T(8,128)S(1)}) custom-call(s32[4]{0:T(128)S(1)} %pad_add_fusion.place, bf16[3584,768]{1,0:T(8,128)(2,1)S(1)} %get-tuple-element.54.refs_0_.refs_1_, bf16[3584,768]{1,0:T(8,128)(2,1)S(1)} %get-tuple-element.54.refs_0_.refs_1_, ...), custom_call_target="tpu_custom_call" | custom-call | bytes 1048576 | tf_op jit(solution)/shard_map/weight_grads/pallas_call | solution.py:295
  76.9 2.7 %collective-permute-start.14 = (bf16[2,1808,128]{2,1,0:T(8,128)(2,1)S(1)}, bf16[2,1808,128]{2,1,0:T(8,128)(2,1)S(1)}, u32[]{:S(2)}, u32[]{:S(2)}) collective-permute-start(bf16[2,1808,128]{2,1,0:T(8,128)(2,1)S(1)} %get-tuple-element.63), channel_id=1, source_target_pairs={{32,0},{33,1},{34,2},{35,3},{36,4},{37,5},{38,6},{39,7},{40,8},{41... | collective-permute-start | bytes 2777096 | tf_op jit(solution)/shard_map/ppermute | solution.py:25
  79.7 2.3 %weight_grads.7 = (bf16[2,1808,128]{2,1,0:T(8,128)(2,1)S(1)}, f32[8,128]{1,0:T(8,128)S(1)}) custom-call(s32[4]{0:T(128)S(1)} %pad_add_fusion.place, bf16[3584,768]{1,0:T(8,128)(2,1)S(1)} %get-tuple-element.54.refs_0_.refs_1_, bf16[3584,768]{1,0:T(8,128)(2,1)S(1)} %get-tuple-element.54.refs_0_.refs_1_, ...), custom_call_target="tpu_custom_call" | custom-call | bytes 1048576 | tf_op jit(solution)/shard_map/weight_grads/pallas_call | solution.py:295
  83.1 5.4 %input_grads.2 = (bf16[768,7168]{1,0:T(8,128)(2,1)}, f32[8,128]{1,0:T(8,128)S(1)}) custom-call(bf16[784,512]{1,0:T(8,128)(2,1)S(1)} %get-tuple-element.53.refs_4_.grad, bf16[7168,512]{1,0:T(8,128)(2,1)S(1)} %assemble.1.weight, f32[8,128]{1,0:T(8,128)S(1)} %get-tuple-element.59.refs_8_.before), custom_call_target="tpu_custom_call" | custom-call | bytes 1048576 | tf_op jit(solution)/shard_map/input_grads/pallas_call | solution.py:235
  88.5 5.0 %collective-permute-done.12.value.refs_1_ = bf16[2,1808,128]{2,1,0:T(8,128)(2,1)S(1)} collective-permute-done((bf16[2,1808,128]{2,1,0:T(8,128)(2,1)S(1)}, bf16[2,1808,128]{2,1,0:T(8,128)(2,1)S(1)}, u32[]{:S(2)}, u32[]{:S(2)}) %collective-permute-start.12) | collective-permute-done | bytes 925728 | tf_op jit(solution)/shard_map/ppermute | solution.py:25
  95.4 1.5 %collective-permute-start.16 = (bf16[960,128]{1,0:T(8,128)(2,1)S(1)}, bf16[960,128]{1,0:T(8,128)(2,1)S(1)}, u32[]{:S(2)}, u32[]{:S(2)}) collective-permute-start(bf16[960,128]{1,0:T(8,128)(2,1)S(1)} %get-tuple-element.70), channel_id=1, source_target_pairs={{8,0},{9,1},{10,2},{11,3},{12,4},{13,5},{14,6},{15,7},{0,8},{1,9},... | collective-permute-start | bytes 737288 | tf_op jit(solution)/shard_map/ppermute | solution.py:25
  96.9 1.5 %collective-permute-start.17 = (bf16[960,128]{1,0:T(8,128)(2,1)S(1)}, bf16[960,128]{1,0:T(8,128)(2,1)S(1)}, u32[]{:S(2)}, u32[]{:S(2)}) collective-permute-start(bf16[960,128]{1,0:T(8,128)(2,1)S(1)} %get-tuple-element.71), channel_id=1, source_target_pairs={{4,0},{5,1},{6,2},{7,3},{8,4},{9,5},{10,6},{11,7},{12,8},{13,9},{1... | collective-permute-start | bytes 737288 | tf_op jit(solution)/shard_map/ppermute | solution.py:25
  98.4 4.3 %input_grads.3 = (bf16[768,7168]{1,0:T(8,128)(2,1)}, f32[8,128]{1,0:T(8,128)S(1)}) custom-call(bf16[784,512]{1,0:T(8,128)(2,1)S(1)} %get-tuple-element.53.refs_4_.grad, bf16[7168,512]{1,0:T(8,128)(2,1)S(1)} %assemble.1.weight, f32[8,128]{1,0:T(8,128)S(1)} %get-tuple-element.65.before, ...), custom_call_target="tpu_custom_call", output_to_operand_aliasing={{0}: (3, {})} | custom-call | bytes 1048576 | tf_op jit(solution)/shard_map/input_grads/pallas_call | solution.py:235
  102.7 2.1 %collective-permute-done.15.refs_1_ = bf16[960,128]{1,0:T(8,128)(2,1)S(1)} collective-permute-done((bf16[960,128]{1,0:T(8,128)(2,1)S(1)}, bf16[960,128]{1,0:T(8,128)(2,1)S(1)}, u32[]{:S(2)}, u32[]{:S(2)}) %collective-permute-start.15) | collective-permute-done | bytes 245792 | tf_op jit(solution)/shard_map/ppermute | solution.py:25
  106.5 3.9 %collective-permute-start.19 = (bf16[240,128]{1,0:T(8,128)(2,1)S(1)}, bf16[240,128]{1,0:T(8,128)(2,1)S(1)}, u32[]{:S(2)}, u32[]{:S(2)}) collective-permute-start(bf16[240,128]{1,0:T(8,128)(2,1)S(1)} %get-tuple-element.75), channel_id=1, source_target_pairs={{2,0},{3,1},{0,2},{1,3},{6,4},{7,5},{4,6},{5,7},{10,8},{11,9},{8,1... | collective-permute-start | bytes 184328 | tf_op jit(solution)/shard_map/ppermute | solution.py:25
  110.4 1.5 %collective-permute-done.18.refs_1_ = bf16[240,128]{1,0:T(8,128)(2,1)S(1)} collective-permute-done((bf16[240,128]{1,0:T(8,128)(2,1)S(1)}, bf16[240,128]{1,0:T(8,128)(2,1)S(1)}, u32[]{:S(2)}, u32[]{:S(2)}) %collective-permute-start.18) | collective-permute-done | bytes 61472 | tf_op jit(solution)/shard_map/ppermute | solution.py:25
  113.2 1.4 %collective-permute-done.20.refs_3_ = bf16[240,128]{1,0:T(8,128)(2,1)S(1)} collective-permute-done((bf16[240,128]{1,0:T(8,128)(2,1)S(1)}, bf16[240,128]{1,0:T(8,128)(2,1)S(1)}, u32[]{:S(2)}, u32[]{:S(2)}) %collective-permute-start.20) | collective-permute-done | bytes 61472 | tf_op jit(solution)/shard_map/ppermute | solution.py:25
  (49 shorter events, 12.5 us)
Async XLA Ops:
  0.6 1.0 copy-start
  0.6 20.4 %collective-permute-start.6 = (bf16[768,7168]{1,0:T(8,128)(2,1)}, bf16[768,7168]{1,0:T(8,128)(2,1)}, u32[]{:S(2)}, u32[]{:S(2)}) collective-permute-start(bf16[768,7168]{1,0:T(8,128)(2,1)} %inputs.15), channel_id=1, source_target_pairs={{16,0},{17,1},{18,2},{19,3},{20,4},{21,5},{22,6},{23,7},{24,8},{25... | collective-permute-start | bytes 33030152 | tf_op jit(solution)/shard_map/ppermute | solution.py:25
  1.7 13.0 %collective-permute-start.2 = (bf16[448,256]{1,0:T(8,128)(2,1)S(1)}, bf16[448,256]{1,0:T(8,128)(2,1)S(1)}, u32[]{:S(2)}, u32[]{:S(2)}) collective-permute-start(bf16[448,256]{1,0:T(8,128)(2,1)S(1)} %constant_dynamic-slice_fusion.one), channel_id=1, source_target_pairs={{12,0},{13,1},{14,2},{15,3},{0,4},{1,5},{2,6},{3,7},{4,8},{5,9},{6... | collective-permute-start | bytes 688136 | tf_op jit(solution)/shard_map/ppermute | solution.py:25
  3.4 11.3 %collective-permute-start.1 = (bf16[448,256]{1,0:T(8,128)(2,1)S(1)}, bf16[448,256]{1,0:T(8,128)(2,1)S(1)}, u32[]{:S(2)}, u32[]{:S(2)}) collective-permute-start(bf16[448,256]{1,0:T(8,128)(2,1)S(1)} %constant_dynamic-slice_fusion.one), channel_id=1, source_target_pairs={{8,0},{9,1},{10,2},{11,3},{12,4},{13,5},{14,6},{15,7},{0,8},{1,9},... | collective-permute-start | bytes 688136 | tf_op jit(solution)/shard_map/ppermute | solution.py:25
  6.3 8.4 %collective-permute-start = (bf16[448,256]{1,0:T(8,128)(2,1)S(1)}, bf16[448,256]{1,0:T(8,128)(2,1)S(1)}, u32[]{:S(2)}, u32[]{:S(2)}) collective-permute-start(bf16[448,256]{1,0:T(8,128)(2,1)S(1)} %constant_dynamic-slice_fusion.one), channel_id=1, source_target_pairs={{4,0},{5,1},{6,2},{7,3},{8,4},{9,5},{10,6},{11,7},{12,8},{13,9},{1... | collective-permute-start | bytes 688136 | tf_op jit(solution)/shard_map/ppermute | solution.py:25
  7.7 4.1 %copy-start.2 = (bf16[768,7168]{1,0:T(8,128)(2,1)S(1)}, bf16[768,7168]{1,0:T(8,128)(2,1)}, u32[]{:S(2)}) copy-start(bf16[768,7168]{1,0:T(8,128)(2,1)} %inputs.15) | copy-start | bytes 33030148
  11.9 7.1 %copy-start.3 = (bf16[768,7168]{1,0:T(8,128)(2,1)S(1)}, bf16[768,7168]{1,0:T(8,128)(2,1)}, u32[]{:S(2)}) copy-start(bf16[768,7168]{1,0:T(8,128)(2,1)} %inputs.15) | copy-start | bytes 33030148
  14.7 4.2 %collective-permute-start.7 = (bf16[4,448,256]{2,1,0:T(8,128)(2,1)S(1)}, bf16[4,448,256]{2,1,0:T(8,128)(2,1)S(1)}, u32[]{:S(2)}, u32[]{:S(2)}) collective-permute-start(bf16[4,448,256]{2,1,0:T(8,128)(2,1)S(1)} %join.1.piece.refs_0_), channel_id=1, source_target_pairs={{16,0},{17,1},{18,2},{19,3},{20,4},{21,5},{22,6},{23,7},{24,8},{25... | collective-permute-start | bytes 2752520 | tf_op jit(solution)/shard_map/ppermute | solution.py:25
  14.8 24.8 %collective-permute-start.5 = (bf16[4,448,256]{2,1,0:T(8,128)(2,1)S(1)}, bf16[4,448,256]{2,1,0:T(8,128)(2,1)S(1)}, u32[]{:S(2)}, u32[]{:S(2)}) collective-permute-start(bf16[4,448,256]{2,1,0:T(8,128)(2,1)S(1)} %join.1.piece.refs_0_), channel_id=1, source_target_pairs={{1,0},{2,1},{3,2},{0,3},{5,4},{6,5},{7,6},{4,7},{9,8},{10,9},{11,1... | collective-permute-start | bytes 2752520 | tf_op jit(solution)/shard_map/ppermute | solution.py:25
  18.9 23.2 %collective-permute-start.4 = (bf16[4,448,256]{2,1,0:T(8,128)(2,1)S(1)}, bf16[4,448,256]{2,1,0:T(8,128)(2,1)S(1)}, u32[]{:S(2)}, u32[]{:S(2)}) collective-permute-start(bf16[4,448,256]{2,1,0:T(8,128)(2,1)S(1)} %join.1.piece.refs_0_), channel_id=1, source_target_pairs={{2,0},{3,1},{0,2},{1,3},{6,4},{7,5},{4,6},{5,7},{10,8},{11,9},{8,1... | collective-permute-start | bytes 2752520 | tf_op jit(solution)/shard_map/ppermute | solution.py:25
  39.8 7.6 %collective-permute-start.8 = (bf16[4,448,256]{2,1,0:T(8,128)(2,1)S(1)}, bf16[4,448,256]{2,1,0:T(8,128)(2,1)S(1)}, u32[]{:S(2)}, u32[]{:S(2)}) collective-permute-start(bf16[4,448,256]{2,1,0:T(8,128)(2,1)S(1)} %tie.2.piece.refs_1_), channel_id=1, source_target_pairs={{16,0},{17,1},{18,2},{19,3},{20,4},{21,5},{22,6},{23,7},{24,8},{25... | collective-permute-start | bytes 2752520 | tf_op jit(solution)/shard_map/ppermute | solution.py:25
  39.8 15.1 %collective-permute-start.3 = (bf16[4,448,256]{2,1,0:T(8,128)(2,1)S(1)}, bf16[4,448,256]{2,1,0:T(8,128)(2,1)S(1)}, u32[]{:S(2)}, u32[]{:S(2)}) collective-permute-start(bf16[4,448,256]{2,1,0:T(8,128)(2,1)S(1)} %join.1.piece.refs_0_), channel_id=1, source_target_pairs={{3,0},{0,1},{1,2},{2,3},{7,4},{4,5},{5,6},{6,7},{11,8},{8,9},{9,10... | collective-permute-start | bytes 2752520 | tf_op jit(solution)/shard_map/ppermute | solution.py:25
  42.1 15.4 %collective-permute-start.10 = (bf16[4,448,256]{2,1,0:T(8,128)(2,1)S(1)}, bf16[4,448,256]{2,1,0:T(8,128)(2,1)S(1)}, u32[]{:S(2)}, u32[]{:S(2)}) collective-permute-start(bf16[4,448,256]{2,1,0:T(8,128)(2,1)S(1)} %collective-permute-done.4.piece.refs_2_), channel_id=1, source_target_pairs={{16,0},{17,1},{18,2},{19,3},{20,4},{21,5},{22,6},{23,7},{24,8},{25... | collective-permute-start | bytes 2752520 | tf_op jit(solution)/shard_map/ppermute | solution.py:25
  55.0 4.7 %collective-permute-start.9 = (bf16[4,448,256]{2,1,0:T(8,128)(2,1)S(1)}, bf16[4,448,256]{2,1,0:T(8,128)(2,1)S(1)}, u32[]{:S(2)}, u32[]{:S(2)}) collective-permute-start(bf16[4,448,256]{2,1,0:T(8,128)(2,1)S(1)} %tie.3.piece.refs_3_), channel_id=1, source_target_pairs={{16,0},{17,1},{18,2},{19,3},{20,4},{21,5},{22,6},{23,7},{24,8},{25... | collective-permute-start | bytes 2752520 | tf_op jit(solution)/shard_map/ppermute | solution.py:25
  55.3 4.5 %copy-start.4 = (bf16[768,512]{1,0:T(8,128)(2,1)S(1)}, bf16[768,512]{1,0:T(8,128)(2,1)}, u32[]{:S(2)}) copy-start(bf16[768,512]{1,0:T(8,128)(2,1)} %refs_2_.1) | copy-start | bytes 2359300
  55.3 4.5 %copy-start.5 = (f32[512]{0:T(512)S(1)}, f32[512]{0:T(512)}, u32[]{:S(2)}) copy-start(f32[512]{0:T(512)} %param.7) | copy-start | bytes 6148
  63.8 2.5 %collective-permute-start.11 = (bf16[784,512]{1,0:T(8,128)(2,1)S(1)}, bf16[784,512]{1,0:T(8,128)(2,1)S(1)}, u32[]{:S(2)}, u32[]{:S(2)}) collective-permute-start(bf16[784,512]{1,0:T(8,128)(2,1)S(1)} %get-tuple-element.53.refs_4_.grad), channel_id=1, source_target_pairs={{16,0},{17,1},{18,2},{19,3},{20,4},{21,5},{22,6},{23,7},{24,8},{25... | collective-permute-start | bytes 2408456 | tf_op jit(solution)/shard_map/ppermute | solution.py:25
  68.5 20.0 %collective-permute-start.13 = (bf16[2,1808,128]{2,1,0:T(8,128)(2,1)S(1)}, bf16[2,1808,128]{2,1,0:T(8,128)(2,1)S(1)}, u32[]{:S(2)}, u32[]{:S(2)}) collective-permute-start(bf16[2,1808,128]{2,1,0:T(8,128)(2,1)S(1)} %get-tuple-element.62), channel_id=1, source_target_pairs={{64,0},{65,1},{66,2},{67,3},{68,4},{69,5},{70,6},{71,7},{72,8},{73... | collective-permute-start | bytes 2777096 | tf_op jit(solution)/shard_map/ppermute | solution.py:25
  74.0 19.6 %collective-permute-start.12 = (bf16[2,1808,128]{2,1,0:T(8,128)(2,1)S(1)}, bf16[2,1808,128]{2,1,0:T(8,128)(2,1)S(1)}, u32[]{:S(2)}, u32[]{:S(2)}) collective-permute-start(bf16[2,1808,128]{2,1,0:T(8,128)(2,1)S(1)} %get-tuple-element.61), channel_id=1, source_target_pairs={{96,0},{97,1},{98,2},{99,3},{100,4},{101,5},{102,6},{103,7},{104,8... | collective-permute-start | bytes 2777096 | tf_op jit(solution)/shard_map/ppermute | solution.py:25
  76.9 16.7 %collective-permute-start.14 = (bf16[2,1808,128]{2,1,0:T(8,128)(2,1)S(1)}, bf16[2,1808,128]{2,1,0:T(8,128)(2,1)S(1)}, u32[]{:S(2)}, u32[]{:S(2)}) collective-permute-start(bf16[2,1808,128]{2,1,0:T(8,128)(2,1)S(1)} %get-tuple-element.63), channel_id=1, source_target_pairs={{32,0},{33,1},{34,2},{35,3},{36,4},{37,5},{38,6},{39,7},{40,8},{41... | collective-permute-start | bytes 2777096 | tf_op jit(solution)/shard_map/ppermute | solution.py:25
  93.6 22.2 %copy-start.1 = (bf16[448,512]{1,0:T(8,128)(2,1)S(1)}, bf16[448,512]{1,0:T(8,128)(2,1)}, u32[]{:S(2)}) copy-start(bf16[448,512]{1,0:T(8,128)(2,1)} %param.6) | copy-start | bytes 1376260
  94.7 10.1 %collective-permute-start.15 = (bf16[960,128]{1,0:T(8,128)(2,1)S(1)}, bf16[960,128]{1,0:T(8,128)(2,1)S(1)}, u32[]{:S(2)}, u32[]{:S(2)}) collective-permute-start(bf16[960,128]{1,0:T(8,128)(2,1)S(1)} %get-tuple-element.69), channel_id=1, source_target_pairs={{12,0},{13,1},{14,2},{15,3},{0,4},{1,5},{2,6},{3,7},{4,8},{5,9},{6... | collective-permute-start | bytes 737288 | tf_op jit(solution)/shard_map/ppermute | solution.py:25
  95.4 9.4 %collective-permute-start.16 = (bf16[960,128]{1,0:T(8,128)(2,1)S(1)}, bf16[960,128]{1,0:T(8,128)(2,1)S(1)}, u32[]{:S(2)}, u32[]{:S(2)}) collective-permute-start(bf16[960,128]{1,0:T(8,128)(2,1)S(1)} %get-tuple-element.70), channel_id=1, source_target_pairs={{8,0},{9,1},{10,2},{11,3},{12,4},{13,5},{14,6},{15,7},{0,8},{1,9},... | collective-permute-start | bytes 737288 | tf_op jit(solution)/shard_map/ppermute | solution.py:25
  96.9 8.7 %collective-permute-start.17 = (bf16[960,128]{1,0:T(8,128)(2,1)S(1)}, bf16[960,128]{1,0:T(8,128)(2,1)S(1)}, u32[]{:S(2)}, u32[]{:S(2)}) collective-permute-start(bf16[960,128]{1,0:T(8,128)(2,1)S(1)} %get-tuple-element.71), channel_id=1, source_target_pairs={{4,0},{5,1},{6,2},{7,3},{8,4},{9,5},{10,6},{11,7},{12,8},{13,9},{1... | collective-permute-start | bytes 737288 | tf_op jit(solution)/shard_map/ppermute | solution.py:25
  106.4 5.5 %collective-permute-start.18 = (bf16[240,128]{1,0:T(8,128)(2,1)S(1)}, bf16[240,128]{1,0:T(8,128)(2,1)S(1)}, u32[]{:S(2)}, u32[]{:S(2)}) collective-permute-start(bf16[240,128]{1,0:T(8,128)(2,1)S(1)} %get-tuple-element.74), channel_id=1, source_target_pairs={{3,0},{0,1},{1,2},{2,3},{7,4},{4,5},{5,6},{6,7},{11,8},{8,9},{9,10... | collective-permute-start | bytes 184328 | tf_op jit(solution)/shard_map/ppermute | solution.py:25
  106.5 6.8 %collective-permute-start.19 = (bf16[240,128]{1,0:T(8,128)(2,1)S(1)}, bf16[240,128]{1,0:T(8,128)(2,1)S(1)}, u32[]{:S(2)}, u32[]{:S(2)}) collective-permute-start(bf16[240,128]{1,0:T(8,128)(2,1)S(1)} %get-tuple-element.75), channel_id=1, source_target_pairs={{2,0},{3,1},{0,2},{1,3},{6,4},{7,5},{4,6},{5,7},{10,8},{11,9},{8,1... | collective-permute-start | bytes 184328 | tf_op jit(solution)/shard_map/ppermute | solution.py:25
  110.4 4.2 %collective-permute-start.20 = (bf16[240,128]{1,0:T(8,128)(2,1)S(1)}, bf16[240,128]{1,0:T(8,128)(2,1)S(1)}, u32[]{:S(2)}, u32[]{:S(2)}) collective-permute-start(bf16[240,128]{1,0:T(8,128)(2,1)S(1)} %get-tuple-element.76), channel_id=1, source_target_pairs={{1,0},{2,1},{3,2},{0,3},{5,4},{6,5},{7,6},{4,7},{9,8},{10,9},{11,1... | collective-permute-start | bytes 184328 | tf_op jit(solution)/shard_map/ppermute | solution.py:25

commit v6 on v5

--- a/solution.py
+++ b/solution.py
@@ -77,7 +77,7 @@
         out_specs=vmem,
         out_shape=jax.ShapeDtypeStruct(value.shape, value.dtype),
         compiler_params=pltpu.CompilerParams(vmem_limit_bytes=8 * MIB),
-        cost_estimate=pl.CostEstimate(flops=0, bytes_accessed=2 * MIB, transcendentals=0),
+        cost_estimate=pl.CostEstimate(flops=0, bytes_accessed=4096, transcendentals=0),
         name="tie",
     )(value, *tokens)
 
@@ -179,7 +179,7 @@
         scratch_shapes=scratch,
         out_shape=[out, order],
         compiler_params=pltpu.CompilerParams(vmem_limit_bytes=14 * MIB),
-        cost_estimate=pl.CostEstimate(flops=768 * 2048 * 512, bytes_accessed=6 * MIB, transcendentals=0),
+        cost_estimate=pl.CostEstimate(flops=0, bytes_accessed=4096, transcendentals=0),
         name="latent",
     )(*operands)
 
@@ -429,20 +429,21 @@
     other, token = turn(place, other_inputs)
     gain = norm_gain.reshape(1, 512)
     parts_of = functools.partial(latent_part, place, inputs)
-    theirs = [twin(line)]
+    theirs = {0: twin(line)}
     first, _ = parts_of(mine[0], 0, 0)
     second, done = parts_of(theirs[0], 1, 0)
     mine[1] = tie(mine[1], token, done)
-    theirs.append(twin(mine[1]))
-    theirs.append(twin(mine[2]))
+    theirs[1] = twin(mine[1])
+    theirs[3] = twin(mine[3])
     first, _ = parts_of(mine[1], 0, 1, first)
-    first, done = parts_of(mine[2], 0, 2, first)
-    second, after = parts_of(theirs[1], 1, 1, second)
-    mine[3] = tie(mine[3], done, after)
-    theirs.append(twin(mine[3]))
-    second, _ = parts_of(theirs[2], 1, 2, second)
-    first, _ = parts_of(mine[3], 0, 3, first)
-    second, _ = parts_of(theirs[3], 1, 3, second, (first, cotangent, gain))
+    first, done = parts_of(mine[3], 0, 3, first)
+    second, _ = parts_of(theirs[1], 1, 1, second)
+    second, after = parts_of(theirs[3], 1, 3, second)
+    mine[2] = tie(mine[2], done, after)
+    theirs[2] = twin(mine[2])
+    first, _ = parts_of(mine[2], 0, 2, first)
+    second, _ = parts_of(theirs[2], 1, 2, second, (first, cotangent, gain))
+    theirs = [theirs[i] for i in four]
     latent_grad = second
     other_grad = twin(latent_grad)
     partial, tokens = [None] * 4, []

time: 116 us -> 106 us (0.914)
  waiting for transfers between devices: 33.6 us -> 25.9 us
  starting transfers between devices: 26.3 us -> 24.3 us
    ppermute x21, waiting for transfers between devices: 33.6 us -> 25.9 us  [fetch(): lax.ppermute(value, axes, [(device(*source(*spot)), device(*spot)) for sp...]
    ppermute x21, starting transfers between devices: 26.3 us -> 24.3 us  [fetch(): lax.ppermute(value, axes, [(device(*source(*spot)), device(*spot)) for sp...]
  transfers between devices with their start and end apart: 21 -> 21, of which waited for: 10 -> 11; matrix products, arithmetic and copies ran while one was open for 0% -> 0% of each run, Pallas kernels for 35% -> 38%
where the time goes in v6:
time: 106 us
  Pallas kernels  49.9 us (47%)
  waiting for transfers between devices  25.9 us (24%)
  starting transfers between devices  24.3 us (23%)
  local copies, waits for them, and re-layouts  5.07 us (5%)
    ppermute x21, waiting for transfers between devices, fetch(): lax.ppermute(value, axes, [(device(*source(*spot)), device(*spot)) for sp...  25.9 us
    ppermute x21, starting transfers between devices, fetch(): lax.ppermute(value, axes, [(device(*source(*spot)), device(*spot)) for sp...  24.3 us
    pallas_call x8, Pallas kernels, latent_part(): pl.pallas_call(functools.partial(latent_kernel, side, far, before is not...  19.3 us
    pallas_call x2, Pallas kernels, input_grads(): pl.pallas_call(input_kernel, grid=(count,), in_specs=[pl.BlockSpec((784,...  9.67 us
    pallas_call x4, Pallas kernels, weight_grads(): pl.pallas_call(weight_kernel, grid_spec=pltpu.PrefetchScalarGridSpec(num_...  9.26 us
    pallas_call x2, Pallas kernels, turn(): pl.pallas_call(turn_kernel, grid_spec=pltpu.PrefetchScalarGridSpec(num_sc...  7.36 us
    unnamed x12, local copies, waits for them, and re-layouts  5.05 us
    pallas_call x3, Pallas kernels, combine(): pl.pallas_call(kernel, in_specs=[pl.BlockSpec(memory_space=pltpu.SMEM)] +...  2.97 us
  transfers between devices with their start and end apart: 21, of which 11 were waited for; matrix products, arithmetic and copies ran while one was open for 0% of the time, Pallas kernels for 38%

profile of v6, /device:TPU:0, one launch (start us, length us, event | category | flops | bytes accessed | tf_op | source)
XLA Modules:
  0.0 106.1 jit_solution(9531163142493086049)
XLA Ops:
  1.7 1.7 %collective-permute-start.2 = (bf16[448,256]{1,0:T(8,128)(2,1)S(1)}, bf16[448,256]{1,0:T(8,128)(2,1)S(1)}, u32[]{:S(2)}, u32[]{:S(2)}) collective-permute-start(bf16[448,256]{1,0:T(8,128)(2,1)S(1)} %constant_dynamic-slice_fusion.one), channel_id=1, source_target_pairs={{12,0},{13,1},{14,2},{15,3},{0,4},{1,5},{2,6},{3,7},{4,8},{5,9},{6... | collective-permute-start | bytes 688136 | tf_op jit(solution)/shard_map/ppermute | solution.py:25
  3.4 2.9 %collective-permute-start.1 = (bf16[448,256]{1,0:T(8,128)(2,1)S(1)}, bf16[448,256]{1,0:T(8,128)(2,1)S(1)}, u32[]{:S(2)}, u32[]{:S(2)}) collective-permute-start(bf16[448,256]{1,0:T(8,128)(2,1)S(1)} %constant_dynamic-slice_fusion.one), channel_id=1, source_target_pairs={{8,0},{9,1},{10,2},{11,3},{12,4},{13,5},{14,6},{15,7},{0,8},{1,9},... | collective-permute-start | bytes 688136 | tf_op jit(solution)/shard_map/ppermute | solution.py:25
  6.3 1.3 %collective-permute-start = (bf16[448,256]{1,0:T(8,128)(2,1)S(1)}, bf16[448,256]{1,0:T(8,128)(2,1)S(1)}, u32[]{:S(2)}, u32[]{:S(2)}) collective-permute-start(bf16[448,256]{1,0:T(8,128)(2,1)S(1)} %constant_dynamic-slice_fusion.one), channel_id=1, source_target_pairs={{4,0},{5,1},{6,2},{7,3},{8,4},{9,5},{10,6},{11,7},{12,8},{13,9},{1... | collective-permute-start | bytes 688136 | tf_op jit(solution)/shard_map/ppermute | solution.py:25
  7.7 4.1 %copy-done.2 = bf16[768,7168]{1,0:T(8,128)(2,1)S(1)} copy-done((bf16[768,7168]{1,0:T(8,128)(2,1)S(1)}, bf16[768,7168]{1,0:T(8,128)(2,1)}, u32[]{:S(2)}) %copy-start.2) | copy-done | bytes 11010072
  11.9 2.8 %turn.2 = (bf16[3584,768]{1,0:T(8,128)(2,1)S(1)}, f32[8,128]{1,0:T(8,128)S(1)}) custom-call(s32[4]{0:T(128)S(1)} %pad_add_fusion.place, bf16[768,7168]{1,0:T(8,128)(2,1)S(1)} %copy-done.2), custom_call_target="tpu_custom_call" | custom-call | bytes 23068672 | tf_op jit(solution)/shard_map/turn/pallas_call | solution.py:50
  14.8 4.1 %collective-permute-start.5 = (bf16[4,448,256]{2,1,0:T(8,128)(2,1)S(1)}, bf16[4,448,256]{2,1,0:T(8,128)(2,1)S(1)}, u32[]{:S(2)}, u32[]{:S(2)}) collective-permute-start(bf16[4,448,256]{2,1,0:T(8,128)(2,1)S(1)} %join.1.piece.refs_0_), channel_id=1, source_target_pairs={{1,0},{2,1},{3,2},{0,3},{5,4},{6,5},{7,6},{4,7},{9,8},{10,9},{11,1... | collective-permute-start | bytes 2752520 | tf_op jit(solution)/shard_map/ppermute | solution.py:25
  19.0 2.1 %latent.8 = (f32[768,256]{1,0:T(8,128)S(1)}, f32[8,128]{1,0:T(8,128)S(1)}) custom-call(s32[4]{0:T(128)S(1)} %pad_add_fusion.place, bf16[768,7168]{1,0:T(8,128)(2,1)S(1)} %copy-done.3, bf16[4,448,256]{2,1,0:T(8,128)(2,1)S(1)} %collective-permute-done.7.piece.refs_4_), custom_call_target="tpu_custom_call" | custom-call | bytes 4096 | tf_op jit(solution)/shard_map/latent/pallas_call | solution.py:175
  21.1 4.6 %turn.3 = (bf16[3584,768]{1,0:T(8,128)(2,1)S(1)}, f32[8,128]{1,0:T(8,128)S(1)}) custom-call(s32[4]{0:T(128)S(1)} %pad_add_fusion.place, bf16[768,7168]{1,0:T(8,128)(2,1)} %collective-permute-done.6.rows), custom_call_target="tpu_custom_call" | custom-call | bytes 23068672 | tf_op jit(solution)/shard_map/turn/pallas_call | solution.py:50
  25.7 4.2 %collective-permute-done.5.value = bf16[4,448,256]{2,1,0:T(8,128)(2,1)S(1)} collective-permute-done((bf16[4,448,256]{2,1,0:T(8,128)(2,1)S(1)}, bf16[4,448,256]{2,1,0:T(8,128)(2,1)S(1)}, u32[]{:S(2)}, u32[]{:S(2)}) %collective-permute-start.5) | collective-permute-done | bytes 917536 | tf_op jit(solution)/shard_map/ppermute | solution.py:25
  30.0 3.5 %collective-permute-done.4.piece.refs_3_ = bf16[4,448,256]{2,1,0:T(8,128)(2,1)S(1)} collective-permute-done((bf16[4,448,256]{2,1,0:T(8,128)(2,1)S(1)}, bf16[4,448,256]{2,1,0:T(8,128)(2,1)S(1)}, u32[]{:S(2)}, u32[]{:S(2)}) %collective-permute-start.4) | collective-permute-done | bytes 917536 | tf_op jit(solution)/shard_map/ppermute | solution.py:25
  33.6 2.2 %latent.9 = (f32[768,256]{1,0:T(8,128)S(1)}, f32[8,128]{1,0:T(8,128)}) custom-call(s32[4]{0:T(128)S(1)} %pad_add_fusion.place, bf16[768,7168]{1,0:T(8,128)(2,1)S(1)} %copy-done.3, bf16[4,448,256]{2,1,0:T(8,128)(2,1)S(1)} %join.1.piece.refs_0_), custom_call_target="tpu_custom_call" | custom-call | bytes 4096 | tf_op jit(solution)/shard_map/latent/pallas_call | solution.py:175
  35.7 2.2 %latent.10 = (f32[768,256]{1,0:T(8,128)S(1)}, f32[8,128]{1,0:T(8,128)}) custom-call(s32[4]{0:T(128)S(1)} %pad_add_fusion.place, bf16[768,7168]{1,0:T(8,128)(2,1)S(1)} %copy-done.3, bf16[4,448,256]{2,1,0:T(8,128)(2,1)S(1)} %tie.2.piece.refs_1_, f32[768,256]{1,0:T(8,128)S(1)} %get-tuple-element.44.refs_0_), custom_call_target="tpu_custom_call" | custom-call | bytes 4096 | tf_op jit(solution)/shard_map/latent/pallas_call | solution.py:175
  37.9 2.2 %latent.11 = (f32[768,256]{1,0:T(8,128)S(1)}, f32[8,128]{1,0:T(8,128)S(1)}) custom-call(s32[4]{0:T(128)S(1)} %pad_add_fusion.place, bf16[768,7168]{1,0:T(8,128)(2,1)S(1)} %copy-done.3, bf16[4,448,256]{2,1,0:T(8,128)(2,1)S(1)} %collective-permute-done.4.piece.refs_3_, f32[768,256]{1,0:T(8,128)S(1)} %get-tuple-element.45.refs_0_), custom_call_target="tpu_custom_call" | custom-call | bytes 4096 | tf_op jit(solution)/shard_map/latent/pallas_call | solution.py:175
  40.1 2.2 %latent.12 = (f32[768,256]{1,0:T(8,128)S(1)}, f32[8,128]{1,0:T(8,128)}) custom-call(s32[4]{0:T(128)S(1)} %pad_add_fusion.place, bf16[768,7168]{1,0:T(8,128)(2,1)S(1)} %copy-done.3, bf16[4,448,256]{2,1,0:T(8,128)(2,1)S(1)} %collective-permute-done.9.piece.refs_5_, f32[768,256]{1,0:T(8,128)S(1)} %get-tuple-element.47.refs_0_), custom_call_target="tpu_custom_call" | custom-call | bytes 4096 | tf_op jit(solution)/shard_map/latent/pallas_call | solution.py:175
  42.4 2.1 %latent.13 = (f32[768,256]{1,0:T(8,128)S(1)}, f32[8,128]{1,0:T(8,128)S(1)}) custom-call(s32[4]{0:T(128)S(1)} %pad_add_fusion.place, bf16[768,7168]{1,0:T(8,128)(2,1)S(1)} %copy-done.3, bf16[4,448,256]{2,1,0:T(8,128)(2,1)S(1)} %collective-permute-done.8.piece.refs_7_, f32[768,256]{1,0:T(8,128)S(1)} %get-tuple-element.48.refs_0_), custom_call_target="tpu_custom_call" | custom-call | bytes 4096 | tf_op jit(solution)/shard_map/latent/pallas_call | solution.py:175
  44.5 3.9 %collective-permute-done.3.value = bf16[4,448,256]{2,1,0:T(8,128)(2,1)S(1)} collective-permute-done((bf16[4,448,256]{2,1,0:T(8,128)(2,1)S(1)}, bf16[4,448,256]{2,1,0:T(8,128)(2,1)S(1)}, u32[]{:S(2)}, u32[]{:S(2)}) %collective-permute-start.3) | collective-permute-done | bytes 917536 | tf_op jit(solution)/shard_map/ppermute | solution.py:25
  48.8 2.2 %latent.14 = (f32[768,256]{1,0:T(8,128)S(1)}, f32[8,128]{1,0:T(8,128)}) custom-call(s32[4]{0:T(128)S(1)} %pad_add_fusion.place, bf16[768,7168]{1,0:T(8,128)(2,1)S(1)} %copy-done.3, bf16[4,448,256]{2,1,0:T(8,128)(2,1)S(1)} %tie.3.piece.refs_2_, f32[768,256]{1,0:T(8,128)S(1)} %get-tuple-element.51.refs_0_), custom_call_target="tpu_custom_call" | custom-call | bytes 4096 | tf_op jit(solution)/shard_map/latent/pallas_call | solution.py:175
  51.3 4.1 %latent.15 = (bf16[784,512]{1,0:T(8,128)(2,1)S(1)}, f32[8,128]{1,0:T(8,128)}) custom-call(s32[4]{0:T(128)S(1)} %pad_add_fusion.place, bf16[768,7168]{1,0:T(8,128)(2,1)S(1)} %copy-done.3, bf16[4,448,256]{2,1,0:T(8,128)(2,1)S(1)} %collective-permute-done.10.piece.refs_6_, f32[768,256]{1,0:T(8,128)S(1)} %get-tuple-element.50.refs_0_, ...), custom_call_target="tpu_custom_call" | custom-call | bytes 4096 | tf_op jit(solution)/shard_map/latent/pallas_call | solution.py:175
  55.7 2.0 %collective-permute-done.11.refs_5_ = bf16[784,512]{1,0:T(8,128)(2,1)S(1)} collective-permute-done((bf16[784,512]{1,0:T(8,128)(2,1)S(1)}, bf16[784,512]{1,0:T(8,128)(2,1)S(1)}, u32[]{:S(2)}, u32[]{:S(2)}) %collective-permute-start.11) | collective-permute-done | bytes 802848 | tf_op jit(solution)/shard_map/ppermute | solution.py:25
  57.7 2.3 %weight_grads.4 = (bf16[2,1808,128]{2,1,0:T(8,128)(2,1)S(1)}, f32[8,128]{1,0:T(8,128)S(1)}) custom-call(s32[4]{0:T(128)S(1)} %pad_add_fusion.place, bf16[3584,768]{1,0:T(8,128)(2,1)S(1)} %get-tuple-element.54.refs_0_.refs_1_, bf16[3584,768]{1,0:T(8,128)(2,1)S(1)} %get-tuple-element.54.refs_0_.refs_1_, ...), custom_call_target="tpu_custom_call" | custom-call | bytes 1048576 | tf_op jit(solution)/shard_map/weight_grads/pallas_call | solution.py:295
  60.0 3.1 %collective-permute-start.13 = (bf16[2,1808,128]{2,1,0:T(8,128)(2,1)S(1)}, bf16[2,1808,128]{2,1,0:T(8,128)(2,1)S(1)}, u32[]{:S(2)}, u32[]{:S(2)}) collective-permute-start(bf16[2,1808,128]{2,1,0:T(8,128)(2,1)S(1)} %get-tuple-element.62), channel_id=1, source_target_pairs={{64,0},{65,1},{66,2},{67,3},{68,4},{69,5},{70,6},{71,7},{72,8},{73... | collective-permute-start | bytes 2777096 | tf_op jit(solution)/shard_map/ppermute | solution.py:25
  63.1 2.3 %weight_grads.5 = (bf16[2,1808,128]{2,1,0:T(8,128)(2,1)S(1)}, f32[8,128]{1,0:T(8,128)S(1)}) custom-call(s32[4]{0:T(128)S(1)} %pad_add_fusion.place, bf16[3584,768]{1,0:T(8,128)(2,1)S(1)} %get-tuple-element.54.refs_0_.refs_1_, bf16[3584,768]{1,0:T(8,128)(2,1)S(1)} %get-tuple-element.54.refs_0_.refs_1_, ...), custom_call_target="tpu_custom_call" | custom-call | bytes 1048576 | tf_op jit(solution)/shard_map/weight_grads/pallas_call | solution.py:295
  66.1 2.3 %weight_grads.6 = (bf16[2,1808,128]{2,1,0:T(8,128)(2,1)S(1)}, f32[8,128]{1,0:T(8,128)S(1)}) custom-call(s32[4]{0:T(128)S(1)} %pad_add_fusion.place, bf16[3584,768]{1,0:T(8,128)(2,1)S(1)} %get-tuple-element.54.refs_0_.refs_1_, bf16[3584,768]{1,0:T(8,128)(2,1)S(1)} %get-tuple-element.54.refs_0_.refs_1_, ...), custom_call_target="tpu_custom_call" | custom-call | bytes 1048576 | tf_op jit(solution)/shard_map/weight_grads/pallas_call | solution.py:295
  68.4 2.7 %collective-permute-start.14 = (bf16[2,1808,128]{2,1,0:T(8,128)(2,1)S(1)}, bf16[2,1808,128]{2,1,0:T(8,128)(2,1)S(1)}, u32[]{:S(2)}, u32[]{:S(2)}) collective-permute-start(bf16[2,1808,128]{2,1,0:T(8,128)(2,1)S(1)} %get-tuple-element.63), channel_id=1, source_target_pairs={{32,0},{33,1},{34,2},{35,3},{36,4},{37,5},{38,6},{39,7},{40,8},{41... | collective-permute-start | bytes 2777096 | tf_op jit(solution)/shard_map/ppermute | solution.py:25
  71.1 2.3 %weight_grads.7 = (bf16[2,1808,128]{2,1,0:T(8,128)(2,1)S(1)}, f32[8,128]{1,0:T(8,128)S(1)}) custom-call(s32[4]{0:T(128)S(1)} %pad_add_fusion.place, bf16[3584,768]{1,0:T(8,128)(2,1)S(1)} %get-tuple-element.54.refs_0_.refs_1_, bf16[3584,768]{1,0:T(8,128)(2,1)S(1)} %get-tuple-element.54.refs_0_.refs_1_, ...), custom_call_target="tpu_custom_call" | custom-call | bytes 1048576 | tf_op jit(solution)/shard_map/weight_grads/pallas_call | solution.py:295
  74.6 5.4 %input_grads.2 = (bf16[768,7168]{1,0:T(8,128)(2,1)}, f32[8,128]{1,0:T(8,128)S(1)}) custom-call(bf16[784,512]{1,0:T(8,128)(2,1)S(1)} %get-tuple-element.53.refs_4_.grad, bf16[7168,512]{1,0:T(8,128)(2,1)S(1)} %assemble.1.weight, f32[8,128]{1,0:T(8,128)S(1)} %get-tuple-element.59.refs_8_.before), custom_call_target="tpu_custom_call" | custom-call | bytes 1048576 | tf_op jit(solution)/shard_map/input_grads/pallas_call | solution.py:235
  80.0 5.0 %collective-permute-done.12.value.refs_1_ = bf16[2,1808,128]{2,1,0:T(8,128)(2,1)S(1)} collective-permute-done((bf16[2,1808,128]{2,1,0:T(8,128)(2,1)S(1)}, bf16[2,1808,128]{2,1,0:T(8,128)(2,1)S(1)}, u32[]{:S(2)}, u32[]{:S(2)}) %collective-permute-start.12) | collective-permute-done | bytes 925728 | tf_op jit(solution)/shard_map/ppermute | solution.py:25
  88.1 1.6 %collective-permute-start.17 = (bf16[960,128]{1,0:T(8,128)(2,1)S(1)}, bf16[960,128]{1,0:T(8,128)(2,1)S(1)}, u32[]{:S(2)}, u32[]{:S(2)}) collective-permute-start(bf16[960,128]{1,0:T(8,128)(2,1)S(1)} %get-tuple-element.71), channel_id=1, source_target_pairs={{4,0},{5,1},{6,2},{7,3},{8,4},{9,5},{10,6},{11,7},{12,8},{13,9},{1... | collective-permute-start | bytes 737288 | tf_op jit(solution)/shard_map/ppermute | solution.py:25
  89.7 4.3 %input_grads.3 = (bf16[768,7168]{1,0:T(8,128)(2,1)}, f32[8,128]{1,0:T(8,128)S(1)}) custom-call(bf16[784,512]{1,0:T(8,128)(2,1)S(1)} %get-tuple-element.53.refs_4_.grad, bf16[7168,512]{1,0:T(8,128)(2,1)S(1)} %assemble.1.weight, f32[8,128]{1,0:T(8,128)S(1)} %get-tuple-element.65.before, ...), custom_call_target="tpu_custom_call", output_to_operand_aliasing={{0}: (3, {})} | custom-call | bytes 1048576 | tf_op jit(solution)/shard_map/input_grads/pallas_call | solution.py:235
  94.0 2.3 %collective-permute-done.15.refs_1_ = bf16[960,128]{1,0:T(8,128)(2,1)S(1)} collective-permute-done((bf16[960,128]{1,0:T(8,128)(2,1)S(1)}, bf16[960,128]{1,0:T(8,128)(2,1)S(1)}, u32[]{:S(2)}, u32[]{:S(2)}) %collective-permute-start.15) | collective-permute-done | bytes 245792 | tf_op jit(solution)/shard_map/ppermute | solution.py:25
  98.0 2.0 %collective-permute-start.19 = (bf16[240,128]{1,0:T(8,128)(2,1)S(1)}, bf16[240,128]{1,0:T(8,128)(2,1)S(1)}, u32[]{:S(2)}, u32[]{:S(2)}) collective-permute-start(bf16[240,128]{1,0:T(8,128)(2,1)S(1)} %get-tuple-element.75), channel_id=1, source_target_pairs={{2,0},{3,1},{0,2},{1,3},{6,4},{7,5},{4,6},{5,7},{10,8},{11,9},{8,1... | collective-permute-start | bytes 184328 | tf_op jit(solution)/shard_map/ppermute | solution.py:25
  101.2 2.9 %collective-permute-done.18.refs_1_ = bf16[240,128]{1,0:T(8,128)(2,1)S(1)} collective-permute-done((bf16[240,128]{1,0:T(8,128)(2,1)S(1)}, bf16[240,128]{1,0:T(8,128)(2,1)S(1)}, u32[]{:S(2)}, u32[]{:S(2)}) %collective-permute-start.18) | collective-permute-done | bytes 61472 | tf_op jit(solution)/shard_map/ppermute | solution.py:25
  (49 shorter events, 12.2 us)
Async XLA Ops:
  0.6 1.0 copy-start
  0.6 20.4 %collective-permute-start.6 = (bf16[768,7168]{1,0:T(8,128)(2,1)}, bf16[768,7168]{1,0:T(8,128)(2,1)}, u32[]{:S(2)}, u32[]{:S(2)}) collective-permute-start(bf16[768,7168]{1,0:T(8,128)(2,1)} %inputs.15), channel_id=1, source_target_pairs={{16,0},{17,1},{18,2},{19,3},{20,4},{21,5},{22,6},{23,7},{24,8},{25... | collective-permute-start | bytes 33030152 | tf_op jit(solution)/shard_map/ppermute | solution.py:25
  1.7 13.0 %collective-permute-start.2 = (bf16[448,256]{1,0:T(8,128)(2,1)S(1)}, bf16[448,256]{1,0:T(8,128)(2,1)S(1)}, u32[]{:S(2)}, u32[]{:S(2)}) collective-permute-start(bf16[448,256]{1,0:T(8,128)(2,1)S(1)} %constant_dynamic-slice_fusion.one), channel_id=1, source_target_pairs={{12,0},{13,1},{14,2},{15,3},{0,4},{1,5},{2,6},{3,7},{4,8},{5,9},{6... | collective-permute-start | bytes 688136 | tf_op jit(solution)/shard_map/ppermute | solution.py:25
  3.4 11.3 %collective-permute-start.1 = (bf16[448,256]{1,0:T(8,128)(2,1)S(1)}, bf16[448,256]{1,0:T(8,128)(2,1)S(1)}, u32[]{:S(2)}, u32[]{:S(2)}) collective-permute-start(bf16[448,256]{1,0:T(8,128)(2,1)S(1)} %constant_dynamic-slice_fusion.one), channel_id=1, source_target_pairs={{8,0},{9,1},{10,2},{11,3},{12,4},{13,5},{14,6},{15,7},{0,8},{1,9},... | collective-permute-start | bytes 688136 | tf_op jit(solution)/shard_map/ppermute | solution.py:25
  6.3 8.4 %collective-permute-start = (bf16[448,256]{1,0:T(8,128)(2,1)S(1)}, bf16[448,256]{1,0:T(8,128)(2,1)S(1)}, u32[]{:S(2)}, u32[]{:S(2)}) collective-permute-start(bf16[448,256]{1,0:T(8,128)(2,1)S(1)} %constant_dynamic-slice_fusion.one), channel_id=1, source_target_pairs={{4,0},{5,1},{6,2},{7,3},{8,4},{9,5},{10,6},{11,7},{12,8},{13,9},{1... | collective-permute-start | bytes 688136 | tf_op jit(solution)/shard_map/ppermute | solution.py:25
  7.7 4.1 %copy-start.2 = (bf16[768,7168]{1,0:T(8,128)(2,1)S(1)}, bf16[768,7168]{1,0:T(8,128)(2,1)}, u32[]{:S(2)}) copy-start(bf16[768,7168]{1,0:T(8,128)(2,1)} %inputs.15) | copy-start | bytes 33030148
  11.9 7.1 %copy-start.3 = (bf16[768,7168]{1,0:T(8,128)(2,1)S(1)}, bf16[768,7168]{1,0:T(8,128)(2,1)}, u32[]{:S(2)}) copy-start(bf16[768,7168]{1,0:T(8,128)(2,1)} %inputs.15) | copy-start | bytes 33030148
  14.7 4.2 %collective-permute-start.7 = (bf16[4,448,256]{2,1,0:T(8,128)(2,1)S(1)}, bf16[4,448,256]{2,1,0:T(8,128)(2,1)S(1)}, u32[]{:S(2)}, u32[]{:S(2)}) collective-permute-start(bf16[4,448,256]{2,1,0:T(8,128)(2,1)S(1)} %join.1.piece.refs_0_), channel_id=1, source_target_pairs={{16,0},{17,1},{18,2},{19,3},{20,4},{21,5},{22,6},{23,7},{24,8},{25... | collective-permute-start | bytes 2752520 | tf_op jit(solution)/shard_map/ppermute | solution.py:25
  14.8 15.0 %collective-permute-start.5 = (bf16[4,448,256]{2,1,0:T(8,128)(2,1)S(1)}, bf16[4,448,256]{2,1,0:T(8,128)(2,1)S(1)}, u32[]{:S(2)}, u32[]{:S(2)}) collective-permute-start(bf16[4,448,256]{2,1,0:T(8,128)(2,1)S(1)} %join.1.piece.refs_0_), channel_id=1, source_target_pairs={{1,0},{2,1},{3,2},{0,3},{5,4},{6,5},{7,6},{4,7},{9,8},{10,9},{11,1... | collective-permute-start | bytes 2752520 | tf_op jit(solution)/shard_map/ppermute | solution.py:25
  18.9 14.6 %collective-permute-start.4 = (bf16[4,448,256]{2,1,0:T(8,128)(2,1)S(1)}, bf16[4,448,256]{2,1,0:T(8,128)(2,1)S(1)}, u32[]{:S(2)}, u32[]{:S(2)}) collective-permute-start(bf16[4,448,256]{2,1,0:T(8,128)(2,1)S(1)} %join.1.piece.refs_0_), channel_id=1, source_target_pairs={{3,0},{0,1},{1,2},{2,3},{7,4},{4,5},{5,6},{6,7},{11,8},{8,9},{9,10... | collective-permute-start | bytes 2752520 | tf_op jit(solution)/shard_map/ppermute | solution.py:25
  29.9 10.2 %collective-permute-start.9 = (bf16[4,448,256]{2,1,0:T(8,128)(2,1)S(1)}, bf16[4,448,256]{2,1,0:T(8,128)(2,1)S(1)}, u32[]{:S(2)}, u32[]{:S(2)}) collective-permute-start(bf16[4,448,256]{2,1,0:T(8,128)(2,1)S(1)} %tie.2.piece.refs_1_), channel_id=1, source_target_pairs={{16,0},{17,1},{18,2},{19,3},{20,4},{21,5},{22,6},{23,7},{24,8},{25... | collective-permute-start | bytes 2752520 | tf_op jit(solution)/shard_map/ppermute | solution.py:25
  33.5 8.8 %collective-permute-start.8 = (bf16[4,448,256]{2,1,0:T(8,128)(2,1)S(1)}, bf16[4,448,256]{2,1,0:T(8,128)(2,1)S(1)}, u32[]{:S(2)}, u32[]{:S(2)}) collective-permute-start(bf16[4,448,256]{2,1,0:T(8,128)(2,1)S(1)} %collective-permute-done.4.piece.refs_3_), channel_id=1, source_target_pairs={{16,0},{17,1},{18,2},{19,3},{20,4},{21,5},{22,6},{23,7},{24,8},{25... | collective-permute-start | bytes 2752520 | tf_op jit(solution)/shard_map/ppermute | solution.py:25
  33.6 14.9 %collective-permute-start.3 = (bf16[4,448,256]{2,1,0:T(8,128)(2,1)S(1)}, bf16[4,448,256]{2,1,0:T(8,128)(2,1)S(1)}, u32[]{:S(2)}, u32[]{:S(2)}) collective-permute-start(bf16[4,448,256]{2,1,0:T(8,128)(2,1)S(1)} %join.1.piece.refs_0_), channel_id=1, source_target_pairs={{2,0},{3,1},{0,2},{1,3},{6,4},{7,5},{4,6},{5,7},{10,8},{11,9},{8,1... | collective-permute-start | bytes 2752520 | tf_op jit(solution)/shard_map/ppermute | solution.py:25
  42.4 8.9 %copy-start.4 = (bf16[768,512]{1,0:T(8,128)(2,1)S(1)}, bf16[768,512]{1,0:T(8,128)(2,1)}, u32[]{:S(2)}) copy-start(bf16[768,512]{1,0:T(8,128)(2,1)} %refs_2_.1) | copy-start | bytes 2359300
  42.4 8.9 %copy-start.5 = (f32[512]{0:T(512)S(1)}, f32[512]{0:T(512)}, u32[]{:S(2)}) copy-start(f32[512]{0:T(512)} %param.7) | copy-start | bytes 6148
  48.5 2.7 %collective-permute-start.10 = (bf16[4,448,256]{2,1,0:T(8,128)(2,1)S(1)}, bf16[4,448,256]{2,1,0:T(8,128)(2,1)S(1)}, u32[]{:S(2)}, u32[]{:S(2)}) collective-permute-start(bf16[4,448,256]{2,1,0:T(8,128)(2,1)S(1)} %tie.3.piece.refs_2_), channel_id=1, source_target_pairs={{16,0},{17,1},{18,2},{19,3},{20,4},{21,5},{22,6},{23,7},{24,8},{25... | collective-permute-start | bytes 2752520 | tf_op jit(solution)/shard_map/ppermute | solution.py:25
  55.3 2.4 %collective-permute-start.11 = (bf16[784,512]{1,0:T(8,128)(2,1)S(1)}, bf16[784,512]{1,0:T(8,128)(2,1)S(1)}, u32[]{:S(2)}, u32[]{:S(2)}) collective-permute-start(bf16[784,512]{1,0:T(8,128)(2,1)S(1)} %get-tuple-element.53.refs_4_.grad), channel_id=1, source_target_pairs={{16,0},{17,1},{18,2},{19,3},{20,4},{21,5},{22,6},{23,7},{24,8},{25... | collective-permute-start | bytes 2408456 | tf_op jit(solution)/shard_map/ppermute | solution.py:25
  60.0 20.0 %collective-permute-start.13 = (bf16[2,1808,128]{2,1,0:T(8,128)(2,1)S(1)}, bf16[2,1808,128]{2,1,0:T(8,128)(2,1)S(1)}, u32[]{:S(2)}, u32[]{:S(2)}) collective-permute-start(bf16[2,1808,128]{2,1,0:T(8,128)(2,1)S(1)} %get-tuple-element.62), channel_id=1, source_target_pairs={{64,0},{65,1},{66,2},{67,3},{68,4},{69,5},{70,6},{71,7},{72,8},{73... | collective-permute-start | bytes 2777096 | tf_op jit(solution)/shard_map/ppermute | solution.py:25
  65.4 19.6 %collective-permute-start.12 = (bf16[2,1808,128]{2,1,0:T(8,128)(2,1)S(1)}, bf16[2,1808,128]{2,1,0:T(8,128)(2,1)S(1)}, u32[]{:S(2)}, u32[]{:S(2)}) collective-permute-start(bf16[2,1808,128]{2,1,0:T(8,128)(2,1)S(1)} %get-tuple-element.61), channel_id=1, source_target_pairs={{96,0},{97,1},{98,2},{99,3},{100,4},{101,5},{102,6},{103,7},{104,8... | collective-permute-start | bytes 2777096 | tf_op jit(solution)/shard_map/ppermute | solution.py:25
  68.4 16.7 %collective-permute-start.14 = (bf16[2,1808,128]{2,1,0:T(8,128)(2,1)S(1)}, bf16[2,1808,128]{2,1,0:T(8,128)(2,1)S(1)}, u32[]{:S(2)}, u32[]{:S(2)}) collective-permute-start(bf16[2,1808,128]{2,1,0:T(8,128)(2,1)S(1)} %get-tuple-element.63), channel_id=1, source_target_pairs={{32,0},{33,1},{34,2},{35,3},{36,4},{37,5},{38,6},{39,7},{40,8},{41... | collective-permute-start | bytes 2777096 | tf_op jit(solution)/shard_map/ppermute | solution.py:25
  85.1 21.0 %copy-start.1 = (bf16[448,512]{1,0:T(8,128)(2,1)S(1)}, bf16[448,512]{1,0:T(8,128)(2,1)}, u32[]{:S(2)}) copy-start(bf16[448,512]{1,0:T(8,128)(2,1)} %param.6) | copy-start | bytes 1376260
  86.1 10.1 %collective-permute-start.15 = (bf16[960,128]{1,0:T(8,128)(2,1)S(1)}, bf16[960,128]{1,0:T(8,128)(2,1)S(1)}, u32[]{:S(2)}, u32[]{:S(2)}) collective-permute-start(bf16[960,128]{1,0:T(8,128)(2,1)S(1)} %get-tuple-element.69), channel_id=1, source_target_pairs={{12,0},{13,1},{14,2},{15,3},{0,4},{1,5},{2,6},{3,7},{4,8},{5,9},{6... | collective-permute-start | bytes 737288 | tf_op jit(solution)/shard_map/ppermute | solution.py:25
  86.8 9.5 %collective-permute-start.16 = (bf16[960,128]{1,0:T(8,128)(2,1)S(1)}, bf16[960,128]{1,0:T(8,128)(2,1)S(1)}, u32[]{:S(2)}, u32[]{:S(2)}) collective-permute-start(bf16[960,128]{1,0:T(8,128)(2,1)S(1)} %get-tuple-element.70), channel_id=1, source_target_pairs={{8,0},{9,1},{10,2},{11,3},{12,4},{13,5},{14,6},{15,7},{0,8},{1,9},... | collective-permute-start | bytes 737288 | tf_op jit(solution)/shard_map/ppermute | solution.py:25
  88.1 9.1 %collective-permute-start.17 = (bf16[960,128]{1,0:T(8,128)(2,1)S(1)}, bf16[960,128]{1,0:T(8,128)(2,1)S(1)}, u32[]{:S(2)}, u32[]{:S(2)}) collective-permute-start(bf16[960,128]{1,0:T(8,128)(2,1)S(1)} %get-tuple-element.71), channel_id=1, source_target_pairs={{4,0},{5,1},{6,2},{7,3},{8,4},{9,5},{10,6},{11,7},{12,8},{13,9},{1... | collective-permute-start | bytes 737288 | tf_op jit(solution)/shard_map/ppermute | solution.py:25
  97.9 6.2 %collective-permute-start.18 = (bf16[240,128]{1,0:T(8,128)(2,1)S(1)}, bf16[240,128]{1,0:T(8,128)(2,1)S(1)}, u32[]{:S(2)}, u32[]{:S(2)}) collective-permute-start(bf16[240,128]{1,0:T(8,128)(2,1)S(1)} %get-tuple-element.74), channel_id=1, source_target_pairs={{3,0},{0,1},{1,2},{2,3},{7,4},{4,5},{5,6},{6,7},{11,8},{8,9},{9,10... | collective-permute-start | bytes 184328 | tf_op jit(solution)/shard_map/ppermute | solution.py:25
  98.0 6.1 %collective-permute-start.19 = (bf16[240,128]{1,0:T(8,128)(2,1)S(1)}, bf16[240,128]{1,0:T(8,128)(2,1)S(1)}, u32[]{:S(2)}, u32[]{:S(2)}) collective-permute-start(bf16[240,128]{1,0:T(8,128)(2,1)S(1)} %get-tuple-element.75), channel_id=1, source_target_pairs={{2,0},{3,1},{0,2},{1,3},{6,4},{7,5},{4,6},{5,7},{10,8},{11,9},{8,1... | collective-permute-start | bytes 184328 | tf_op jit(solution)/shard_map/ppermute | solution.py:25
  100.0 4.9 %collective-permute-start.20 = (bf16[240,128]{1,0:T(8,128)(2,1)S(1)}, bf16[240,128]{1,0:T(8,128)(2,1)S(1)}, u32[]{:S(2)}, u32[]{:S(2)}) collective-permute-start(bf16[240,128]{1,0:T(8,128)(2,1)S(1)} %get-tuple-element.76), channel_id=1, source_target_pairs={{1,0},{2,1},{3,2},{0,3},{5,4},{6,5},{7,6},{4,7},{9,8},{10,9},{11,1... | collective-permute-start | bytes 184328 | tf_op jit(solution)/shard_map/ppermute | solution.py:25

commit v7 on v6

--- a/solution.py
+++ b/solution.py
@@ -107,13 +107,13 @@
     return along_y * 4 + along_z, part
 
 
-def norm(place, first, second, cotangent, gain, out, row):
+def norm(place, start, sums, first, second, cotangent, gain, out):
     core = place[1]
     own = pl.ds(pl.multiple_of(core * 256, 256), 256)
     other = pl.ds(pl.multiple_of(256 - core * 256, 256), 256)
 
-    def body(i, sums):
-        tokens = pl.ds(pl.multiple_of(i * 64, 64), 64)
+    for i in range(4):
+        tokens = pl.ds(start + i * 64, 64)
         latent = [first[tokens, :], second[tokens, :]]
         square = sum(jnp.sum(value * value, axis=1, keepdims=True) for value in latent)
         scale = lax.rsqrt(square * (1.0 / 512) + epsilon)
@@ -123,12 +123,16 @@
         center = sum(jnp.sum(u * v, axis=1, keepdims=True) for u, v in zip(scaled, normed)) * (1.0 / 512)
         for lane, u, v in zip((own, other), scaled, normed):
             out[tokens, lane] = (scale * (u - v * center)).astype(bf16)
-        return tuple(
+        sums = tuple(
             total + jnp.sum((u * v).reshape(8, 8, 256), axis=0) for total, u, v in zip(sums, upstream, normed)
         )
-
-    sums = lax.fori_loop(0, 12, body, (jnp.zeros((8, 256), f32),) * 2, unroll=2)
-    for lane, value in zip((own, other), sums):
+    return sums
+
+
+def norm_gain_rows(place, sums, out, row):
+    core = place[1]
+    for half, value in zip((core, 1 - core), sums):
+        lane = pl.ds(pl.multiple_of(half * 256, 256), 256)
         row[:, lane] = jnp.broadcast_to(jnp.sum(value, axis=0, keepdims=True), (8, 256))
     out[768:784, :] = split(row[0:1, :])
 
@@ -155,11 +159,14 @@
         filled[pl.ds(pl.multiple_of(512 * near + 448 - odd * 448, 64), 64), :] = jnp.zeros((64, 256), bf16)
     for copy in copies:
         copy.wait()
+    sums = (jnp.zeros((8, 256), f32),) * 2
     for start in range(0, 768, 256):
         product = jnp.dot(window[start : start + 256, :], filled[...], preferred_element_type=f32)
         total[start : start + 256, :] = refs[0][start : start + 256, :] + product if has_before else product
+        if last:
+            sums = norm(place, start, sums, ending[0], total, ending[1], ending[2], out)
     if last:
-        norm(place, ending[0], total, ending[1], ending[2], out, extra[1])
+        norm_gain_rows(place, sums, out, extra[1])
 
 
 def latent_part(place, inputs, piece, side, far, before=None, ending=()):

time: 106 us -> 105 us (level)
  Pallas kernels: 49.9 us -> 48.7 us
    pallas_call x8, Pallas kernels: 19.3 us -> 18.1 us  [latent_part(): pl.pallas_call(functools.partial(latent_kernel, side, far, before is not...]
  transfers between devices with their start and end apart: 21 -> 21, of which waited for: 11 -> 11; matrix products, arithmetic and copies ran while one was open for 0% -> 0% of each run, Pallas kernels for 38% -> 39%
where the time goes in v7:
time: 105 us
  Pallas kernels  48.7 us (46%)
  waiting for transfers between devices  25.9 us (25%)
  starting transfers between devices  24.3 us (23%)
  local copies, waits for them, and re-layouts  5.07 us (5%)
    ppermute x21, waiting for transfers between devices, fetch(): lax.ppermute(value, axes, [(device(*source(*spot)), device(*spot)) for sp...  25.9 us
    ppermute x21, starting transfers between devices, fetch(): lax.ppermute(value, axes, [(device(*source(*spot)), device(*spot)) for sp...  24.3 us
    pallas_call x8, Pallas kernels, latent_part(): pl.pallas_call(functools.partial(latent_kernel, side, far, before is not...  18.1 us
    pallas_call x2, Pallas kernels, input_grads(): pl.pallas_call(input_kernel, grid=(count,), in_specs=[pl.BlockSpec((784,...  9.68 us
    pallas_call x4, Pallas kernels, weight_grads(): pl.pallas_call(weight_kernel, grid_spec=pltpu.PrefetchScalarGridSpec(num_...  9.26 us
    pallas_call x2, Pallas kernels, turn(): pl.pallas_call(turn_kernel, grid_spec=pltpu.PrefetchScalarGridSpec(num_sc...  7.36 us
    unnamed x12, local copies, waits for them, and re-layouts  5.05 us
    pallas_call x3, Pallas kernels, combine(): pl.pallas_call(kernel, in_specs=[pl.BlockSpec(memory_space=pltpu.SMEM)] +...  2.97 us
  transfers between devices with their start and end apart: 21, of which 11 were waited for; matrix products, arithmetic and copies ran while one was open for 0% of the time, Pallas kernels for 39%

profile of v7, /device:TPU:0, one launch (start us, length us, event | category | flops | bytes accessed | tf_op | source)
XLA Modules:
  0.0 104.9 jit_solution(11374179174505817406)
XLA Ops:
  1.7 1.7 %collective-permute-start.2 = (bf16[448,256]{1,0:T(8,128)(2,1)S(1)}, bf16[448,256]{1,0:T(8,128)(2,1)S(1)}, u32[]{:S(2)}, u32[]{:S(2)}) collective-permute-start(bf16[448,256]{1,0:T(8,128)(2,1)S(1)} %constant_dynamic-slice_fusion.one), channel_id=1, source_target_pairs={{12,0},{13,1},{14,2},{15,3},{0,4},{1,5},{2,6},{3,7},{4,8},{5,9},{6... | collective-permute-start | bytes 688136 | tf_op jit(solution)/shard_map/ppermute | solution.py:25
  3.4 2.9 %collective-permute-start.1 = (bf16[448,256]{1,0:T(8,128)(2,1)S(1)}, bf16[448,256]{1,0:T(8,128)(2,1)S(1)}, u32[]{:S(2)}, u32[]{:S(2)}) collective-permute-start(bf16[448,256]{1,0:T(8,128)(2,1)S(1)} %constant_dynamic-slice_fusion.one), channel_id=1, source_target_pairs={{8,0},{9,1},{10,2},{11,3},{12,4},{13,5},{14,6},{15,7},{0,8},{1,9},... | collective-permute-start | bytes 688136 | tf_op jit(solution)/shard_map/ppermute | solution.py:25
  6.3 1.3 %collective-permute-start = (bf16[448,256]{1,0:T(8,128)(2,1)S(1)}, bf16[448,256]{1,0:T(8,128)(2,1)S(1)}, u32[]{:S(2)}, u32[]{:S(2)}) collective-permute-start(bf16[448,256]{1,0:T(8,128)(2,1)S(1)} %constant_dynamic-slice_fusion.one), channel_id=1, source_target_pairs={{4,0},{5,1},{6,2},{7,3},{8,4},{9,5},{10,6},{11,7},{12,8},{13,9},{1... | collective-permute-start | bytes 688136 | tf_op jit(solution)/shard_map/ppermute | solution.py:25
  7.7 4.1 %copy-done.2 = bf16[768,7168]{1,0:T(8,128)(2,1)S(1)} copy-done((bf16[768,7168]{1,0:T(8,128)(2,1)S(1)}, bf16[768,7168]{1,0:T(8,128)(2,1)}, u32[]{:S(2)}) %copy-start.2) | copy-done | bytes 11010072
  11.9 2.8 %turn.2 = (bf16[3584,768]{1,0:T(8,128)(2,1)S(1)}, f32[8,128]{1,0:T(8,128)S(1)}) custom-call(s32[4]{0:T(128)S(1)} %pad_add_fusion.place, bf16[768,7168]{1,0:T(8,128)(2,1)S(1)} %copy-done.2), custom_call_target="tpu_custom_call" | custom-call | bytes 23068672 | tf_op jit(solution)/shard_map/turn/pallas_call | solution.py:50
  14.8 4.1 %collective-permute-start.5 = (bf16[4,448,256]{2,1,0:T(8,128)(2,1)S(1)}, bf16[4,448,256]{2,1,0:T(8,128)(2,1)S(1)}, u32[]{:S(2)}, u32[]{:S(2)}) collective-permute-start(bf16[4,448,256]{2,1,0:T(8,128)(2,1)S(1)} %join.1.piece.refs_0_), channel_id=1, source_target_pairs={{1,0},{2,1},{3,2},{0,3},{5,4},{6,5},{7,6},{4,7},{9,8},{10,9},{11,1... | collective-permute-start | bytes 2752520 | tf_op jit(solution)/shard_map/ppermute | solution.py:25
  19.0 2.1 %latent.8 = (f32[768,256]{1,0:T(8,128)S(1)}, f32[8,128]{1,0:T(8,128)S(1)}) custom-call(s32[4]{0:T(128)S(1)} %pad_add_fusion.place, bf16[768,7168]{1,0:T(8,128)(2,1)S(1)} %copy-done.3, bf16[4,448,256]{2,1,0:T(8,128)(2,1)S(1)} %collective-permute-done.7.piece.refs_4_), custom_call_target="tpu_custom_call" | custom-call | bytes 4096 | tf_op jit(solution)/shard_map/latent/pallas_call | solution.py:182
  21.1 4.6 %turn.3 = (bf16[3584,768]{1,0:T(8,128)(2,1)S(1)}, f32[8,128]{1,0:T(8,128)S(1)}) custom-call(s32[4]{0:T(128)S(1)} %pad_add_fusion.place, bf16[768,7168]{1,0:T(8,128)(2,1)} %collective-permute-done.6.rows), custom_call_target="tpu_custom_call" | custom-call | bytes 23068672 | tf_op jit(solution)/shard_map/turn/pallas_call | solution.py:50
  25.7 4.2 %collective-permute-done.5.value = bf16[4,448,256]{2,1,0:T(8,128)(2,1)S(1)} collective-permute-done((bf16[4,448,256]{2,1,0:T(8,128)(2,1)S(1)}, bf16[4,448,256]{2,1,0:T(8,128)(2,1)S(1)}, u32[]{:S(2)}, u32[]{:S(2)}) %collective-permute-start.5) | collective-permute-done | bytes 917536 | tf_op jit(solution)/shard_map/ppermute | solution.py:25
  30.0 3.5 %collective-permute-done.4.piece.refs_3_ = bf16[4,448,256]{2,1,0:T(8,128)(2,1)S(1)} collective-permute-done((bf16[4,448,256]{2,1,0:T(8,128)(2,1)S(1)}, bf16[4,448,256]{2,1,0:T(8,128)(2,1)S(1)}, u32[]{:S(2)}, u32[]{:S(2)}) %collective-permute-start.4) | collective-permute-done | bytes 917536 | tf_op jit(solution)/shard_map/ppermute | solution.py:25
  33.6 2.2 %latent.9 = (f32[768,256]{1,0:T(8,128)S(1)}, f32[8,128]{1,0:T(8,128)}) custom-call(s32[4]{0:T(128)S(1)} %pad_add_fusion.place, bf16[768,7168]{1,0:T(8,128)(2,1)S(1)} %copy-done.3, bf16[4,448,256]{2,1,0:T(8,128)(2,1)S(1)} %join.1.piece.refs_0_), custom_call_target="tpu_custom_call" | custom-call | bytes 4096 | tf_op jit(solution)/shard_map/latent/pallas_call | solution.py:182
  35.7 2.2 %latent.10 = (f32[768,256]{1,0:T(8,128)S(1)}, f32[8,128]{1,0:T(8,128)}) custom-call(s32[4]{0:T(128)S(1)} %pad_add_fusion.place, bf16[768,7168]{1,0:T(8,128)(2,1)S(1)} %copy-done.3, bf16[4,448,256]{2,1,0:T(8,128)(2,1)S(1)} %tie.2.piece.refs_1_, f32[768,256]{1,0:T(8,128)S(1)} %get-tuple-element.44.refs_0_), custom_call_target="tpu_custom_call" | custom-call | bytes 4096 | tf_op jit(solution)/shard_map/latent/pallas_call | solution.py:182
  37.9 2.2 %latent.11 = (f32[768,256]{1,0:T(8,128)S(1)}, f32[8,128]{1,0:T(8,128)S(1)}) custom-call(s32[4]{0:T(128)S(1)} %pad_add_fusion.place, bf16[768,7168]{1,0:T(8,128)(2,1)S(1)} %copy-done.3, bf16[4,448,256]{2,1,0:T(8,128)(2,1)S(1)} %collective-permute-done.4.piece.refs_3_, f32[768,256]{1,0:T(8,128)S(1)} %get-tuple-element.45.refs_0_), custom_call_target="tpu_custom_call" | custom-call | bytes 4096 | tf_op jit(solution)/shard_map/latent/pallas_call | solution.py:182
  40.1 2.2 %latent.12 = (f32[768,256]{1,0:T(8,128)S(1)}, f32[8,128]{1,0:T(8,128)}) custom-call(s32[4]{0:T(128)S(1)} %pad_add_fusion.place, bf16[768,7168]{1,0:T(8,128)(2,1)S(1)} %copy-done.3, bf16[4,448,256]{2,1,0:T(8,128)(2,1)S(1)} %collective-permute-done.9.piece.refs_5_, f32[768,256]{1,0:T(8,128)S(1)} %get-tuple-element.47.refs_0_), custom_call_target="tpu_custom_call" | custom-call | bytes 4096 | tf_op jit(solution)/shard_map/latent/pallas_call | solution.py:182
  42.4 2.1 %latent.13 = (f32[768,256]{1,0:T(8,128)S(1)}, f32[8,128]{1,0:T(8,128)S(1)}) custom-call(s32[4]{0:T(128)S(1)} %pad_add_fusion.place, bf16[768,7168]{1,0:T(8,128)(2,1)S(1)} %copy-done.3, bf16[4,448,256]{2,1,0:T(8,128)(2,1)S(1)} %collective-permute-done.8.piece.refs_7_, f32[768,256]{1,0:T(8,128)S(1)} %get-tuple-element.48.refs_0_), custom_call_target="tpu_custom_call" | custom-call | bytes 4096 | tf_op jit(solution)/shard_map/latent/pallas_call | solution.py:182
  44.5 3.9 %collective-permute-done.3.value = bf16[4,448,256]{2,1,0:T(8,128)(2,1)S(1)} collective-permute-done((bf16[4,448,256]{2,1,0:T(8,128)(2,1)S(1)}, bf16[4,448,256]{2,1,0:T(8,128)(2,1)S(1)}, u32[]{:S(2)}, u32[]{:S(2)}) %collective-permute-start.3) | collective-permute-done | bytes 917536 | tf_op jit(solution)/shard_map/ppermute | solution.py:25
  48.8 2.2 %latent.14 = (f32[768,256]{1,0:T(8,128)S(1)}, f32[8,128]{1,0:T(8,128)}) custom-call(s32[4]{0:T(128)S(1)} %pad_add_fusion.place, bf16[768,7168]{1,0:T(8,128)(2,1)S(1)} %copy-done.3, bf16[4,448,256]{2,1,0:T(8,128)(2,1)S(1)} %tie.3.piece.refs_2_, f32[768,256]{1,0:T(8,128)S(1)} %get-tuple-element.51.refs_0_), custom_call_target="tpu_custom_call" | custom-call | bytes 4096 | tf_op jit(solution)/shard_map/latent/pallas_call | solution.py:182
  51.3 2.8 %latent.15 = (bf16[784,512]{1,0:T(8,128)(2,1)S(1)}, f32[8,128]{1,0:T(8,128)}) custom-call(s32[4]{0:T(128)S(1)} %pad_add_fusion.place, bf16[768,7168]{1,0:T(8,128)(2,1)S(1)} %copy-done.3, bf16[4,448,256]{2,1,0:T(8,128)(2,1)S(1)} %collective-permute-done.10.piece.refs_6_, f32[768,256]{1,0:T(8,128)S(1)} %get-tuple-element.50.refs_0_, ...), custom_call_target="tpu_custom_call" | custom-call | bytes 4096 | tf_op jit(solution)/shard_map/latent/pallas_call | solution.py:182
  54.5 2.0 %collective-permute-done.11.refs_5_ = bf16[784,512]{1,0:T(8,128)(2,1)S(1)} collective-permute-done((bf16[784,512]{1,0:T(8,128)(2,1)S(1)}, bf16[784,512]{1,0:T(8,128)(2,1)S(1)}, u32[]{:S(2)}, u32[]{:S(2)}) %collective-permute-start.11) | collective-permute-done | bytes 802848 | tf_op jit(solution)/shard_map/ppermute | solution.py:25
  56.5 2.3 %weight_grads.4 = (bf16[2,1808,128]{2,1,0:T(8,128)(2,1)S(1)}, f32[8,128]{1,0:T(8,128)S(1)}) custom-call(s32[4]{0:T(128)S(1)} %pad_add_fusion.place, bf16[3584,768]{1,0:T(8,128)(2,1)S(1)} %get-tuple-element.54.refs_0_.refs_1_, bf16[3584,768]{1,0:T(8,128)(2,1)S(1)} %get-tuple-element.54.refs_0_.refs_1_, ...), custom_call_target="tpu_custom_call" | custom-call | bytes 1048576 | tf_op jit(solution)/shard_map/weight_grads/pallas_call | solution.py:302
  58.8 3.1 %collective-permute-start.13 = (bf16[2,1808,128]{2,1,0:T(8,128)(2,1)S(1)}, bf16[2,1808,128]{2,1,0:T(8,128)(2,1)S(1)}, u32[]{:S(2)}, u32[]{:S(2)}) collective-permute-start(bf16[2,1808,128]{2,1,0:T(8,128)(2,1)S(1)} %get-tuple-element.62), channel_id=1, source_target_pairs={{64,0},{65,1},{66,2},{67,3},{68,4},{69,5},{70,6},{71,7},{72,8},{73... | collective-permute-start | bytes 2777096 | tf_op jit(solution)/shard_map/ppermute | solution.py:25
  61.9 2.3 %weight_grads.5 = (bf16[2,1808,128]{2,1,0:T(8,128)(2,1)S(1)}, f32[8,128]{1,0:T(8,128)S(1)}) custom-call(s32[4]{0:T(128)S(1)} %pad_add_fusion.place, bf16[3584,768]{1,0:T(8,128)(2,1)S(1)} %get-tuple-element.54.refs_0_.refs_1_, bf16[3584,768]{1,0:T(8,128)(2,1)S(1)} %get-tuple-element.54.refs_0_.refs_1_, ...), custom_call_target="tpu_custom_call" | custom-call | bytes 1048576 | tf_op jit(solution)/shard_map/weight_grads/pallas_call | solution.py:302
  64.9 2.3 %weight_grads.6 = (bf16[2,1808,128]{2,1,0:T(8,128)(2,1)S(1)}, f32[8,128]{1,0:T(8,128)S(1)}) custom-call(s32[4]{0:T(128)S(1)} %pad_add_fusion.place, bf16[3584,768]{1,0:T(8,128)(2,1)S(1)} %get-tuple-element.54.refs_0_.refs_1_, bf16[3584,768]{1,0:T(8,128)(2,1)S(1)} %get-tuple-element.54.refs_0_.refs_1_, ...), custom_call_target="tpu_custom_call" | custom-call | bytes 1048576 | tf_op jit(solution)/shard_map/weight_grads/pallas_call | solution.py:302
  67.2 2.7 %collective-permute-start.14 = (bf16[2,1808,128]{2,1,0:T(8,128)(2,1)S(1)}, bf16[2,1808,128]{2,1,0:T(8,128)(2,1)S(1)}, u32[]{:S(2)}, u32[]{:S(2)}) collective-permute-start(bf16[2,1808,128]{2,1,0:T(8,128)(2,1)S(1)} %get-tuple-element.63), channel_id=1, source_target_pairs={{32,0},{33,1},{34,2},{35,3},{36,4},{37,5},{38,6},{39,7},{40,8},{41... | collective-permute-start | bytes 2777096 | tf_op jit(solution)/shard_map/ppermute | solution.py:25
  69.9 2.3 %weight_grads.7 = (bf16[2,1808,128]{2,1,0:T(8,128)(2,1)S(1)}, f32[8,128]{1,0:T(8,128)S(1)}) custom-call(s32[4]{0:T(128)S(1)} %pad_add_fusion.place, bf16[3584,768]{1,0:T(8,128)(2,1)S(1)} %get-tuple-element.54.refs_0_.refs_1_, bf16[3584,768]{1,0:T(8,128)(2,1)S(1)} %get-tuple-element.54.refs_0_.refs_1_, ...), custom_call_target="tpu_custom_call" | custom-call | bytes 1048576 | tf_op jit(solution)/shard_map/weight_grads/pallas_call | solution.py:302
  73.4 5.4 %input_grads.2 = (bf16[768,7168]{1,0:T(8,128)(2,1)}, f32[8,128]{1,0:T(8,128)S(1)}) custom-call(bf16[784,512]{1,0:T(8,128)(2,1)S(1)} %get-tuple-element.53.refs_4_.grad, bf16[7168,512]{1,0:T(8,128)(2,1)S(1)} %assemble.1.weight, f32[8,128]{1,0:T(8,128)S(1)} %get-tuple-element.59.refs_8_.before), custom_call_target="tpu_custom_call" | custom-call | bytes 1048576 | tf_op jit(solution)/shard_map/input_grads/pallas_call | solution.py:242
  78.8 5.0 %collective-permute-done.12.value.refs_1_ = bf16[2,1808,128]{2,1,0:T(8,128)(2,1)S(1)} collective-permute-done((bf16[2,1808,128]{2,1,0:T(8,128)(2,1)S(1)}, bf16[2,1808,128]{2,1,0:T(8,128)(2,1)S(1)}, u32[]{:S(2)}, u32[]{:S(2)}) %collective-permute-start.12) | collective-permute-done | bytes 925728 | tf_op jit(solution)/shard_map/ppermute | solution.py:25
  86.9 1.6 %collective-permute-start.17 = (bf16[960,128]{1,0:T(8,128)(2,1)S(1)}, bf16[960,128]{1,0:T(8,128)(2,1)S(1)}, u32[]{:S(2)}, u32[]{:S(2)}) collective-permute-start(bf16[960,128]{1,0:T(8,128)(2,1)S(1)} %get-tuple-element.71), channel_id=1, source_target_pairs={{4,0},{5,1},{6,2},{7,3},{8,4},{9,5},{10,6},{11,7},{12,8},{13,9},{1... | collective-permute-start | bytes 737288 | tf_op jit(solution)/shard_map/ppermute | solution.py:25
  88.5 4.3 %input_grads.3 = (bf16[768,7168]{1,0:T(8,128)(2,1)}, f32[8,128]{1,0:T(8,128)S(1)}) custom-call(bf16[784,512]{1,0:T(8,128)(2,1)S(1)} %get-tuple-element.53.refs_4_.grad, bf16[7168,512]{1,0:T(8,128)(2,1)S(1)} %assemble.1.weight, f32[8,128]{1,0:T(8,128)S(1)} %get-tuple-element.65.before, ...), custom_call_target="tpu_custom_call", output_to_operand_aliasing={{0}: (3, {})} | custom-call | bytes 1048576 | tf_op jit(solution)/shard_map/input_grads/pallas_call | solution.py:242
  92.8 2.3 %collective-permute-done.15.refs_1_ = bf16[960,128]{1,0:T(8,128)(2,1)S(1)} collective-permute-done((bf16[960,128]{1,0:T(8,128)(2,1)S(1)}, bf16[960,128]{1,0:T(8,128)(2,1)S(1)}, u32[]{:S(2)}, u32[]{:S(2)}) %collective-permute-start.15) | collective-permute-done | bytes 245792 | tf_op jit(solution)/shard_map/ppermute | solution.py:25
  96.8 2.0 %collective-permute-start.19 = (bf16[240,128]{1,0:T(8,128)(2,1)S(1)}, bf16[240,128]{1,0:T(8,128)(2,1)S(1)}, u32[]{:S(2)}, u32[]{:S(2)}) collective-permute-start(bf16[240,128]{1,0:T(8,128)(2,1)S(1)} %get-tuple-element.75), channel_id=1, source_target_pairs={{2,0},{3,1},{0,2},{1,3},{6,4},{7,5},{4,6},{5,7},{10,8},{11,9},{8,1... | collective-permute-start | bytes 184328 | tf_op jit(solution)/shard_map/ppermute | solution.py:25
  100.0 2.9 %collective-permute-done.18.refs_1_ = bf16[240,128]{1,0:T(8,128)(2,1)S(1)} collective-permute-done((bf16[240,128]{1,0:T(8,128)(2,1)S(1)}, bf16[240,128]{1,0:T(8,128)(2,1)S(1)}, u32[]{:S(2)}, u32[]{:S(2)}) %collective-permute-start.18) | collective-permute-done | bytes 61472 | tf_op jit(solution)/shard_map/ppermute | solution.py:25
  (49 shorter events, 12.2 us)
Async XLA Ops:
  0.6 1.0 copy-start
  0.6 20.4 %collective-permute-start.6 = (bf16[768,7168]{1,0:T(8,128)(2,1)}, bf16[768,7168]{1,0:T(8,128)(2,1)}, u32[]{:S(2)}, u32[]{:S(2)}) collective-permute-start(bf16[768,7168]{1,0:T(8,128)(2,1)} %inputs.15), channel_id=1, source_target_pairs={{16,0},{17,1},{18,2},{19,3},{20,4},{21,5},{22,6},{23,7},{24,8},{25... | collective-permute-start | bytes 33030152 | tf_op jit(solution)/shard_map/ppermute | solution.py:25
  1.7 13.0 %collective-permute-start.2 = (bf16[448,256]{1,0:T(8,128)(2,1)S(1)}, bf16[448,256]{1,0:T(8,128)(2,1)S(1)}, u32[]{:S(2)}, u32[]{:S(2)}) collective-permute-start(bf16[448,256]{1,0:T(8,128)(2,1)S(1)} %constant_dynamic-slice_fusion.one), channel_id=1, source_target_pairs={{12,0},{13,1},{14,2},{15,3},{0,4},{1,5},{2,6},{3,7},{4,8},{5,9},{6... | collective-permute-start | bytes 688136 | tf_op jit(solution)/shard_map/ppermute | solution.py:25
  3.4 11.3 %collective-permute-start.1 = (bf16[448,256]{1,0:T(8,128)(2,1)S(1)}, bf16[448,256]{1,0:T(8,128)(2,1)S(1)}, u32[]{:S(2)}, u32[]{:S(2)}) collective-permute-start(bf16[448,256]{1,0:T(8,128)(2,1)S(1)} %constant_dynamic-slice_fusion.one), channel_id=1, source_target_pairs={{8,0},{9,1},{10,2},{11,3},{12,4},{13,5},{14,6},{15,7},{0,8},{1,9},... | collective-permute-start | bytes 688136 | tf_op jit(solution)/shard_map/ppermute | solution.py:25
  6.3 8.4 %collective-permute-start = (bf16[448,256]{1,0:T(8,128)(2,1)S(1)}, bf16[448,256]{1,0:T(8,128)(2,1)S(1)}, u32[]{:S(2)}, u32[]{:S(2)}) collective-permute-start(bf16[448,256]{1,0:T(8,128)(2,1)S(1)} %constant_dynamic-slice_fusion.one), channel_id=1, source_target_pairs={{4,0},{5,1},{6,2},{7,3},{8,4},{9,5},{10,6},{11,7},{12,8},{13,9},{1... | collective-permute-start | bytes 688136 | tf_op jit(solution)/shard_map/ppermute | solution.py:25
  7.7 4.1 %copy-start.2 = (bf16[768,7168]{1,0:T(8,128)(2,1)S(1)}, bf16[768,7168]{1,0:T(8,128)(2,1)}, u32[]{:S(2)}) copy-start(bf16[768,7168]{1,0:T(8,128)(2,1)} %inputs.15) | copy-start | bytes 33030148
  11.9 7.1 %copy-start.3 = (bf16[768,7168]{1,0:T(8,128)(2,1)S(1)}, bf16[768,7168]{1,0:T(8,128)(2,1)}, u32[]{:S(2)}) copy-start(bf16[768,7168]{1,0:T(8,128)(2,1)} %inputs.15) | copy-start | bytes 33030148
  14.7 4.2 %collective-permute-start.7 = (bf16[4,448,256]{2,1,0:T(8,128)(2,1)S(1)}, bf16[4,448,256]{2,1,0:T(8,128)(2,1)S(1)}, u32[]{:S(2)}, u32[]{:S(2)}) collective-permute-start(bf16[4,448,256]{2,1,0:T(8,128)(2,1)S(1)} %join.1.piece.refs_0_), channel_id=1, source_target_pairs={{16,0},{17,1},{18,2},{19,3},{20,4},{21,5},{22,6},{23,7},{24,8},{25... | collective-permute-start | bytes 2752520 | tf_op jit(solution)/shard_map/ppermute | solution.py:25
  14.8 15.0 %collective-permute-start.5 = (bf16[4,448,256]{2,1,0:T(8,128)(2,1)S(1)}, bf16[4,448,256]{2,1,0:T(8,128)(2,1)S(1)}, u32[]{:S(2)}, u32[]{:S(2)}) collective-permute-start(bf16[4,448,256]{2,1,0:T(8,128)(2,1)S(1)} %join.1.piece.refs_0_), channel_id=1, source_target_pairs={{1,0},{2,1},{3,2},{0,3},{5,4},{6,5},{7,6},{4,7},{9,8},{10,9},{11,1... | collective-permute-start | bytes 2752520 | tf_op jit(solution)/shard_map/ppermute | solution.py:25
  18.9 14.6 %collective-permute-start.4 = (bf16[4,448,256]{2,1,0:T(8,128)(2,1)S(1)}, bf16[4,448,256]{2,1,0:T(8,128)(2,1)S(1)}, u32[]{:S(2)}, u32[]{:S(2)}) collective-permute-start(bf16[4,448,256]{2,1,0:T(8,128)(2,1)S(1)} %join.1.piece.refs_0_), channel_id=1, source_target_pairs={{3,0},{0,1},{1,2},{2,3},{7,4},{4,5},{5,6},{6,7},{11,8},{8,9},{9,10... | collective-permute-start | bytes 2752520 | tf_op jit(solution)/shard_map/ppermute | solution.py:25
  29.9 10.2 %collective-permute-start.9 = (bf16[4,448,256]{2,1,0:T(8,128)(2,1)S(1)}, bf16[4,448,256]{2,1,0:T(8,128)(2,1)S(1)}, u32[]{:S(2)}, u32[]{:S(2)}) collective-permute-start(bf16[4,448,256]{2,1,0:T(8,128)(2,1)S(1)} %tie.2.piece.refs_1_), channel_id=1, source_target_pairs={{16,0},{17,1},{18,2},{19,3},{20,4},{21,5},{22,6},{23,7},{24,8},{25... | collective-permute-start | bytes 2752520 | tf_op jit(solution)/shard_map/ppermute | solution.py:25
  33.5 8.8 %collective-permute-start.8 = (bf16[4,448,256]{2,1,0:T(8,128)(2,1)S(1)}, bf16[4,448,256]{2,1,0:T(8,128)(2,1)S(1)}, u32[]{:S(2)}, u32[]{:S(2)}) collective-permute-start(bf16[4,448,256]{2,1,0:T(8,128)(2,1)S(1)} %collective-permute-done.4.piece.refs_3_), channel_id=1, source_target_pairs={{16,0},{17,1},{18,2},{19,3},{20,4},{21,5},{22,6},{23,7},{24,8},{25... | collective-permute-start | bytes 2752520 | tf_op jit(solution)/shard_map/ppermute | solution.py:25
  33.6 14.9 %collective-permute-start.3 = (bf16[4,448,256]{2,1,0:T(8,128)(2,1)S(1)}, bf16[4,448,256]{2,1,0:T(8,128)(2,1)S(1)}, u32[]{:S(2)}, u32[]{:S(2)}) collective-permute-start(bf16[4,448,256]{2,1,0:T(8,128)(2,1)S(1)} %join.1.piece.refs_0_), channel_id=1, source_target_pairs={{2,0},{3,1},{0,2},{1,3},{6,4},{7,5},{4,6},{5,7},{10,8},{11,9},{8,1... | collective-permute-start | bytes 2752520 | tf_op jit(solution)/shard_map/ppermute | solution.py:25
  42.4 8.9 %copy-start.4 = (bf16[768,512]{1,0:T(8,128)(2,1)S(1)}, bf16[768,512]{1,0:T(8,128)(2,1)}, u32[]{:S(2)}) copy-start(bf16[768,512]{1,0:T(8,128)(2,1)} %refs_2_.1) | copy-start | bytes 2359300
  42.4 8.9 %copy-start.5 = (f32[512]{0:T(512)S(1)}, f32[512]{0:T(512)}, u32[]{:S(2)}) copy-start(f32[512]{0:T(512)} %param.7) | copy-start | bytes 6148
  48.5 2.7 %collective-permute-start.10 = (bf16[4,448,256]{2,1,0:T(8,128)(2,1)S(1)}, bf16[4,448,256]{2,1,0:T(8,128)(2,1)S(1)}, u32[]{:S(2)}, u32[]{:S(2)}) collective-permute-start(bf16[4,448,256]{2,1,0:T(8,128)(2,1)S(1)} %tie.3.piece.refs_2_), channel_id=1, source_target_pairs={{16,0},{17,1},{18,2},{19,3},{20,4},{21,5},{22,6},{23,7},{24,8},{25... | collective-permute-start | bytes 2752520 | tf_op jit(solution)/shard_map/ppermute | solution.py:25
  54.1 2.4 %collective-permute-start.11 = (bf16[784,512]{1,0:T(8,128)(2,1)S(1)}, bf16[784,512]{1,0:T(8,128)(2,1)S(1)}, u32[]{:S(2)}, u32[]{:S(2)}) collective-permute-start(bf16[784,512]{1,0:T(8,128)(2,1)S(1)} %get-tuple-element.53.refs_4_.grad), channel_id=1, source_target_pairs={{16,0},{17,1},{18,2},{19,3},{20,4},{21,5},{22,6},{23,7},{24,8},{25... | collective-permute-start | bytes 2408456 | tf_op jit(solution)/shard_map/ppermute | solution.py:25
  58.8 20.0 %collective-permute-start.13 = (bf16[2,1808,128]{2,1,0:T(8,128)(2,1)S(1)}, bf16[2,1808,128]{2,1,0:T(8,128)(2,1)S(1)}, u32[]{:S(2)}, u32[]{:S(2)}) collective-permute-start(bf16[2,1808,128]{2,1,0:T(8,128)(2,1)S(1)} %get-tuple-element.62), channel_id=1, source_target_pairs={{64,0},{65,1},{66,2},{67,3},{68,4},{69,5},{70,6},{71,7},{72,8},{73... | collective-permute-start | bytes 2777096 | tf_op jit(solution)/shard_map/ppermute | solution.py:25
  64.2 19.6 %collective-permute-start.12 = (bf16[2,1808,128]{2,1,0:T(8,128)(2,1)S(1)}, bf16[2,1808,128]{2,1,0:T(8,128)(2,1)S(1)}, u32[]{:S(2)}, u32[]{:S(2)}) collective-permute-start(bf16[2,1808,128]{2,1,0:T(8,128)(2,1)S(1)} %get-tuple-element.61), channel_id=1, source_target_pairs={{96,0},{97,1},{98,2},{99,3},{100,4},{101,5},{102,6},{103,7},{104,8... | collective-permute-start | bytes 2777096 | tf_op jit(solution)/shard_map/ppermute | solution.py:25
  67.2 16.7 %collective-permute-start.14 = (bf16[2,1808,128]{2,1,0:T(8,128)(2,1)S(1)}, bf16[2,1808,128]{2,1,0:T(8,128)(2,1)S(1)}, u32[]{:S(2)}, u32[]{:S(2)}) collective-permute-start(bf16[2,1808,128]{2,1,0:T(8,128)(2,1)S(1)} %get-tuple-element.63), channel_id=1, source_target_pairs={{32,0},{33,1},{34,2},{35,3},{36,4},{37,5},{38,6},{39,7},{40,8},{41... | collective-permute-start | bytes 2777096 | tf_op jit(solution)/shard_map/ppermute | solution.py:25
  83.9 21.0 %copy-start.1 = (bf16[448,512]{1,0:T(8,128)(2,1)S(1)}, bf16[448,512]{1,0:T(8,128)(2,1)}, u32[]{:S(2)}) copy-start(bf16[448,512]{1,0:T(8,128)(2,1)} %param.6) | copy-start | bytes 1376260
  84.9 10.1 %collective-permute-start.15 = (bf16[960,128]{1,0:T(8,128)(2,1)S(1)}, bf16[960,128]{1,0:T(8,128)(2,1)S(1)}, u32[]{:S(2)}, u32[]{:S(2)}) collective-permute-start(bf16[960,128]{1,0:T(8,128)(2,1)S(1)} %get-tuple-element.69), channel_id=1, source_target_pairs={{12,0},{13,1},{14,2},{15,3},{0,4},{1,5},{2,6},{3,7},{4,8},{5,9},{6... | collective-permute-start | bytes 737288 | tf_op jit(solution)/shard_map/ppermute | solution.py:25
  85.6 9.5 %collective-permute-start.16 = (bf16[960,128]{1,0:T(8,128)(2,1)S(1)}, bf16[960,128]{1,0:T(8,128)(2,1)S(1)}, u32[]{:S(2)}, u32[]{:S(2)}) collective-permute-start(bf16[960,128]{1,0:T(8,128)(2,1)S(1)} %get-tuple-element.70), channel_id=1, source_target_pairs={{8,0},{9,1},{10,2},{11,3},{12,4},{13,5},{14,6},{15,7},{0,8},{1,9},... | collective-permute-start | bytes 737288 | tf_op jit(solution)/shard_map/ppermute | solution.py:25
  86.9 9.1 %collective-permute-start.17 = (bf16[960,128]{1,0:T(8,128)(2,1)S(1)}, bf16[960,128]{1,0:T(8,128)(2,1)S(1)}, u32[]{:S(2)}, u32[]{:S(2)}) collective-permute-start(bf16[960,128]{1,0:T(8,128)(2,1)S(1)} %get-tuple-element.71), channel_id=1, source_target_pairs={{4,0},{5,1},{6,2},{7,3},{8,4},{9,5},{10,6},{11,7},{12,8},{13,9},{1... | collective-permute-start | bytes 737288 | tf_op jit(solution)/shard_map/ppermute | solution.py:25
  96.7 6.2 %collective-permute-start.18 = (bf16[240,128]{1,0:T(8,128)(2,1)S(1)}, bf16[240,128]{1,0:T(8,128)(2,1)S(1)}, u32[]{:S(2)}, u32[]{:S(2)}) collective-permute-start(bf16[240,128]{1,0:T(8,128)(2,1)S(1)} %get-tuple-element.74), channel_id=1, source_target_pairs={{3,0},{0,1},{1,2},{2,3},{7,4},{4,5},{5,6},{6,7},{11,8},{8,9},{9,10... | collective-permute-start | bytes 184328 | tf_op jit(solution)/shard_map/ppermute | solution.py:25
  96.8 6.1 %collective-permute-start.19 = (bf16[240,128]{1,0:T(8,128)(2,1)S(1)}, bf16[240,128]{1,0:T(8,128)(2,1)S(1)}, u32[]{:S(2)}, u32[]{:S(2)}) collective-permute-start(bf16[240,128]{1,0:T(8,128)(2,1)S(1)} %get-tuple-element.75), channel_id=1, source_target_pairs={{2,0},{3,1},{0,2},{1,3},{6,4},{7,5},{4,6},{5,7},{10,8},{11,9},{8,1... | collective-permute-start | bytes 184328 | tf_op jit(solution)/shard_map/ppermute | solution.py:25
  98.8 4.9 %collective-permute-start.20 = (bf16[240,128]{1,0:T(8,128)(2,1)S(1)}, bf16[240,128]{1,0:T(8,128)(2,1)S(1)}, u32[]{:S(2)}, u32[]{:S(2)}) collective-permute-start(bf16[240,128]{1,0:T(8,128)(2,1)S(1)} %get-tuple-element.76), channel_id=1, source_target_pairs={{1,0},{2,1},{3,2},{0,3},{5,4},{6,5},{7,6},{4,7},{9,8},{10,9},{11,1... | collective-permute-start | bytes 184328 | tf_op jit(solution)/shard_map/ppermute | solution.py:25

commit v8 on v7

--- a/solution.py
+++ b/solution.py
@@ -237,24 +237,22 @@
     ).astype(bf16)
 
 
-def input_grads(grad, weight, token, first, count, begun=()):
+def input_grads(grad, weight, token):
     small = pl.BlockSpec((8, 128), lambda i: (0, 0))
     return pl.pallas_call(
         input_kernel,
-        grid=(count,),
+        grid=(7,),
         in_specs=[
             pl.BlockSpec((784, 512), lambda i: (0, 0)),
-            pl.BlockSpec((1024, 512), lambda i: (first + i, 0)),
+            pl.BlockSpec((1024, 512), lambda i: (i, 0)),
             small,
-        ]
-        + [pl.BlockSpec(memory_space=pltpu.HBM)] * len(begun),
-        out_specs=[pl.BlockSpec((768, 1024), lambda i: (0, first + i)), small],
+        ],
+        out_specs=[pl.BlockSpec((768, 1024), lambda i: (0, i)), small],
         out_shape=[jax.ShapeDtypeStruct((768, 7168), bf16), order],
-        input_output_aliases={3: 0} if begun else {},
         compiler_params=pltpu.CompilerParams(vmem_limit_bytes=40 * MIB),
         cost_estimate=pl.CostEstimate(flops=0, bytes_accessed=MIB, transcendentals=0),
         name="input_grads",
-    )(grad, weight, token, *begun)
+    )(grad, weight, token)
 
 
 lanes = [slice(128 * i, 128 * i + 128) for i in four]
@@ -321,8 +319,7 @@
 
 
 def first_kernel(place, *refs):
-    partial, out, token = refs[:4], refs[-5:-1], refs[-1]
-    token[...] = jnp.zeros((8, 128), f32)
+    partial, out = refs[:4], refs[-4:]
     other = jnp.where(place[1] == 0, place[2], place[0])
     for to in four:
         at = lax.rem(other + to, 4)
@@ -334,7 +331,7 @@
 
 
 def second_kernel(place, *refs):
-    sums, out, held = refs[:4], refs[5:9], refs[9]
+    sums, out, held = refs[:4], refs[4:8], refs[8]
     x, core, y, z = [place[i] for i in four]
     for i in four:
         held[i] = sums[i][896:960, :].astype(f32)
@@ -408,20 +405,18 @@
 
 def first_sums(place, partial, latent_grad, gathered, token):
     sums = exchange(partial, along_major)
-    input_grad, token = input_grads(latent_grad, gathered, token, 0, 4)
+    input_grad, token = input_grads(latent_grad, gathered, token)
     token = touch(sums[1], touch(sums[2], token))
-    outs = [((960, 128), bf16)] * 4 + [((8, 128), f32)]
+    outs = [((960, 128), bf16)] * 4
     return combine(first_kernel, outs, place, sums, tokens=[token]), input_grad
 
 
-def last_sums(place, sums, latent_grad, gathered, input_grad):
-    token = sums[4]
-    sums = exchange(sums[:4], along_other)
-    input_grad, token = input_grads(latent_grad, gathered, token, 4, 3, [input_grad])
+def last_sums(place, sums):
+    sums = exchange(sums, along_other)
     scratch = [pltpu.VMEM((4, 64, 128), f32)]
-    sums = combine(second_kernel, [((240, 128), bf16)] * 4, place, sums, scratch, [token])
+    sums = combine(second_kernel, [((240, 128), bf16)] * 4, place, sums, scratch)
     sums = exchange(sums, along_z)
-    return *combine(third_kernel, [((56, 512), f32), ((4, 128), f32)], place, sums), input_grad
+    return combine(third_kernel, [((56, 512), f32), ((4, 128), f32)], place, sums)
 
 
 def shards(inputs, cotangent, weight, norm_gain):
@@ -459,7 +454,7 @@
         tokens = [token]
     gathered = assemble(place, mine + theirs, token)
     sums, input_grad = first_sums(place, partial, latent_grad, gathered, token)
-    weight_grad, gain_grad, input_grad = last_sums(place, sums, latent_grad, gathered, input_grad)
+    weight_grad, gain_grad = last_sums(place, sums)
     return (input_grad, weight_grad, gain_grad.reshape(512))
 
 

time: 105 us -> 105 us (level)
  waiting for transfers between devices: 25.9 us -> 28.5 us
  starting transfers between devices: 24.3 us -> 22.8 us
    ppermute x21, waiting for transfers between devices: 25.9 us -> 28.5 us  [fetch(): lax.ppermute(value, axes, [(device(*source(*spot)), device(*spot)) for sp...]
    ppermute x21, starting transfers between devices: 24.3 us -> 22.8 us  [fetch(): lax.ppermute(value, axes, [(device(*source(*spot)), device(*spot)) for sp...]
    pallas_call x2 -> x1, Pallas kernels: 9.68 us -> 8.67 us  [input_grads(): pl.pallas_call(input_kernel, grid=(7,), in_specs=[pl.BlockSpec((784, 512)...]
  transfers between devices with their start and end apart: 21 -> 21, of which waited for: 11 -> 12; matrix products, arithmetic and copies ran while one was open for 0% -> 0% of each run, Pallas kernels for 39% -> 38%
where the time goes in v8:
time: 105 us
  Pallas kernels  47.7 us (45%)
  waiting for transfers between devices  28.5 us (27%)
  starting transfers between devices  22.8 us (22%)
  local copies, waits for them, and re-layouts  5.07 us (5%)
    ppermute x21, waiting for transfers between devices, fetch(): lax.ppermute(value, axes, [(device(*source(*spot)), device(*spot)) for sp...  28.5 us
    ppermute x21, starting transfers between devices, fetch(): lax.ppermute(value, axes, [(device(*source(*spot)), device(*spot)) for sp...  22.8 us
    pallas_call x8, Pallas kernels, latent_part(): pl.pallas_call(functools.partial(latent_kernel, side, far, before is not...  18.1 us
    pallas_call x4, Pallas kernels, weight_grads(): pl.pallas_call(weight_kernel, grid_spec=pltpu.PrefetchScalarGridSpec(num_...  9.26 us
    pallas_call x1, Pallas kernels, input_grads(): pl.pallas_call(input_kernel, grid=(7,), in_specs=[pl.BlockSpec((784, 512)...  8.67 us
    pallas_call x2, Pallas kernels, turn(): pl.pallas_call(turn_kernel, grid_spec=pltpu.PrefetchScalarGridSpec(num_sc...  7.36 us
    unnamed x12, local copies, waits for them, and re-layouts  5.05 us
    pallas_call x3, Pallas kernels, combine(): pl.pallas_call(kernel, in_specs=[pl.BlockSpec(memory_space=pltpu.SMEM)] +...  2.96 us
  transfers between devices with their start and end apart: 21, of which 12 were waited for; matrix products, arithmetic and copies ran while one was open for 0% of the time, Pallas kernels for 38%

profile of v8, /device:TPU:0, one launch (start us, length us, event | category | flops | bytes accessed | tf_op | source)
XLA Modules:
  0.0 105.1 jit_solution(301306823842360837)
XLA Ops:
  1.7 3.2 %collective-permute-start = (bf16[448,256]{1,0:T(8,128)(2,1)S(1)}, bf16[448,256]{1,0:T(8,128)(2,1)S(1)}, u32[]{:S(2)}, u32[]{:S(2)}) collective-permute-start(bf16[448,256]{1,0:T(8,128)(2,1)S(1)} %constant_dynamic-slice_fusion.one), channel_id=1, source_target_pairs={{4,0},{5,1},{6,2},{7,3},{8,4},{9,5},{10,6},{11,7},{12,8},{13,9},{1... | collective-permute-start | bytes 688136 | tf_op jit(solution)/shard_map/ppermute | solution.py:25
  6.5 4.1 %copy-done.2 = bf16[768,7168]{1,0:T(8,128)(2,1)S(1)} copy-done((bf16[768,7168]{1,0:T(8,128)(2,1)S(1)}, bf16[768,7168]{1,0:T(8,128)(2,1)}, u32[]{:S(2)}) %copy-start.2) | copy-done | bytes 11010072
  10.7 2.8 %turn.2 = (bf16[3584,768]{1,0:T(8,128)(2,1)S(1)}, f32[8,128]{1,0:T(8,128)S(1)}) custom-call(s32[4]{0:T(128)S(1)} %pad_add_fusion.place, bf16[768,7168]{1,0:T(8,128)(2,1)S(1)} %copy-done.2), custom_call_target="tpu_custom_call" | custom-call | bytes 23068672 | tf_op jit(solution)/shard_map/turn/pallas_call | solution.py:50
  13.5 1.4 %collective-permute-done.2.four_ = bf16[448,256]{1,0:T(8,128)(2,1)S(1)} collective-permute-done((bf16[448,256]{1,0:T(8,128)(2,1)S(1)}, bf16[448,256]{1,0:T(8,128)(2,1)S(1)}, u32[]{:S(2)}, u32[]{:S(2)}) %collective-permute-start.2) | collective-permute-done | bytes 229408 | tf_op jit(solution)/shard_map/ppermute | solution.py:25
  15.0 4.1 %collective-permute-start.5 = (bf16[4,448,256]{2,1,0:T(8,128)(2,1)S(1)}, bf16[4,448,256]{2,1,0:T(8,128)(2,1)S(1)}, u32[]{:S(2)}, u32[]{:S(2)}) collective-permute-start(bf16[4,448,256]{2,1,0:T(8,128)(2,1)S(1)} %join.1.piece.refs_0_), channel_id=1, source_target_pairs={{1,0},{2,1},{3,2},{0,3},{5,4},{6,5},{7,6},{4,7},{9,8},{10,9},{11,1... | collective-permute-start | bytes 2752520 | tf_op jit(solution)/shard_map/ppermute | solution.py:25
  19.1 2.1 %latent.8 = (f32[768,256]{1,0:T(8,128)S(1)}, f32[8,128]{1,0:T(8,128)S(1)}) custom-call(s32[4]{0:T(128)S(1)} %pad_add_fusion.place, bf16[768,7168]{1,0:T(8,128)(2,1)S(1)} %copy-done.3, bf16[4,448,256]{2,1,0:T(8,128)(2,1)S(1)} %collective-permute-done.7.piece.refs_4_), custom_call_target="tpu_custom_call" | custom-call | bytes 4096 | tf_op jit(solution)/shard_map/latent/pallas_call | solution.py:182
  21.2 4.6 %turn.3 = (bf16[3584,768]{1,0:T(8,128)(2,1)S(1)}, f32[8,128]{1,0:T(8,128)S(1)}) custom-call(s32[4]{0:T(128)S(1)} %pad_add_fusion.place, bf16[768,7168]{1,0:T(8,128)(2,1)} %collective-permute-done.6.rows), custom_call_target="tpu_custom_call" | custom-call | bytes 23068672 | tf_op jit(solution)/shard_map/turn/pallas_call | solution.py:50
  25.8 4.2 %collective-permute-done.5.value = bf16[4,448,256]{2,1,0:T(8,128)(2,1)S(1)} collective-permute-done((bf16[4,448,256]{2,1,0:T(8,128)(2,1)S(1)}, bf16[4,448,256]{2,1,0:T(8,128)(2,1)S(1)}, u32[]{:S(2)}, u32[]{:S(2)}) %collective-permute-start.5) | collective-permute-done | bytes 917536 | tf_op jit(solution)/shard_map/ppermute | solution.py:25
  30.2 3.5 %collective-permute-done.4.piece.refs_3_ = bf16[4,448,256]{2,1,0:T(8,128)(2,1)S(1)} collective-permute-done((bf16[4,448,256]{2,1,0:T(8,128)(2,1)S(1)}, bf16[4,448,256]{2,1,0:T(8,128)(2,1)S(1)}, u32[]{:S(2)}, u32[]{:S(2)}) %collective-permute-start.4) | collective-permute-done | bytes 917536 | tf_op jit(solution)/shard_map/ppermute | solution.py:25
  33.7 2.2 %latent.9 = (f32[768,256]{1,0:T(8,128)S(1)}, f32[8,128]{1,0:T(8,128)}) custom-call(s32[4]{0:T(128)S(1)} %pad_add_fusion.place, bf16[768,7168]{1,0:T(8,128)(2,1)S(1)} %copy-done.3, bf16[4,448,256]{2,1,0:T(8,128)(2,1)S(1)} %join.1.piece.refs_0_), custom_call_target="tpu_custom_call" | custom-call | bytes 4096 | tf_op jit(solution)/shard_map/latent/pallas_call | solution.py:182
  35.9 2.2 %latent.10 = (f32[768,256]{1,0:T(8,128)S(1)}, f32[8,128]{1,0:T(8,128)}) custom-call(s32[4]{0:T(128)S(1)} %pad_add_fusion.place, bf16[768,7168]{1,0:T(8,128)(2,1)S(1)} %copy-done.3, bf16[4,448,256]{2,1,0:T(8,128)(2,1)S(1)} %tie.2.piece.refs_1_, f32[768,256]{1,0:T(8,128)S(1)} %get-tuple-element.41.refs_0_), custom_call_target="tpu_custom_call" | custom-call | bytes 4096 | tf_op jit(solution)/shard_map/latent/pallas_call | solution.py:182
  38.1 2.2 %latent.11 = (f32[768,256]{1,0:T(8,128)S(1)}, f32[8,128]{1,0:T(8,128)S(1)}) custom-call(s32[4]{0:T(128)S(1)} %pad_add_fusion.place, bf16[768,7168]{1,0:T(8,128)(2,1)S(1)} %copy-done.3, bf16[4,448,256]{2,1,0:T(8,128)(2,1)S(1)} %collective-permute-done.4.piece.refs_3_, f32[768,256]{1,0:T(8,128)S(1)} %get-tuple-element.42.refs_0_), custom_call_target="tpu_custom_call" | custom-call | bytes 4096 | tf_op jit(solution)/shard_map/latent/pallas_call | solution.py:182
  40.3 2.2 %latent.12 = (f32[768,256]{1,0:T(8,128)S(1)}, f32[8,128]{1,0:T(8,128)}) custom-call(s32[4]{0:T(128)S(1)} %pad_add_fusion.place, bf16[768,7168]{1,0:T(8,128)(2,1)S(1)} %copy-done.3, bf16[4,448,256]{2,1,0:T(8,128)(2,1)S(1)} %collective-permute-done.9.piece.refs_5_, f32[768,256]{1,0:T(8,128)S(1)} %get-tuple-element.44.refs_0_), custom_call_target="tpu_custom_call" | custom-call | bytes 4096 | tf_op jit(solution)/shard_map/latent/pallas_call | solution.py:182
  42.5 2.1 %latent.13 = (f32[768,256]{1,0:T(8,128)S(1)}, f32[8,128]{1,0:T(8,128)S(1)}) custom-call(s32[4]{0:T(128)S(1)} %pad_add_fusion.place, bf16[768,7168]{1,0:T(8,128)(2,1)S(1)} %copy-done.3, bf16[4,448,256]{2,1,0:T(8,128)(2,1)S(1)} %collective-permute-done.8.piece.refs_7_, f32[768,256]{1,0:T(8,128)S(1)} %get-tuple-element.45.refs_0_), custom_call_target="tpu_custom_call" | custom-call | bytes 4096 | tf_op jit(solution)/shard_map/latent/pallas_call | solution.py:182
  44.7 3.9 %collective-permute-done.3.value = bf16[4,448,256]{2,1,0:T(8,128)(2,1)S(1)} collective-permute-done((bf16[4,448,256]{2,1,0:T(8,128)(2,1)S(1)}, bf16[4,448,256]{2,1,0:T(8,128)(2,1)S(1)}, u32[]{:S(2)}, u32[]{:S(2)}) %collective-permute-start.3) | collective-permute-done | bytes 917536 | tf_op jit(solution)/shard_map/ppermute | solution.py:25
  48.9 2.2 %latent.14 = (f32[768,256]{1,0:T(8,128)S(1)}, f32[8,128]{1,0:T(8,128)}) custom-call(s32[4]{0:T(128)S(1)} %pad_add_fusion.place, bf16[768,7168]{1,0:T(8,128)(2,1)S(1)} %copy-done.3, bf16[4,448,256]{2,1,0:T(8,128)(2,1)S(1)} %tie.3.piece.refs_2_, f32[768,256]{1,0:T(8,128)S(1)} %get-tuple-element.48.refs_0_), custom_call_target="tpu_custom_call" | custom-call | bytes 4096 | tf_op jit(solution)/shard_map/latent/pallas_call | solution.py:182
  51.4 2.9 %latent.15 = (bf16[784,512]{1,0:T(8,128)(2,1)S(1)}, f32[8,128]{1,0:T(8,128)}) custom-call(s32[4]{0:T(128)S(1)} %pad_add_fusion.place, bf16[768,7168]{1,0:T(8,128)(2,1)S(1)} %copy-done.3, bf16[4,448,256]{2,1,0:T(8,128)(2,1)S(1)} %collective-permute-done.10.piece.refs_6_, f32[768,256]{1,0:T(8,128)S(1)} %get-tuple-element.47.refs_0_, ...), custom_call_target="tpu_custom_call" | custom-call | bytes 4096 | tf_op jit(solution)/shard_map/latent/pallas_call | solution.py:182
  54.6 2.0 %collective-permute-done.11.refs_5_ = bf16[784,512]{1,0:T(8,128)(2,1)S(1)} collective-permute-done((bf16[784,512]{1,0:T(8,128)(2,1)S(1)}, bf16[784,512]{1,0:T(8,128)(2,1)S(1)}, u32[]{:S(2)}, u32[]{:S(2)}) %collective-permute-start.11) | collective-permute-done | bytes 802848 | tf_op jit(solution)/shard_map/ppermute | solution.py:25
  56.6 2.3 %weight_grads.4 = (bf16[2,1808,128]{2,1,0:T(8,128)(2,1)S(1)}, f32[8,128]{1,0:T(8,128)S(1)}) custom-call(s32[4]{0:T(128)S(1)} %pad_add_fusion.place, bf16[3584,768]{1,0:T(8,128)(2,1)S(1)} %get-tuple-element.51.refs_0_.refs_1_, bf16[3584,768]{1,0:T(8,128)(2,1)S(1)} %get-tuple-element.51.refs_0_.refs_1_, ...), custom_call_target="tpu_custom_call" | custom-call | bytes 1048576 | tf_op jit(solution)/shard_map/weight_grads/pallas_call | solution.py:300
  59.0 3.1 %collective-permute-start.13 = (bf16[2,1808,128]{2,1,0:T(8,128)(2,1)S(1)}, bf16[2,1808,128]{2,1,0:T(8,128)(2,1)S(1)}, u32[]{:S(2)}, u32[]{:S(2)}) collective-permute-start(bf16[2,1808,128]{2,1,0:T(8,128)(2,1)S(1)} %get-tuple-element.60), channel_id=1, source_target_pairs={{64,0},{65,1},{66,2},{67,3},{68,4},{69,5},{70,6},{71,7},{72,8},{73... | collective-permute-start | bytes 2777096 | tf_op jit(solution)/shard_map/ppermute | solution.py:25
  62.1 2.3 %weight_grads.5 = (bf16[2,1808,128]{2,1,0:T(8,128)(2,1)S(1)}, f32[8,128]{1,0:T(8,128)S(1)}) custom-call(s32[4]{0:T(128)S(1)} %pad_add_fusion.place, bf16[3584,768]{1,0:T(8,128)(2,1)S(1)} %get-tuple-element.51.refs_0_.refs_1_, bf16[3584,768]{1,0:T(8,128)(2,1)S(1)} %get-tuple-element.51.refs_0_.refs_1_, ...), custom_call_target="tpu_custom_call" | custom-call | bytes 1048576 | tf_op jit(solution)/shard_map/weight_grads/pallas_call | solution.py:300
  65.1 2.3 %weight_grads.6 = (bf16[2,1808,128]{2,1,0:T(8,128)(2,1)S(1)}, f32[8,128]{1,0:T(8,128)S(1)}) custom-call(s32[4]{0:T(128)S(1)} %pad_add_fusion.place, bf16[3584,768]{1,0:T(8,128)(2,1)S(1)} %get-tuple-element.51.refs_0_.refs_1_, bf16[3584,768]{1,0:T(8,128)(2,1)S(1)} %get-tuple-element.51.refs_0_.refs_1_, ...), custom_call_target="tpu_custom_call" | custom-call | bytes 1048576 | tf_op jit(solution)/shard_map/weight_grads/pallas_call | solution.py:300
  67.4 2.7 %collective-permute-start.14 = (bf16[2,1808,128]{2,1,0:T(8,128)(2,1)S(1)}, bf16[2,1808,128]{2,1,0:T(8,128)(2,1)S(1)}, u32[]{:S(2)}, u32[]{:S(2)}) collective-permute-start(bf16[2,1808,128]{2,1,0:T(8,128)(2,1)S(1)} %get-tuple-element.61), channel_id=1, source_target_pairs={{32,0},{33,1},{34,2},{35,3},{36,4},{37,5},{38,6},{39,7},{40,8},{41... | collective-permute-start | bytes 2777096 | tf_op jit(solution)/shard_map/ppermute | solution.py:25
  70.1 2.3 %weight_grads.7 = (bf16[2,1808,128]{2,1,0:T(8,128)(2,1)S(1)}, f32[8,128]{1,0:T(8,128)S(1)}) custom-call(s32[4]{0:T(128)S(1)} %pad_add_fusion.place, bf16[3584,768]{1,0:T(8,128)(2,1)S(1)} %get-tuple-element.51.refs_0_.refs_1_, bf16[3584,768]{1,0:T(8,128)(2,1)S(1)} %get-tuple-element.51.refs_0_.refs_1_, ...), custom_call_target="tpu_custom_call" | custom-call | bytes 1048576 | tf_op jit(solution)/shard_map/weight_grads/pallas_call | solution.py:300
  73.6 8.7 %input_grads.1 = (bf16[768,7168]{1,0:T(8,128)(2,1)}, f32[8,128]{1,0:T(8,128)S(1)}) custom-call(bf16[784,512]{1,0:T(8,128)(2,1)S(1)} %get-tuple-element.50.refs_4_.grad, bf16[7168,512]{1,0:T(8,128)(2,1)S(1)} %assemble.1.weight, f32[8,128]{1,0:T(8,128)S(1)} %get-tuple-element.56.refs_8_.before), custom_call_target="tpu_custom_call" | custom-call | bytes 1048576 | tf_op jit(solution)/shard_map/input_grads/pallas_call | solution.py:242
  82.2 1.7 %collective-permute-done.12.value.refs_1_ = bf16[2,1808,128]{2,1,0:T(8,128)(2,1)S(1)} collective-permute-done((bf16[2,1808,128]{2,1,0:T(8,128)(2,1)S(1)}, bf16[2,1808,128]{2,1,0:T(8,128)(2,1)S(1)}, u32[]{:S(2)}, u32[]{:S(2)}) %collective-permute-start.12) | collective-permute-done | bytes 925728 | tf_op jit(solution)/shard_map/ppermute | solution.py:25
  85.6 1.9 %collective-permute-start.16 = (bf16[960,128]{1,0:T(8,128)(2,1)S(1)}, bf16[960,128]{1,0:T(8,128)(2,1)S(1)}, u32[]{:S(2)}, u32[]{:S(2)}) collective-permute-start(bf16[960,128]{1,0:T(8,128)(2,1)S(1)} %get-tuple-element.65), channel_id=1, source_target_pairs={{8,0},{9,1},{10,2},{11,3},{12,4},{13,5},{14,6},{15,7},{0,8},{1,9},... | collective-permute-start | bytes 737288 | tf_op jit(solution)/shard_map/ppermute | solution.py:25
  88.4 6.8 %collective-permute-done.15.refs_1_ = bf16[960,128]{1,0:T(8,128)(2,1)S(1)} collective-permute-done((bf16[960,128]{1,0:T(8,128)(2,1)S(1)}, bf16[960,128]{1,0:T(8,128)(2,1)S(1)}, u32[]{:S(2)}, u32[]{:S(2)}) %collective-permute-start.15) | collective-permute-done | bytes 245792 | tf_op jit(solution)/shard_map/ppermute | solution.py:25
  96.9 2.0 %collective-permute-start.19 = (bf16[240,128]{1,0:T(8,128)(2,1)S(1)}, bf16[240,128]{1,0:T(8,128)(2,1)S(1)}, u32[]{:S(2)}, u32[]{:S(2)}) collective-permute-start(bf16[240,128]{1,0:T(8,128)(2,1)S(1)} %get-tuple-element.69), channel_id=1, source_target_pairs={{2,0},{3,1},{0,2},{1,3},{6,4},{7,5},{4,6},{5,7},{10,8},{11,9},{8,1... | collective-permute-start | bytes 184328 | tf_op jit(solution)/shard_map/ppermute | solution.py:25
  98.9 1.2 %collective-permute-start.20 = (bf16[240,128]{1,0:T(8,128)(2,1)S(1)}, bf16[240,128]{1,0:T(8,128)(2,1)S(1)}, u32[]{:S(2)}, u32[]{:S(2)}) collective-permute-start(bf16[240,128]{1,0:T(8,128)(2,1)S(1)} %get-tuple-element.70), channel_id=1, source_target_pairs={{1,0},{2,1},{3,2},{0,3},{5,4},{6,5},{7,6},{4,7},{9,8},{10,9},{11,1... | collective-permute-start | bytes 184328 | tf_op jit(solution)/shard_map/ppermute | solution.py:25
  100.2 2.9 %collective-permute-done.18.refs_1_ = bf16[240,128]{1,0:T(8,128)(2,1)S(1)} collective-permute-done((bf16[240,128]{1,0:T(8,128)(2,1)S(1)}, bf16[240,128]{1,0:T(8,128)(2,1)S(1)}, u32[]{:S(2)}, u32[]{:S(2)}) %collective-permute-start.18) | collective-permute-done | bytes 61472 | tf_op jit(solution)/shard_map/ppermute | solution.py:25
  103.9 1.2 %third_kernel.1 = (f32[56,512]{1,0:T(8,128)}, f32[4,128]{1,0:T(4,128)}) custom-call(s32[4]{0:T(128)S(1)} %pad_add_fusion.place, bf16[240,128]{1,0:T(8,128)(2,1)S(1)} %get-tuple-element.67.refs_0_, bf16[240,128]{1,0:T(8,128)(2,1)S(1)} %collective-permute-done.18.refs_1_, bf16[240,128]{1,0:T(8,128)(2,1)S(1)} %collective-permute-done.19.refs_2_, ...), custom_call_target="tpu_custom_call" | custom-call | bytes 1048576 | tf_op jit(solution)/shard_map/third_kernel/pallas_call | solution.py:377
  (48 shorter events, 10.8 us)
Async XLA Ops:
  0.6 1.0 copy-start
  0.6 20.6 %collective-permute-start.6 = (bf16[768,7168]{1,0:T(8,128)(2,1)}, bf16[768,7168]{1,0:T(8,128)(2,1)}, u32[]{:S(2)}, u32[]{:S(2)}) collective-permute-start(bf16[768,7168]{1,0:T(8,128)(2,1)} %inputs.15), channel_id=1, source_target_pairs={{16,0},{17,1},{18,2},{19,3},{20,4},{21,5},{22,6},{23,7},{24,8},{25... | collective-permute-start | bytes 33030152 | tf_op jit(solution)/shard_map/ppermute | solution.py:25
  1.7 11.8 %collective-permute-start = (bf16[448,256]{1,0:T(8,128)(2,1)S(1)}, bf16[448,256]{1,0:T(8,128)(2,1)S(1)}, u32[]{:S(2)}, u32[]{:S(2)}) collective-permute-start(bf16[448,256]{1,0:T(8,128)(2,1)S(1)} %constant_dynamic-slice_fusion.one), channel_id=1, source_target_pairs={{4,0},{5,1},{6,2},{7,3},{8,4},{9,5},{10,6},{11,7},{12,8},{13,9},{1... | collective-permute-start | bytes 688136 | tf_op jit(solution)/shard_map/ppermute | solution.py:25
  4.8 8.6 %collective-permute-start.1 = (bf16[448,256]{1,0:T(8,128)(2,1)S(1)}, bf16[448,256]{1,0:T(8,128)(2,1)S(1)}, u32[]{:S(2)}, u32[]{:S(2)}) collective-permute-start(bf16[448,256]{1,0:T(8,128)(2,1)S(1)} %constant_dynamic-slice_fusion.one), channel_id=1, source_target_pairs={{8,0},{9,1},{10,2},{11,3},{12,4},{13,5},{14,6},{15,7},{0,8},{1,9},... | collective-permute-start | bytes 688136 | tf_op jit(solution)/shard_map/ppermute | solution.py:25
  5.5 9.4 %collective-permute-start.2 = (bf16[448,256]{1,0:T(8,128)(2,1)S(1)}, bf16[448,256]{1,0:T(8,128)(2,1)S(1)}, u32[]{:S(2)}, u32[]{:S(2)}) collective-permute-start(bf16[448,256]{1,0:T(8,128)(2,1)S(1)} %constant_dynamic-slice_fusion.one), channel_id=1, source_target_pairs={{12,0},{13,1},{14,2},{15,3},{0,4},{1,5},{2,6},{3,7},{4,8},{5,9},{6... | collective-permute-start | bytes 688136 | tf_op jit(solution)/shard_map/ppermute | solution.py:25
  6.5 4.1 %copy-start.2 = (bf16[768,7168]{1,0:T(8,128)(2,1)S(1)}, bf16[768,7168]{1,0:T(8,128)(2,1)}, u32[]{:S(2)}) copy-start(bf16[768,7168]{1,0:T(8,128)(2,1)} %inputs.15) | copy-start | bytes 33030148
  10.7 8.4 %copy-start.3 = (bf16[768,7168]{1,0:T(8,128)(2,1)S(1)}, bf16[768,7168]{1,0:T(8,128)(2,1)}, u32[]{:S(2)}) copy-start(bf16[768,7168]{1,0:T(8,128)(2,1)} %inputs.15) | copy-start | bytes 33030148
  14.9 4.2 %collective-permute-start.7 = (bf16[4,448,256]{2,1,0:T(8,128)(2,1)S(1)}, bf16[4,448,256]{2,1,0:T(8,128)(2,1)S(1)}, u32[]{:S(2)}, u32[]{:S(2)}) collective-permute-start(bf16[4,448,256]{2,1,0:T(8,128)(2,1)S(1)} %join.1.piece.refs_0_), channel_id=1, source_target_pairs={{16,0},{17,1},{18,2},{19,3},{20,4},{21,5},{22,6},{23,7},{24,8},{25... | collective-permute-start | bytes 2752520 | tf_op jit(solution)/shard_map/ppermute | solution.py:25
  15.0 15.0 %collective-permute-start.5 = (bf16[4,448,256]{2,1,0:T(8,128)(2,1)S(1)}, bf16[4,448,256]{2,1,0:T(8,128)(2,1)S(1)}, u32[]{:S(2)}, u32[]{:S(2)}) collective-permute-start(bf16[4,448,256]{2,1,0:T(8,128)(2,1)S(1)} %join.1.piece.refs_0_), channel_id=1, source_target_pairs={{1,0},{2,1},{3,2},{0,3},{5,4},{6,5},{7,6},{4,7},{9,8},{10,9},{11,1... | collective-permute-start | bytes 2752520 | tf_op jit(solution)/shard_map/ppermute | solution.py:25
  19.1 14.6 %collective-permute-start.4 = (bf16[4,448,256]{2,1,0:T(8,128)(2,1)S(1)}, bf16[4,448,256]{2,1,0:T(8,128)(2,1)S(1)}, u32[]{:S(2)}, u32[]{:S(2)}) collective-permute-start(bf16[4,448,256]{2,1,0:T(8,128)(2,1)S(1)} %join.1.piece.refs_0_), channel_id=1, source_target_pairs={{3,0},{0,1},{1,2},{2,3},{7,4},{4,5},{5,6},{6,7},{11,8},{8,9},{9,10... | collective-permute-start | bytes 2752520 | tf_op jit(solution)/shard_map/ppermute | solution.py:25
  30.1 10.2 %collective-permute-start.9 = (bf16[4,448,256]{2,1,0:T(8,128)(2,1)S(1)}, bf16[4,448,256]{2,1,0:T(8,128)(2,1)S(1)}, u32[]{:S(2)}, u32[]{:S(2)}) collective-permute-start(bf16[4,448,256]{2,1,0:T(8,128)(2,1)S(1)} %tie.2.piece.refs_1_), channel_id=1, source_target_pairs={{16,0},{17,1},{18,2},{19,3},{20,4},{21,5},{22,6},{23,7},{24,8},{25... | collective-permute-start | bytes 2752520 | tf_op jit(solution)/shard_map/ppermute | solution.py:25
  33.7 8.8 %collective-permute-start.8 = (bf16[4,448,256]{2,1,0:T(8,128)(2,1)S(1)}, bf16[4,448,256]{2,1,0:T(8,128)(2,1)S(1)}, u32[]{:S(2)}, u32[]{:S(2)}) collective-permute-start(bf16[4,448,256]{2,1,0:T(8,128)(2,1)S(1)} %collective-permute-done.4.piece.refs_3_), channel_id=1, source_target_pairs={{16,0},{17,1},{18,2},{19,3},{20,4},{21,5},{22,6},{23,7},{24,8},{25... | collective-permute-start | bytes 2752520 | tf_op jit(solution)/shard_map/ppermute | solution.py:25
  33.7 14.9 %collective-permute-start.3 = (bf16[4,448,256]{2,1,0:T(8,128)(2,1)S(1)}, bf16[4,448,256]{2,1,0:T(8,128)(2,1)S(1)}, u32[]{:S(2)}, u32[]{:S(2)}) collective-permute-start(bf16[4,448,256]{2,1,0:T(8,128)(2,1)S(1)} %join.1.piece.refs_0_), channel_id=1, source_target_pairs={{2,0},{3,1},{0,2},{1,3},{6,4},{7,5},{4,6},{5,7},{10,8},{11,9},{8,1... | collective-permute-start | bytes 2752520 | tf_op jit(solution)/shard_map/ppermute | solution.py:25
  42.5 8.9 %copy-start.4 = (bf16[768,512]{1,0:T(8,128)(2,1)S(1)}, bf16[768,512]{1,0:T(8,128)(2,1)}, u32[]{:S(2)}) copy-start(bf16[768,512]{1,0:T(8,128)(2,1)} %refs_2_.1) | copy-start | bytes 2359300
  42.5 8.9 %copy-start.5 = (f32[512]{0:T(512)S(1)}, f32[512]{0:T(512)}, u32[]{:S(2)}) copy-start(f32[512]{0:T(512)} %param.7) | copy-start | bytes 6148
  48.7 2.7 %collective-permute-start.10 = (bf16[4,448,256]{2,1,0:T(8,128)(2,1)S(1)}, bf16[4,448,256]{2,1,0:T(8,128)(2,1)S(1)}, u32[]{:S(2)}, u32[]{:S(2)}) collective-permute-start(bf16[4,448,256]{2,1,0:T(8,128)(2,1)S(1)} %tie.3.piece.refs_2_), channel_id=1, source_target_pairs={{16,0},{17,1},{18,2},{19,3},{20,4},{21,5},{22,6},{23,7},{24,8},{25... | collective-permute-start | bytes 2752520 | tf_op jit(solution)/shard_map/ppermute | solution.py:25
  54.3 2.4 %collective-permute-start.11 = (bf16[784,512]{1,0:T(8,128)(2,1)S(1)}, bf16[784,512]{1,0:T(8,128)(2,1)S(1)}, u32[]{:S(2)}, u32[]{:S(2)}) collective-permute-start(bf16[784,512]{1,0:T(8,128)(2,1)S(1)} %get-tuple-element.50.refs_4_.grad), channel_id=1, source_target_pairs={{16,0},{17,1},{18,2},{19,3},{20,4},{21,5},{22,6},{23,7},{24,8},{25... | collective-permute-start | bytes 2408456 | tf_op jit(solution)/shard_map/ppermute | solution.py:25
  59.0 23.3 %collective-permute-start.13 = (bf16[2,1808,128]{2,1,0:T(8,128)(2,1)S(1)}, bf16[2,1808,128]{2,1,0:T(8,128)(2,1)S(1)}, u32[]{:S(2)}, u32[]{:S(2)}) collective-permute-start(bf16[2,1808,128]{2,1,0:T(8,128)(2,1)S(1)} %get-tuple-element.60), channel_id=1, source_target_pairs={{64,0},{65,1},{66,2},{67,3},{68,4},{69,5},{70,6},{71,7},{72,8},{73... | collective-permute-start | bytes 2777096 | tf_op jit(solution)/shard_map/ppermute | solution.py:25
  64.4 19.6 %collective-permute-start.12 = (bf16[2,1808,128]{2,1,0:T(8,128)(2,1)S(1)}, bf16[2,1808,128]{2,1,0:T(8,128)(2,1)S(1)}, u32[]{:S(2)}, u32[]{:S(2)}) collective-permute-start(bf16[2,1808,128]{2,1,0:T(8,128)(2,1)S(1)} %get-tuple-element.59), channel_id=1, source_target_pairs={{96,0},{97,1},{98,2},{99,3},{100,4},{101,5},{102,6},{103,7},{104,8... | collective-permute-start | bytes 2777096 | tf_op jit(solution)/shard_map/ppermute | solution.py:25
  67.4 16.7 %collective-permute-start.14 = (bf16[2,1808,128]{2,1,0:T(8,128)(2,1)S(1)}, bf16[2,1808,128]{2,1,0:T(8,128)(2,1)S(1)}, u32[]{:S(2)}, u32[]{:S(2)}) collective-permute-start(bf16[2,1808,128]{2,1,0:T(8,128)(2,1)S(1)} %get-tuple-element.61), channel_id=1, source_target_pairs={{32,0},{33,1},{34,2},{35,3},{36,4},{37,5},{38,6},{39,7},{40,8},{41... | collective-permute-start | bytes 2777096 | tf_op jit(solution)/shard_map/ppermute | solution.py:25
  72.4 32.7 %copy-start.1 = (bf16[448,512]{1,0:T(8,128)(2,1)S(1)}, bf16[448,512]{1,0:T(8,128)(2,1)}, u32[]{:S(2)}) copy-start(bf16[448,512]{1,0:T(8,128)(2,1)} %param.6) | copy-start | bytes 1376260
  85.1 10.1 %collective-permute-start.15 = (bf16[960,128]{1,0:T(8,128)(2,1)S(1)}, bf16[960,128]{1,0:T(8,128)(2,1)S(1)}, u32[]{:S(2)}, u32[]{:S(2)}) collective-permute-start(bf16[960,128]{1,0:T(8,128)(2,1)S(1)} %get-tuple-element.64), channel_id=1, source_target_pairs={{12,0},{13,1},{14,2},{15,3},{0,4},{1,5},{2,6},{3,7},{4,8},{5,9},{6... | collective-permute-start | bytes 737288 | tf_op jit(solution)/shard_map/ppermute | solution.py:25
  85.6 9.6 %collective-permute-start.16 = (bf16[960,128]{1,0:T(8,128)(2,1)S(1)}, bf16[960,128]{1,0:T(8,128)(2,1)S(1)}, u32[]{:S(2)}, u32[]{:S(2)}) collective-permute-start(bf16[960,128]{1,0:T(8,128)(2,1)S(1)} %get-tuple-element.65), channel_id=1, source_target_pairs={{8,0},{9,1},{10,2},{11,3},{12,4},{13,5},{14,6},{15,7},{0,8},{1,9},... | collective-permute-start | bytes 737288 | tf_op jit(solution)/shard_map/ppermute | solution.py:25
  87.5 8.6 %collective-permute-start.17 = (bf16[960,128]{1,0:T(8,128)(2,1)S(1)}, bf16[960,128]{1,0:T(8,128)(2,1)S(1)}, u32[]{:S(2)}, u32[]{:S(2)}) collective-permute-start(bf16[960,128]{1,0:T(8,128)(2,1)S(1)} %get-tuple-element.66), channel_id=1, source_target_pairs={{4,0},{5,1},{6,2},{7,3},{8,4},{9,5},{10,6},{11,7},{12,8},{13,9},{1... | collective-permute-start | bytes 737288 | tf_op jit(solution)/shard_map/ppermute | solution.py:25
  96.8 6.2 %collective-permute-start.18 = (bf16[240,128]{1,0:T(8,128)(2,1)S(1)}, bf16[240,128]{1,0:T(8,128)(2,1)S(1)}, u32[]{:S(2)}, u32[]{:S(2)}) collective-permute-start(bf16[240,128]{1,0:T(8,128)(2,1)S(1)} %get-tuple-element.68), channel_id=1, source_target_pairs={{3,0},{0,1},{1,2},{2,3},{7,4},{4,5},{5,6},{6,7},{11,8},{8,9},{9,10... | collective-permute-start | bytes 184328 | tf_op jit(solution)/shard_map/ppermute | solution.py:25
  96.9 6.1 %collective-permute-start.19 = (bf16[240,128]{1,0:T(8,128)(2,1)S(1)}, bf16[240,128]{1,0:T(8,128)(2,1)S(1)}, u32[]{:S(2)}, u32[]{:S(2)}) collective-permute-start(bf16[240,128]{1,0:T(8,128)(2,1)S(1)} %get-tuple-element.69), channel_id=1, source_target_pairs={{2,0},{3,1},{0,2},{1,3},{6,4},{7,5},{4,6},{5,7},{10,8},{11,9},{8,1... | collective-permute-start | bytes 184328 | tf_op jit(solution)/shard_map/ppermute | solution.py:25
  98.9 4.9 %collective-permute-start.20 = (bf16[240,128]{1,0:T(8,128)(2,1)S(1)}, bf16[240,128]{1,0:T(8,128)(2,1)S(1)}, u32[]{:S(2)}, u32[]{:S(2)}) collective-permute-start(bf16[240,128]{1,0:T(8,128)(2,1)S(1)} %get-tuple-element.70), channel_id=1, source_target_pairs={{1,0},{2,1},{3,2},{0,3},{5,4},{6,5},{7,6},{4,7},{9,8},{10,9},{11,1... | collective-permute-start | bytes 184328 | tf_op jit(solution)/shard_map/ppermute | solution.py:25
